TPU v7x, 768 devices: a whole 4x8x12 slice. The times are simulated.
768 devices in a mesh: gz: 96 (over z, x, core), view: 4 (over y_lo), gy: 2 (over y_hi).
Axes of the slice: x: 4, y: 8 (y_hi: 2, y_lo: 4; y = y_hi * 4 + y_lo), z: 12, core: 2. Of those that a mesh axis runs over, the one named last changes fastest.
Arguments:
- estimate: bfloat16 [384, 64, 1024], P('gz', 'gy', 'view'), may hold values from 0.099609375 to 10
- observed: float32 [8, 384, 64, 1024], P('view', 'gz', 'gy'), may hold values from 0.5 to 20
- psf_blocks: bfloat16 [8, 196608], P('view', 'gz'), may hold values from 0.0007972717 to 0.0079956055
- kernel_y: float32 [8, 9], replicated, may hold values from 0.01 to 1
- block_source: int32 [8, 8], replicated, may hold values from 0 to 7, as said below
- psf_columns: int32 [8, 16, 3], replicated, may hold values from 0 to 15, as said below
Outputs:
- ratio: float32 [8, 384, 64, 1024], P('view', 'gz', 'gy')
Inputs may be any that keep to these rules, and one draw needn't show every extreme that they name: `block_source`: each view v has an offset o_v and reads, for its block j, either block (o_v + j) mod 8 or block (o_v + j // 2) mod 8. Of the entries of one row, at most 4 name blocks held by one index of view (blocks p * 2 to p * 2 + 1), and in every draw some view reaches 4 for some index. psf_columns[v, i, k] = (i + d) mod 16 with the 3 values d of a row distinct, among -2 to 2.
All inputs are finite; a program needn't handle non-finite values.
Results may differ from a plain program's by a relative error of at most 0.0016.
Values may be sent and summed in bfloat16 or wider, within the bound.
No kernel may reach another device: no remote copies, remote signals or barrier semaphores. Data moves between devices by JAX's collectives and lax.ppermute only.
A program may use at most 32 MiB of HBM per device.

v0:
```python
import jax
import jax.numpy as jnp
from jax import lax
from jax.sharding import PartitionSpec as P


def with_halo(cells, sides, width):
    for axis, dim in sides:
        count = lax.axis_size(axis)
        ends = count - 1
        head = lax.slice_in_dim(cells, 0, width, axis=dim)
        tail = lax.slice_in_dim(cells, cells.shape[dim] - width, cells.shape[dim], axis=dim)
        cells = jnp.concatenate(
            [
                lax.ppermute(tail, axis, [(i, (i + 1) % count) for i in range(ends)]),
                cells,
                lax.ppermute(head, axis, [((i + 1) % count, i) for i in range(ends)]),
            ],
            axis=dim,
        )
    return cells


def lateral_blur(rows_in, operator_mat, columns):
    sub_count = rows_in.shape[-1] // 64

    def single_view(view_rows, view_operator, view_columns):
        blocks = view_rows.reshape(-1, sub_count, 64)
        picked = jnp.take(blocks, view_columns, axis=1).reshape(blocks.shape[0], sub_count, -1)
        result = jnp.einsum(
            "rik,iko->rio", picked, view_operator, preferred_element_type=jnp.float32
        )
        return result.reshape(view_rows.shape).astype(jnp.bfloat16)

    return jax.vmap(single_view)(rows_in, operator_mat, columns)


def shards(estimate, observed, psf_blocks, kernel_y, block_source, psf_columns):
    planes, rows_here, local_width = estimate.shape
    per_device = observed.shape[0]
    width_all = observed.shape[3]
    block_count = block_source.shape[1]
    mine_index = lax.axis_index("view")
    first_view = mine_index * per_device
    sources_mine = lax.dynamic_slice_in_dim(block_source, first_view, per_device, 0)
    whole_rows = lax.all_gather(estimate, "view", axis=2, tiled=True)
    pieces = whole_rows.reshape(planes, rows_here, block_count, 128)
    pick = (sources_mine[:, :, None] == jnp.arange(block_count)[None, None, :]).astype(jnp.bfloat16)
    moved = jnp.einsum("wji,zyic->wzyjc", pick, pieces, preferred_element_type=jnp.float32)
    moved = moved.astype(jnp.bfloat16).reshape(per_device, planes, rows_here, width_all)
    operators = lax.all_gather(psf_blocks, "gz", axis=1, tiled=True)
    columns_mine = lax.dynamic_slice_in_dim(psf_columns, first_view, per_device, 0)
    band_size = psf_columns.shape[2]
    operator_mat = operators.reshape(per_device, width_all // 64, band_size * 64, 64)
    reach = kernel_y.shape[1] // 2
    flat = lateral_blur(moved, operator_mat, columns_mine)
    padded = with_halo(flat, (("gy", 2),), reach)
    weights = lax.dynamic_slice_in_dim(kernel_y, first_view, per_device, 0)
    blurred = jnp.zeros(observed.shape, jnp.float32)
    for offset in range(2 * reach + 1):
        blurred = blurred + weights[:, offset][:, None, None, None] * padded[
            :, :, offset : offset + rows_here, :
        ].astype(jnp.float32)
    return observed / blurred


def solution(mesh):
    in_specs = (P("gz", "gy", "view"), P("view", "gz", "gy", None), P("view", "gz"), P(), P(), P())
    out_specs = P("view", "gz", "gy", None)
    return jax.shard_map(shards, mesh=mesh, in_specs=in_specs, out_specs=out_specs, check_vma=False)
```

profile of v0, /device:TPU:6, one launch (start us, length us, event | category | flops | bytes accessed | tf_op | source)
XLA Modules:
  0.0 131.9 jit_solution(15159980098560764462)
XLA Ops:
  0.0 0.0 copy-start
  0.0 0.7 bitcast_or_fusion
  0.7 0.7 compare_and_fusion
  1.5 0.0 copy-start.2
  1.5 84.9 %all_gather.7 = bf16[2,196608]{1,0:T(2,128)(2,1)S(1)} all-gather(bf16[2,2048]{1,0:T(2,128)(2,1)} %param.8), channel_id=1, replica_groups=mesh['gz'=96,'view'=4,'gy'=2] {'gz'}, dimensions={1}, use_global_device_ids=true | all-gather | bytes 794624 | tf_op jit(solution)/shard_map/all_gather | solution.py:51
  86.4 2.1 %reshape.27 = bf16[2,16,192,64]{3,2,1,0:T(8,128)(2,1)} reshape(bf16[2,196608]{1,0:T(2,128)(2,1)S(1)} %all_gather.7) | data formatting | bytes 1572864 | tf_op jit(solution)/shard_map/reshape | solution.py:54
  88.5 0.0 copy-done.2
  88.5 14.1 %all_gather.6 = bf16[4,32,1024]{2,1,0:T(8,128)(2,1)S(1)} all-gather(bf16[4,32,256]{2,1,0:T(8,128)(2,1)S(1)} %copy-done.2), channel_id=1, replica_groups=mesh['gz'=96,'view'=4,'gy'=2] {'view'}, dimensions={2}, use_global_device_ids=true | all-gather | bytes 327680 | tf_op jit(solution)/shard_map/all_gather | solution.py:46
  102.7 0.7 constant_dynamic-slice_fusion
  103.4 0.3 fusion.6
  103.7 0.4 reshape_reshape.3
  104.1 0.9 copy.17
  105.0 0.1 copy.16
  105.1 0.1 reshape.28
  105.2 0.1 copy.15
  105.3 0.1 broadcast_in_dim.18
  105.4 0.1 broadcast_in_dim.19
  105.5 1.3 gather_fusion
  106.8 2.9 %fusion.7 = bf16[2,128,16,64]{1,3,2,0:T(8,128)(2,1)S(1)} fusion(bf16[2,16,192,64]{3,2,1,0:T(8,128)(2,1)} %reshape.27, bf16[2,128,16,192]{1,3,2,0:T(8,128)(2,1)S(1)} %bitcast.31, pred[2,16,192]{2,1,0:T(8,128)(4,1)S(1)} %broadcast_in_dim.19), kind=kOutput, calls=%fused_computation.7 | convolution fusion | flops 101711872 | bytes 2889728 | tf_op jit(solution)/shard_map/vmap(rik,iko->rio)/dot_general | solution.py:30
  109.7 0.8 copy.19
  110.6 0.0 copy-start.1
  110.6 0.7 convert_element_type.47
  111.3 0.1 fusion.18
  111.4 8.0 %collective-permute-start = (bf16[2,4,4,1024]{3,2,1,0:T(4,128)(2,1)S(1)}, bf16[2,4,4,1024]{3,2,1,0:T(4,128)(2,1)S(1)}, u32[]{:S(2)}, u32[]{:S(2)}) collective-permute-start(bf16[2,4,4,1024]{3,2,1,0:T(4,128)(2,1)S(1)} %get-tuple-element.15), channel_id=1, source_target_pairs={{0,1},{2,3},{4,5},{6,7},{8,9},{10,11},{12,13},{14,15},{16,17},{18,... | collective-permute-start | bytes 196616 | tf_op jit(solution)/shard_map/ppermute | solution.py:15
  119.4 1.3 collective-permute-start.1
  120.7 0.0 copy-done
  120.8 0.3 slice_reduce_fusion.8
  121.1 8.4 %collective-permute-done.1 = bf16[2,4,4,1024]{3,2,1,0:T(4,128)(2,1)S(1)} collective-permute-done((bf16[2,4,4,1024]{3,2,1,0:T(4,128)(2,1)S(1)}, bf16[2,4,4,1024]{3,2,1,0:T(4,128)(2,1)S(1)}, u32[]{:S(2)}, u32[]{:S(2)}) %collective-permute-start.1) | collective-permute-done | bytes 65568 | tf_op jit(solution)/shard_map/ppermute | solution.py:17
  129.5 0.0 collective-permute-done
  129.5 0.0 copy-done.1
  129.5 2.4 %add_divide_fusion = f32[2,4,32,1024]{3,2,1,0:T(8,128)} fusion(f32[2,4,32,1024]{3,2,1,0:T(8,128)S(1)} %copy-done.1, bf16[2,4,32,1024]{3,2,1,0:T(8,128)(2,1)S(1)} %convert_element_type.47, bf16[2,4,4,1024]{3,2,1,0:T(4,128)(2,1)S(1)} %collective-permute-done, bf16[2,4,36,1024]{3,2,1,0:T(8,128)(2,1)S(1)} %constant_dynamic-update-slice_fusion, ...), kind=kLoop, calls=%fused_computation.11 | loop fusion | flops 10223616 | bytes 4784200 | tf_op jit(solution)/shard_map/div | solution.py:64
  (4 shorter events, 0.1 us)
Async XLA Ops:
  0.0 120.7 %copy-start = (f32[8,9]{1,0:T(8,128)S(1)}, f32[8,9]{1,0:T(8,128)}, u32[]{:S(2)}) copy-start(f32[8,9]{1,0:T(8,128)} %param.9) | copy-start | bytes 868
  1.5 87.1 %copy-start.2 = (bf16[4,32,256]{2,1,0:T(8,128)(2,1)S(1)}, bf16[4,32,256]{2,1,0:T(8,128)(2,1)}, u32[]{:S(2)}) copy-start(bf16[4,32,256]{2,1,0:T(8,128)(2,1)} %param.6) | copy-start | bytes 196612
  110.6 19.0 %copy-start.1 = (f32[2,4,32,1024]{3,2,1,0:T(8,128)S(1)}, f32[2,4,32,1024]{3,2,1,0:T(8,128)}, u32[]{:S(2)}) copy-start(f32[2,4,32,1024]{3,2,1,0:T(8,128)} %param.7) | copy-start | bytes 3145732
  111.4 18.2 %collective-permute-start = (bf16[2,4,4,1024]{3,2,1,0:T(4,128)(2,1)S(1)}, bf16[2,4,4,1024]{3,2,1,0:T(4,128)(2,1)S(1)}, u32[]{:S(2)}, u32[]{:S(2)}) collective-permute-start(bf16[2,4,4,1024]{3,2,1,0:T(4,128)(2,1)S(1)} %get-tuple-element.15), channel_id=1, source_target_pairs={{0,1},{2,3},{4,5},{6,7},{8,9},{10,11},{12,13},{14,15},{16,17},{18,... | collective-permute-start | bytes 196616 | tf_op jit(solution)/shard_map/ppermute | solution.py:15
  119.4 10.1 %collective-permute-start.1 = (bf16[2,4,4,1024]{3,2,1,0:T(4,128)(2,1)S(1)}, bf16[2,4,4,1024]{3,2,1,0:T(4,128)(2,1)S(1)}, u32[]{:S(2)}, u32[]{:S(2)}) collective-permute-start(bf16[2,4,4,1024]{3,2,1,0:T(4,128)(2,1)S(1)} %get-tuple-element.14), channel_id=1, source_target_pairs={{1,0},{3,2},{5,4},{7,6},{9,8},{11,10},{13,12},{15,14},{17,16},{19,... | collective-permute-start | bytes 196616 | tf_op jit(solution)/shard_map/ppermute | solution.py:17
where the time goes:
time: 132 us
  blocking collectives  99 us (75%)
  starting transfers between devices  9.33 us (7%)
  waiting for transfers between devices  8.4 us (6%)
  local copies, waits for them, and re-layouts  7.94 us (6%)
  other arithmetic  3.82 us (3%)
  matrix products  3.25 us (2%)
    all_gather x1, blocking collectives, shards(): operators = lax.all_gather(psf_blocks, 'gz', axis=1, tiled=True)  84.9 us
    all_gather x1, blocking collectives, shards(): whole_rows = lax.all_gather(estimate, 'view', axis=2, tiled=True)  14.1 us
    ppermute x1, waiting for transfers between devices, with_halo(): lax.ppermute(head, axis, [((i + 1) % count, i) for i in range(ends)])  8.4 us
    ppermute x1, starting transfers between devices, with_halo(): lax.ppermute(tail, axis, [(i, (i + 1) % count) for i in range(ends)])  8.04 us
    dot_general x1, matrix products, single_view(): jnp.einsum('rik,iko->rio', picked, view_operator, preferred_element_type=...  2.9 us
  transfers between devices with their start and end apart: 2, of which 1 were waited for; matrix products, arithmetic and copies ran while one was open for 0% of the time, Pallas kernels for 0%

commit v1 on v0

v1 whole, which is shorter than its diff:
```python
import jax
import jax.numpy as jnp
from jax import lax
from jax.experimental import pallas as pl
from jax.experimental.pallas import tpu as pltpu
from jax.sharding import Mesh, PartitionSpec as P

PLANES, ROWS, HALO = 4, 32, 4
OWN = PLANES * ROWS
EDGE = PLANES * HALO
BLOCKS = 8
BAND = 3


def fused(place, sources, columns, weights, seen, mine, other, observed, ratio, dense, flat):
    view, side, core = place[0], place[1], place[2]
    dense[...] = jnp.zeros_like(dense)
    for w in range(2):
        for i in range(2 * BLOCKS):
            j, half = i // 2, i % 2
            for k in range(BAND):
                shift = (columns[2 * view + w, i * BAND + k] - (2 * j - 2)) & 15
                base = shift * 64
                lanes = pl.ds(64 * half, 64)
                dense[w, j, pl.ds(pl.multiple_of(base + 32 * core, 32), 32), lanes] = mine[
                    i * BAND + k, :, 64 * w : 64 * w + 64
                ]
                dense[w, j, pl.ds(pl.multiple_of(base + 32 * (1 - core), 32), 32), lanes] = other[
                    i * BAND + k, :, 64 * w : 64 * w + 64
                ]

    def block(w, j):
        b = sources[2 * view + w, j % BLOCKS]
        p, half = b // 2, b % 2
        return jnp.concatenate([seen[p, half, :OWN], seen[3 - p, half, OWN:]], axis=0)

    for w in range(2):
        for j in range(BLOCKS):
            near = jnp.concatenate([block(w, j + BLOCKS - 1), block(w, j), block(w, j + 1)], axis=1)
            flat[w, :, 128 * j : 128 * j + 128] = jnp.dot(
                near, dense[w, j], preferred_element_type=jnp.float32
            ).astype(jnp.bfloat16)

    shape = (OWN, OWN + EDGE)
    row = lax.broadcasted_iota(jnp.int32, shape, 0)
    col = lax.broadcasted_iota(jnp.int32, shape, 1)
    outer = col - OWN
    spot = jnp.where(col < OWN, col & (ROWS - 1), (outer & (HALO - 1)) + jnp.where(side == 0, ROWS, -HALO))
    plane = jnp.where(col < OWN, col >> 5, outer >> 2)
    tap = jnp.where(plane == (row >> 5), spot - (row & (ROWS - 1)) + HALO, -1)
    for w in range(2):
        mix = jnp.zeros(shape, jnp.float32)
        for t in range(2 * HALO + 1):
            mix = jnp.where(tap == t, weights[2 * view + w, t], mix)
        high = mix.astype(jnp.bfloat16)
        low = (mix - high.astype(jnp.float32)).astype(jnp.bfloat16)
        lateral = flat[w]
        blurred = jnp.dot(high, lateral, preferred_element_type=jnp.float32)
        blurred = blurred + jnp.dot(low, lateral, preferred_element_type=jnp.float32)
        ratio[w] = observed[w] / blurred


def shards(estimate, observed, psf_blocks, kernel_y, block_source, psf_columns):
    side = lax.axis_index("gy")
    place = jnp.stack([lax.axis_index("view"), side, lax.axis_index("core")]).astype(jnp.int32)
    shard = psf_blocks.reshape(2, 32, 64).transpose(1, 0, 2).reshape(1, 32, 128)
    edge = lax.dynamic_slice_in_dim(estimate, jnp.where(side == 0, ROWS - HALO, 0), HALO, 1)
    mirror = [(v * 2 + g, (3 - v) * 2 + (1 - g)) for v in range(4) for g in range(2)]
    edge = lax.ppermute(edge, ("view", "gy"), mirror)
    across = lax.all_to_all(jnp.broadcast_to(shard, (4, 32, 128)), "x", 0, 0, tiled=True)
    slab = jnp.concatenate([estimate.reshape(OWN, 2, 128), edge.reshape(EDGE, 2, 128)], axis=0)
    slab = slab.transpose(1, 0, 2)
    seen = lax.all_to_all(jnp.broadcast_to(slab[None], (4, *slab.shape)), "view", 0, 0, tiled=True)
    mine = lax.all_to_all(jnp.broadcast_to(across[None], (12, 4, 32, 128)), "z", 0, 0, tiled=True)
    mine = mine.reshape(48, 32, 128)
    other = lax.ppermute(mine, "core", [(0, 1), (1, 0)])
    smem = pl.BlockSpec(memory_space=pltpu.SMEM)
    vmem = pl.BlockSpec(memory_space=pltpu.VMEM)
    ratio = pl.pallas_call(
        fused,
        out_shape=jax.ShapeDtypeStruct((2, OWN, 1024), jnp.float32),
        in_specs=[smem] * 4 + [vmem] * 4,
        out_specs=vmem,
        scratch_shapes=[
            pltpu.VMEM((2, BLOCKS, 384, 128), jnp.bfloat16),
            pltpu.VMEM((2, OWN + EDGE, 1024), jnp.bfloat16),
        ],
        compiler_params=pltpu.CompilerParams(vmem_limit_bytes=32 * 1024 * 1024),
    )(
        place,
        block_source,
        psf_columns.reshape(8, 48),
        kernel_y,
        seen,
        mine,
        other,
        observed.reshape(2, OWN, 1024),
    )
    return ratio.reshape(2, PLANES, ROWS, 1024)


def solution(mesh):
    fine = Mesh(mesh.devices.reshape(12, 4, 2, 4, 2), ("z", "x", "core", "view", "gy"))
    gz = ("z", "x", "core")
    in_specs = (P(gz, "gy", "view"), P("view", gz, "gy", None), P("view", gz), P(), P(), P())
    out_specs = P("view", gz, "gy", None)
    return jax.shard_map(shards, mesh=fine, in_specs=in_specs, out_specs=out_specs, check_vma=False)
```

time: 132 us -> 63.9 us (0.48)
  the two profiles are of different devices: /device:TPU:6 before, /device:TPU:64 now
where the time goes in v1:
time: 63.9 us; the launch traced here: 63.4 us
  starting transfers between devices  27.2 us (43%)
  waiting for transfers between devices  20.2 us (32%)
  blocking collectives  9.54 us (15%)
  Pallas kernels  3.54 us (6%)
  local copies, waits for them, and re-layouts  2.7 us (4%)
    all_to_all x1, starting transfers between devices, shards(): lax.all_to_all(jnp.broadcast_to(across[None], (12, 4, 32, 128)), 'z', 0,...  14.9 us
    all_to_all x1, waiting for transfers between devices, shards(): lax.all_to_all(jnp.broadcast_to(across[None], (12, 4, 32, 128)), 'z', 0,...  11.4 us
    all_to_all x1, blocking collectives, shards(): lax.all_to_all(jnp.broadcast_to(shard, (4, 32, 128)), 'x', 0, 0, tiled=True)  9.54 us
    all_to_all x1, waiting for transfers between devices, shards(): lax.all_to_all(jnp.broadcast_to(slab[None], (4, *slab.shape)), 'view', 0,...  7.31 us
    ppermute x1, starting transfers between devices, shards(): edge = lax.ppermute(edge, ('view', 'gy'), mirror)  5.38 us
    all_to_all x1, starting transfers between devices, shards(): lax.all_to_all(jnp.broadcast_to(slab[None], (4, *slab.shape)), 'view', 0,...  4.87 us
    pallas_call x1, Pallas kernels, shards(): pl.pallas_call(fused, out_shape=jax.ShapeDtypeStruct((2, OWN, 1024), jnp....  3.54 us
    ppermute x1, starting transfers between devices, shards(): other = lax.ppermute(mine, 'core', [(0, 1), (1, 0)])  2.04 us
  transfers between devices with their start and end apart: 4, of which 3 were waited for; matrix products, arithmetic and copies ran while one was open for 0% of the time, Pallas kernels for 0%

profile of v1, /device:TPU:64, one launch (start us, length us, event | category | flops | bytes accessed | tf_op | source)
XLA Modules:
  0.0 63.4 jit_solution(13035229099152965186)
XLA Ops:
  0.0 0.8 %reshape.28 = bf16[2,32,64]{2,1,0:T(8,128)(2,1)S(1)} reshape(bf16[2,2048]{1,0:T(2,128)(2,1)} %param.8) | data formatting | bytes 16384 | tf_op jit(solution)/shard_map/reshape | solution.py:66
  0.8 0.1 broadcast_in_dim.9
  0.9 9.5 %all_to_all.15 = bf16[4,32,128]{2,1,0:T(8,128)(2,1)S(1)} all-to-all(bf16[4,32,128]{2,1,0:T(8,128)(2,1)S(1)} %broadcast_in_dim.10), channel_id=1, replica_groups=mesh['z'=12,'x'=4,'core'=2,'view'=4,'gy'=2] {'x'}, dimensions={0} | all-to-all | bytes 65536 | tf_op jit(solution)/shard_map/all_to_all | solution.py:70
  10.4 0.0 copy-start.3
  10.4 0.8 %broadcast_in_dim.22 = bf16[12,4,32,128]{3,2,1,0:T(8,128)(2,1)} broadcast(bf16[4,32,128]{2,1,0:T(8,128)(2,1)S(1)} %all_to_all.15), dimensions={1,2,3} | broadcast | bytes 425984 | tf_op jit(solution)/shard_map/broadcast_in_dim | solution.py:74
  11.3 0.0 copy-start
  11.3 14.9 %all-to-all-start.2 = ((bf16[12,4,32,128]{3,2,1,0:T(8,128)(2,1)}), bf16[12,4,32,128]{3,2,1,0:T(8,128)(2,1)S(1)}, u32[]{:S(2)}, u32[]{:S(2)}) async-start(bf16[12,4,32,128]{3,2,1,0:T(8,128)(2,1)} %broadcast_in_dim.22), calls=%async_computation.2 | async-start | bytes 786432 | tf_op jit(solution)/shard_map/all_to_all | solution.py:74
  26.2 0.0 copy-done.3
  26.2 5.4 %collective-permute-start = (bf16[4,4,256]{2,1,0:T(4,128)(2,1)S(1)}, bf16[4,4,256]{2,1,0:T(4,128)(2,1)S(1)}, u32[]{:S(2)}, u32[]{:S(2)}) collective-permute-start(bf16[4,4,256]{2,1,0:T(4,128)(2,1)S(1)} %constant_dynamic-slice_fusion), channel_id=1, source_target_pairs={{0,7},{1,6},{2,5},{3,4},{4,3},{5,2},{6,1},{7,0},{8,15},{9,14},{10,... | collective-permute-start | bytes 24584 | tf_op jit(solution)/shard_map/ppermute | solution.py:69
  31.6 1.6 %collective-permute-done = bf16[4,4,256]{2,1,0:T(4,128)(2,1)S(1)} collective-permute-done((bf16[4,4,256]{2,1,0:T(4,128)(2,1)S(1)}, bf16[4,4,256]{2,1,0:T(4,128)(2,1)S(1)}, u32[]{:S(2)}, u32[]{:S(2)}) %collective-permute-start) | collective-permute-done | bytes 8224 | tf_op jit(solution)/shard_map/ppermute | solution.py:69
  33.2 11.4 %all-to-all-done.2 = bf16[12,4,32,128]{3,2,1,0:T(8,128)(2,1)S(1)} async-done(((bf16[12,4,32,128]{3,2,1,0:T(8,128)(2,1)}), bf16[12,4,32,128]{3,2,1,0:T(8,128)(2,1)S(1)}, u32[]{:S(2)}, u32[]{:S(2)}) %all-to-all-start.2) | async-done | bytes 393248 | tf_op jit(solution)/shard_map/all_to_all | solution.py:74
  44.6 0.8 %broadcast_in_dim.8 = bf16[4,2,144,128]{3,2,1,0:T(8,128)(2,1)} broadcast(bf16[2,144,128]{2,1,0:T(8,128)(2,1)S(1)} %maximum_bitcast_fusion), dimensions={1,2,3} | broadcast | bytes 368640 | tf_op jit(solution)/shard_map/broadcast_in_dim | solution.py:73
  45.3 4.9 %all-to-all-start = ((bf16[4,2,144,128]{3,2,1,0:T(8,128)(2,1)}), bf16[4,2,144,128]{3,2,1,0:T(8,128)(2,1)S(1)}, u32[]{:S(2)}, u32[]{:S(2)}) async-start(bf16[4,2,144,128]{3,2,1,0:T(8,128)(2,1)} %broadcast_in_dim.8), calls=%async_computation | async-start | bytes 589824 | tf_op jit(solution)/shard_map/all_to_all | solution.py:73
  50.2 0.0 copy-start.4
  50.2 2.0 %collective-permute-start.1 = (bf16[48,32,128]{2,1,0:T(8,128)(2,1)S(1)}, bf16[48,32,128]{2,1,0:T(8,128)(2,1)S(1)}, u32[]{:S(2)}, u32[]{:S(2)}) collective-permute-start(bf16[48,32,128]{2,1,0:T(8,128)(2,1)S(1)} %bitcast.13), channel_id=1, source_target_pairs={{0,8},{8,0},{1,9},{9,1},{2,10},{10,2},{3,11},{11,3},{4,12},{12,4},... | collective-permute-start | bytes 1179656 | tf_op jit(solution)/shard_map/ppermute | solution.py:76
  52.3 0.0 copy-done.4
  52.3 0.1 copy.10
  52.4 0.1 copy.14.columns
  52.4 0.0 copy-start.2
  52.4 0.0 copy-start.1
  52.4 0.1 pad_add_fusion.place
  52.5 7.3 %all-to-all-done.seen = bf16[4,2,144,128]{3,2,1,0:T(8,128)(2,1)S(1)} async-done(((bf16[4,2,144,128]{3,2,1,0:T(8,128)(2,1)}), bf16[4,2,144,128]{3,2,1,0:T(8,128)(2,1)S(1)}, u32[]{:S(2)}, u32[]{:S(2)}) %all-to-all-start) | async-done | bytes 294944 | tf_op jit(solution)/shard_map/all_to_all | solution.py:73
  59.8 0.0 collective-permute-done.1.other
  59.8 0.0 copy-done
  59.8 0.0 copy-done.2
  59.8 0.0 copy-done.1
  59.9 3.5 %shard_map.64 = f32[2,128,1024]{2,1,0:T(8,128)} custom-call(s32[3]{0:T(128)S(1)} %pad_add_fusion.place, s32[8,8]{1,0:T(8,128)S(1)} %copy-done.1, s32[8,48]{1,0:T(8,128)S(1)} %copy.14.columns, f32[8,9]{1,0:T(8,128)S(1)} %copy-done.2, bf16[4,2,144,128]{3,2,1,0:T(8,128)(2,1)S(1)} %all-to-all-done.seen, bf16[48,32,128]{2,1,0:T(8,128)(2,1)S(1)} %bitcast.14, ...), custom_call_target="tpu_custom_call" | custom-call | tf_op jit(solution)/shard_map/pallas_call | solution.py:79
  (9 shorter events, 0.1 us)
Async XLA Ops:
  10.4 15.7 %copy-start.3 = (bf16[4,32,256]{2,1,0:T(8,128)(2,1)S(1)}, bf16[4,32,256]{2,1,0:T(8,128)(2,1)}, u32[]{:S(2)}) copy-start(bf16[4,32,256]{2,1,0:T(8,128)(2,1)} %param.6) | copy-start | bytes 196612
  11.3 48.6 %copy-start = (f32[2,4,32,1024]{3,2,1,0:T(8,128)S(1)}, f32[2,4,32,1024]{3,2,1,0:T(8,128)}, u32[]{:S(2)}) copy-start(f32[2,4,32,1024]{3,2,1,0:T(8,128)} %param.7) | copy-start | bytes 3145732
  11.3 33.3 %all-to-all-start.2 = ((bf16[12,4,32,128]{3,2,1,0:T(8,128)(2,1)}), bf16[12,4,32,128]{3,2,1,0:T(8,128)(2,1)S(1)}, u32[]{:S(2)}, u32[]{:S(2)}) async-start(bf16[12,4,32,128]{3,2,1,0:T(8,128)(2,1)} %broadcast_in_dim.22), calls=%async_computation.2 | async-start | bytes 786432 | tf_op jit(solution)/shard_map/all_to_all | solution.py:74
  26.2 7.0 %collective-permute-start = (bf16[4,4,256]{2,1,0:T(4,128)(2,1)S(1)}, bf16[4,4,256]{2,1,0:T(4,128)(2,1)S(1)}, u32[]{:S(2)}, u32[]{:S(2)}) collective-permute-start(bf16[4,4,256]{2,1,0:T(4,128)(2,1)S(1)} %constant_dynamic-slice_fusion), channel_id=1, source_target_pairs={{0,7},{1,6},{2,5},{3,4},{4,3},{5,2},{6,1},{7,0},{8,15},{9,14},{10,... | collective-permute-start | bytes 24584 | tf_op jit(solution)/shard_map/ppermute | solution.py:69
  45.3 14.5 %all-to-all-start = ((bf16[4,2,144,128]{3,2,1,0:T(8,128)(2,1)}), bf16[4,2,144,128]{3,2,1,0:T(8,128)(2,1)S(1)}, u32[]{:S(2)}, u32[]{:S(2)}) async-start(bf16[4,2,144,128]{3,2,1,0:T(8,128)(2,1)} %broadcast_in_dim.8), calls=%async_computation | async-start | bytes 589824 | tf_op jit(solution)/shard_map/all_to_all | solution.py:73
  50.2 2.1 %copy-start.4 = (s32[8,16,3]{1,0,2:T(8,128)S(1)}, s32[8,16,3]{1,0,2:T(8,128)}, u32[]{:S(2)}) copy-start(s32[8,16,3]{1,0,2:T(8,128)} %param.11) | copy-start | bytes 4612
  50.2 9.6 %collective-permute-start.1 = (bf16[48,32,128]{2,1,0:T(8,128)(2,1)S(1)}, bf16[48,32,128]{2,1,0:T(8,128)(2,1)S(1)}, u32[]{:S(2)}, u32[]{:S(2)}) collective-permute-start(bf16[48,32,128]{2,1,0:T(8,128)(2,1)S(1)} %bitcast.13), channel_id=1, source_target_pairs={{0,8},{8,0},{1,9},{9,1},{2,10},{10,2},{3,11},{11,3},{4,12},{12,4},... | collective-permute-start | bytes 1179656 | tf_op jit(solution)/shard_map/ppermute | solution.py:76
  52.4 7.4 %copy-start.2 = (f32[8,9]{1,0:T(8,128)S(1)}, f32[8,9]{1,0:T(8,128)}, u32[]{:S(2)}) copy-start(f32[8,9]{1,0:T(8,128)} %weights.1) | copy-start | bytes 868
  52.4 7.4 %copy-start.1 = (s32[8,8]{1,0:T(8,128)S(1)}, s32[8,8]{1,0:T(8,128)}, u32[]{:S(2)}) copy-start(s32[8,8]{1,0:T(8,128)} %sources.1) | copy-start | bytes 772

commit v2 on v1

--- a/solution.py
+++ b/solution.py
@@ -12,8 +12,12 @@
 BAND = 3
 
 
-def fused(place, sources, columns, weights, seen, mine, other, observed, ratio, dense, flat):
+def fused(place, sources, columns, weights, near, far, mine, other, observed, ratio, dense, flat, seen):
     view, side, core = place[0], place[1], place[2]
+    seen[view] = near[0]
+    seen[view ^ 1] = near[1]
+    seen[view ^ 2] = far[0]
+    seen[view ^ 3] = far[1]
     dense[...] = jnp.zeros_like(dense)
     for w in range(2):
         for i in range(2 * BLOCKS):
@@ -36,9 +40,9 @@
 
     for w in range(2):
         for j in range(BLOCKS):
-            near = jnp.concatenate([block(w, j + BLOCKS - 1), block(w, j), block(w, j + 1)], axis=1)
+            wide = jnp.concatenate([block(w, j + BLOCKS - 1), block(w, j), block(w, j + 1)], axis=1)
             flat[w, :, 128 * j : 128 * j + 128] = jnp.dot(
-                near, dense[w, j], preferred_element_type=jnp.float32
+                wide, dense[w, j], preferred_element_type=jnp.float32
             ).astype(jnp.bfloat16)
 
     shape = (OWN, OWN + EDGE)
@@ -68,22 +72,25 @@
     mirror = [(v * 2 + g, (3 - v) * 2 + (1 - g)) for v in range(4) for g in range(2)]
     edge = lax.ppermute(edge, ("view", "gy"), mirror)
     across = lax.all_to_all(jnp.broadcast_to(shard, (4, 32, 128)), "x", 0, 0, tiled=True)
+    edge, across = lax.optimization_barrier((edge, across))
     slab = jnp.concatenate([estimate.reshape(OWN, 2, 128), edge.reshape(EDGE, 2, 128)], axis=0)
-    slab = slab.transpose(1, 0, 2)
-    seen = lax.all_to_all(jnp.broadcast_to(slab[None], (4, *slab.shape)), "view", 0, 0, tiled=True)
+    slab = slab.transpose(1, 0, 2)[None]
+    near = jnp.concatenate([slab, lax.ppermute(slab, "view", [(i, i ^ 1) for i in range(4)])], axis=0)
+    far = lax.ppermute(near, "view", [(i, i ^ 2) for i in range(4)])
     mine = lax.all_to_all(jnp.broadcast_to(across[None], (12, 4, 32, 128)), "z", 0, 0, tiled=True)
-    mine = mine.reshape(48, 32, 128)
+    mine, far = lax.optimization_barrier((mine.reshape(48, 32, 128), far))
     other = lax.ppermute(mine, "core", [(0, 1), (1, 0)])
     smem = pl.BlockSpec(memory_space=pltpu.SMEM)
     vmem = pl.BlockSpec(memory_space=pltpu.VMEM)
     ratio = pl.pallas_call(
         fused,
         out_shape=jax.ShapeDtypeStruct((2, OWN, 1024), jnp.float32),
-        in_specs=[smem] * 4 + [vmem] * 4,
+        in_specs=[smem] * 4 + [vmem] * 5,
         out_specs=vmem,
         scratch_shapes=[
             pltpu.VMEM((2, BLOCKS, 384, 128), jnp.bfloat16),
             pltpu.VMEM((2, OWN + EDGE, 1024), jnp.bfloat16),
+            pltpu.VMEM((4, 2, OWN + EDGE, 128), jnp.bfloat16),
         ],
         compiler_params=pltpu.CompilerParams(vmem_limit_bytes=32 * 1024 * 1024),
     )(
@@ -91,7 +98,8 @@
         block_source,
         psf_columns.reshape(8, 48),
         kernel_y,
-        seen,
+        near,
+        far,
         mine,
         other,
         observed.reshape(2, OWN, 1024),

time: 63.9 us -> 57 us (0.89)
  the two profiles are of different devices: /device:TPU:64 before, /device:TPU:1 now
where the time goes in v2:
time: 57 us; the launch traced here: 56 us
  starting transfers between devices  40.1 us (70%)
  waiting for transfers between devices  9.54 us (17%)
  Pallas kernels  3.55 us (6%)
  local copies, waits for them, and re-layouts  2.57 us (5%)
    all_to_all x1, starting transfers between devices, shards(): lax.all_to_all(jnp.broadcast_to(across[None], (12, 4, 32, 128)), 'z', 0,...  14.9 us
    ppermute x1, starting transfers between devices, shards(): other = lax.ppermute(mine, 'core', [(0, 1), (1, 0)])  6.34 us
    ppermute x1, starting transfers between devices, shards(): edge = lax.ppermute(edge, ('view', 'gy'), mirror)  5.23 us
    all_to_all x1, starting transfers between devices, shards(): lax.all_to_all(jnp.broadcast_to(shard, (4, 32, 128)), 'x', 0, 0, tiled=True)  4.84 us
    ppermute x1, starting transfers between devices, shards(): lax.ppermute(slab, 'view', [(i, i ^ 1) for i in range(4)])  4.48 us
    ppermute x1, starting transfers between devices, shards(): far = lax.ppermute(near, 'view', [(i, i ^ 2) for i in range(4)])  4.37 us
    ppermute x1, waiting for transfers between devices, shards(): far = lax.ppermute(near, 'view', [(i, i ^ 2) for i in range(4)])  4.1 us
    pallas_call x1, Pallas kernels, shards(): pl.pallas_call(fused, out_shape=jax.ShapeDtypeStruct((2, OWN, 1024), jnp....  3.55 us
  transfers between devices with their start and end apart: 6, of which 5 were waited for; matrix products, arithmetic and copies ran while one was open for 1% of the time, Pallas kernels for 0%

profile of v2, /device:TPU:1, one launch (start us, length us, event | category | flops | bytes accessed | tf_op | source)
XLA Modules:
  0.0 56.0 jit_solution(6464907392097002424)
XLA Ops:
  0.0 0.8 %reshape.26 = bf16[2,32,64]{2,1,0:T(8,128)(2,1)S(1)} reshape(bf16[2,2048]{1,0:T(2,128)(2,1)} %param.8) | data formatting | bytes 16384 | tf_op jit(solution)/shard_map/reshape | solution.py:70
  0.8 0.0 copy-start.3
  0.8 0.1 broadcast_in_dim.16
  0.9 0.6 %broadcast_in_dim.17 = bf16[4,32,128]{2,1,0:T(8,128)(2,1)} broadcast(bf16[32,128]{1,0:T(8,128)(2,1)S(1)} %broadcast_in_dim.16), dimensions={1,2} | broadcast | bytes 40960 | tf_op jit(solution)/shard_map/broadcast_in_dim | solution.py:74
  1.5 4.8 %all-to-all-start = ((bf16[4,32,128]{2,1,0:T(8,128)(2,1)}), bf16[4,32,128]{2,1,0:T(8,128)(2,1)S(1)}, u32[]{:S(2)}, u32[]{:S(2)}) async-start(bf16[4,32,128]{2,1,0:T(8,128)(2,1)} %broadcast_in_dim.17), calls=%async_computation | async-start | bytes 65536 | tf_op jit(solution)/shard_map/all_to_all | solution.py:74
  6.4 0.0 copy-done.3
  6.4 0.0 copy-start
  6.4 5.2 %collective-permute-start = (bf16[4,4,256]{2,1,0:T(4,128)(2,1)S(1)}, bf16[4,4,256]{2,1,0:T(4,128)(2,1)S(1)}, u32[]{:S(2)}, u32[]{:S(2)}) collective-permute-start(bf16[4,4,256]{2,1,0:T(4,128)(2,1)S(1)} %constant_dynamic-slice_fusion), channel_id=1, source_target_pairs={{0,7},{1,6},{2,5},{3,4},{4,3},{5,2},{6,1},{7,0},{8,15},{9,14},{10,... | collective-permute-start | bytes 24584 | tf_op jit(solution)/shard_map/ppermute | solution.py:73
  11.6 1.0 %collective-permute-done = bf16[4,4,256]{2,1,0:T(4,128)(2,1)S(1)} collective-permute-done((bf16[4,4,256]{2,1,0:T(4,128)(2,1)S(1)}, bf16[4,4,256]{2,1,0:T(4,128)(2,1)S(1)}, u32[]{:S(2)}, u32[]{:S(2)}) %collective-permute-start) | collective-permute-done | bytes 8224 | tf_op jit(solution)/shard_map/ppermute | solution.py:73
  12.7 0.0 all-to-all-done
  12.7 0.8 %broadcast_in_dim.19 = bf16[12,4,32,128]{3,2,1,0:T(8,128)(2,1)} broadcast(bf16[4,32,128]{2,1,0:T(8,128)(2,1)S(1)} %all-to-all-done), dimensions={1,2,3} | broadcast | bytes 425984 | tf_op jit(solution)/shard_map/broadcast_in_dim | solution.py:80
  13.5 14.9 %all-to-all-start.1 = ((bf16[12,4,32,128]{3,2,1,0:T(8,128)(2,1)}), bf16[12,4,32,128]{3,2,1,0:T(8,128)(2,1)S(1)}, u32[]{:S(2)}, u32[]{:S(2)}) async-start(bf16[12,4,32,128]{3,2,1,0:T(8,128)(2,1)} %broadcast_in_dim.19), calls=%async_computation.1 | async-start | bytes 786432 | tf_op jit(solution)/shard_map/all_to_all | solution.py:80
  28.4 4.5 %collective-permute-start.1 = (bf16[1,2,144,128]{3,2,1,0:T(8,128)(2,1)S(1)}, bf16[1,2,144,128]{3,2,1,0:T(8,128)(2,1)S(1)}, u32[]{:S(2)}, u32[]{:S(2)}) collective-permute-start(bf16[1,2,144,128]{3,2,1,0:T(8,128)(2,1)S(1)} %maximum_bitcast_fusion), channel_id=1, source_target_pairs={{0,2},{2,0},{4,6},{6,4},{1,3},{3,1},{5,7},{7,5},{8,10},{10,8},{12,... | collective-permute-start | bytes 221192 | tf_op jit(solution)/shard_map/ppermute | solution.py:78
  32.9 1.7 %collective-permute-done.1 = bf16[1,2,144,128]{3,2,1,0:T(8,128)(2,1)S(1)} collective-permute-done((bf16[1,2,144,128]{3,2,1,0:T(8,128)(2,1)S(1)}, bf16[1,2,144,128]{3,2,1,0:T(8,128)(2,1)S(1)}, u32[]{:S(2)}, u32[]{:S(2)}) %collective-permute-start.1) | collective-permute-done | bytes 73760 | tf_op jit(solution)/shard_map/ppermute | solution.py:78
  34.7 0.0 copy-start.4
  34.7 4.4 %collective-permute-start.2 = (bf16[2,2,144,128]{3,2,1,0:T(8,128)(2,1)S(1)}, bf16[2,2,144,128]{3,2,1,0:T(8,128)(2,1)S(1)}, u32[]{:S(2)}, u32[]{:S(2)}) collective-permute-start(bf16[2,2,144,128]{3,2,1,0:T(8,128)(2,1)S(1)} %pad_maximum_fusion.near), channel_id=1, source_target_pairs={{0,4},{2,6},{4,0},{6,2},{1,5},{3,7},{5,1},{7,3},{8,12},{10,14},{12... | collective-permute-start | bytes 442376 | tf_op jit(solution)/shard_map/ppermute | solution.py:79
  39.1 4.1 %collective-permute-done.2.far = bf16[2,2,144,128]{3,2,1,0:T(8,128)(2,1)S(1)} collective-permute-done((bf16[2,2,144,128]{3,2,1,0:T(8,128)(2,1)S(1)}, bf16[2,2,144,128]{3,2,1,0:T(8,128)(2,1)S(1)}, u32[]{:S(2)}, u32[]{:S(2)}) %collective-permute-start.2) | collective-permute-done | bytes 147488 | tf_op jit(solution)/shard_map/ppermute | solution.py:79
  43.2 1.6 %all-to-all-done.1 = bf16[12,4,32,128]{3,2,1,0:T(8,128)(2,1)S(1)} async-done(((bf16[12,4,32,128]{3,2,1,0:T(8,128)(2,1)}), bf16[12,4,32,128]{3,2,1,0:T(8,128)(2,1)S(1)}, u32[]{:S(2)}, u32[]{:S(2)}) %all-to-all-start.1) | async-done | bytes 393248 | tf_op jit(solution)/shard_map/all_to_all | solution.py:80
  44.8 6.3 %collective-permute-start.3 = (bf16[48,32,128]{2,1,0:T(8,128)(2,1)S(1)}, bf16[48,32,128]{2,1,0:T(8,128)(2,1)S(1)}, u32[]{:S(2)}, u32[]{:S(2)}) collective-permute-start(bf16[48,32,128]{2,1,0:T(8,128)(2,1)S(1)} %bitcast.15), channel_id=1, source_target_pairs={{0,8},{8,0},{1,9},{9,1},{2,10},{10,2},{3,11},{11,3},{4,12},{12,4},... | collective-permute-start | bytes 1179656 | tf_op jit(solution)/shard_map/ppermute | solution.py:82
  51.2 0.0 copy-done.4
  51.2 0.1 copy.8
  51.3 0.1 copy.12.columns
  51.3 0.0 copy-start.2
  51.3 0.0 copy-start.1
  51.3 0.1 pad_add_fusion.place
  51.4 1.1 %collective-permute-done.3.other = bf16[48,32,128]{2,1,0:T(8,128)(2,1)S(1)} collective-permute-done((bf16[48,32,128]{2,1,0:T(8,128)(2,1)S(1)}, bf16[48,32,128]{2,1,0:T(8,128)(2,1)S(1)}, u32[]{:S(2)}, u32[]{:S(2)}) %collective-permute-start.3) | collective-permute-done | bytes 393248 | tf_op jit(solution)/shard_map/ppermute | solution.py:82
  52.5 0.0 copy-done
  52.5 0.0 copy-done.2
  52.5 0.0 copy-done.1
  52.5 3.5 %shard_map.64 = f32[2,128,1024]{2,1,0:T(8,128)} custom-call(s32[3]{0:T(128)S(1)} %pad_add_fusion.place, s32[8,8]{1,0:T(8,128)S(1)} %copy-done.1, s32[8,48]{1,0:T(8,128)S(1)} %copy.12.columns, f32[8,9]{1,0:T(8,128)S(1)} %copy-done.2, bf16[2,2,144,128]{3,2,1,0:T(8,128)(2,1)S(1)} %pad_maximum_fusion.near, ...), custom_call_target="tpu_custom_call" | custom-call | tf_op jit(solution)/shard_map/pallas_call | solution.py:85
  (9 shorter events, 0.1 us)
Async XLA Ops:
  0.8 5.6 %copy-start.3 = (bf16[4,32,256]{2,1,0:T(8,128)(2,1)S(1)}, bf16[4,32,256]{2,1,0:T(8,128)(2,1)}, u32[]{:S(2)}) copy-start(bf16[4,32,256]{2,1,0:T(8,128)(2,1)} %param.6) | copy-start | bytes 196612
  1.5 11.1 %all-to-all-start = ((bf16[4,32,128]{2,1,0:T(8,128)(2,1)}), bf16[4,32,128]{2,1,0:T(8,128)(2,1)S(1)}, u32[]{:S(2)}, u32[]{:S(2)}) async-start(bf16[4,32,128]{2,1,0:T(8,128)(2,1)} %broadcast_in_dim.17), calls=%async_computation | async-start | bytes 65536 | tf_op jit(solution)/shard_map/all_to_all | solution.py:74
  6.4 46.1 %copy-start = (f32[2,4,32,1024]{3,2,1,0:T(8,128)S(1)}, f32[2,4,32,1024]{3,2,1,0:T(8,128)}, u32[]{:S(2)}) copy-start(f32[2,4,32,1024]{3,2,1,0:T(8,128)} %param.7) | copy-start | bytes 3145732
  6.4 6.3 %collective-permute-start = (bf16[4,4,256]{2,1,0:T(4,128)(2,1)S(1)}, bf16[4,4,256]{2,1,0:T(4,128)(2,1)S(1)}, u32[]{:S(2)}, u32[]{:S(2)}) collective-permute-start(bf16[4,4,256]{2,1,0:T(4,128)(2,1)S(1)} %constant_dynamic-slice_fusion), channel_id=1, source_target_pairs={{0,7},{1,6},{2,5},{3,4},{4,3},{5,2},{6,1},{7,0},{8,15},{9,14},{10,... | collective-permute-start | bytes 24584 | tf_op jit(solution)/shard_map/ppermute | solution.py:73
  13.5 31.3 %all-to-all-start.1 = ((bf16[12,4,32,128]{3,2,1,0:T(8,128)(2,1)}), bf16[12,4,32,128]{3,2,1,0:T(8,128)(2,1)S(1)}, u32[]{:S(2)}, u32[]{:S(2)}) async-start(bf16[12,4,32,128]{3,2,1,0:T(8,128)(2,1)} %broadcast_in_dim.19), calls=%async_computation.1 | async-start | bytes 786432 | tf_op jit(solution)/shard_map/all_to_all | solution.py:80
  28.4 6.2 %collective-permute-start.1 = (bf16[1,2,144,128]{3,2,1,0:T(8,128)(2,1)S(1)}, bf16[1,2,144,128]{3,2,1,0:T(8,128)(2,1)S(1)}, u32[]{:S(2)}, u32[]{:S(2)}) collective-permute-start(bf16[1,2,144,128]{3,2,1,0:T(8,128)(2,1)S(1)} %maximum_bitcast_fusion), channel_id=1, source_target_pairs={{0,2},{2,0},{4,6},{6,4},{1,3},{3,1},{5,7},{7,5},{8,10},{10,8},{12,... | collective-permute-start | bytes 221192 | tf_op jit(solution)/shard_map/ppermute | solution.py:78
  34.7 16.5 %copy-start.4 = (s32[8,16,3]{1,0,2:T(8,128)S(1)}, s32[8,16,3]{1,0,2:T(8,128)}, u32[]{:S(2)}) copy-start(s32[8,16,3]{1,0,2:T(8,128)} %param.11) | copy-start | bytes 4612
  34.7 8.5 %collective-permute-start.2 = (bf16[2,2,144,128]{3,2,1,0:T(8,128)(2,1)S(1)}, bf16[2,2,144,128]{3,2,1,0:T(8,128)(2,1)S(1)}, u32[]{:S(2)}, u32[]{:S(2)}) collective-permute-start(bf16[2,2,144,128]{3,2,1,0:T(8,128)(2,1)S(1)} %pad_maximum_fusion.near), channel_id=1, source_target_pairs={{0,4},{2,6},{4,0},{6,2},{1,5},{3,7},{5,1},{7,3},{8,12},{10,14},{12... | collective-permute-start | bytes 442376 | tf_op jit(solution)/shard_map/ppermute | solution.py:79
  44.8 7.7 %collective-permute-start.3 = (bf16[48,32,128]{2,1,0:T(8,128)(2,1)S(1)}, bf16[48,32,128]{2,1,0:T(8,128)(2,1)S(1)}, u32[]{:S(2)}, u32[]{:S(2)}) collective-permute-start(bf16[48,32,128]{2,1,0:T(8,128)(2,1)S(1)} %bitcast.15), channel_id=1, source_target_pairs={{0,8},{8,0},{1,9},{9,1},{2,10},{10,2},{3,11},{11,3},{4,12},{12,4},... | collective-permute-start | bytes 1179656 | tf_op jit(solution)/shard_map/ppermute | solution.py:82
  51.3 1.2 %copy-start.2 = (f32[8,9]{1,0:T(8,128)S(1)}, f32[8,9]{1,0:T(8,128)}, u32[]{:S(2)}) copy-start(f32[8,9]{1,0:T(8,128)} %weights.1) | copy-start | bytes 868
  51.3 1.2 %copy-start.1 = (s32[8,8]{1,0:T(8,128)S(1)}, s32[8,8]{1,0:T(8,128)}, u32[]{:S(2)}) copy-start(s32[8,8]{1,0:T(8,128)} %sources.1) | copy-start | bytes 772

commit v3 on v1

--- a/solution.py
+++ b/solution.py
@@ -12,8 +12,11 @@
 BAND = 3
 
 
-def fused(place, sources, columns, weights, seen, mine, other, observed, ratio, dense, flat):
+def fused(place, sources, columns, weights, own, one, two, three, edge, mine, other, observed, ratio, dense, flat, seen):
     view, side, core = place[0], place[1], place[2]
+    for k, part in enumerate((own, one, two, three)):
+        seen[view ^ k, :, :OWN] = part[...]
+        seen[view ^ 3 ^ k, :, OWN:] = edge[k]
     dense[...] = jnp.zeros_like(dense)
     for w in range(2):
         for i in range(2 * BLOCKS):
@@ -22,23 +25,25 @@
                 shift = (columns[2 * view + w, i * BAND + k] - (2 * j - 2)) & 15
                 base = shift * 64
                 lanes = pl.ds(64 * half, 64)
+                q = i * BAND + k
+                s = q % 4 * 12 + q // 4
                 dense[w, j, pl.ds(pl.multiple_of(base + 32 * core, 32), 32), lanes] = mine[
-                    i * BAND + k, :, 64 * w : 64 * w + 64
+                    s, :, 64 * w : 64 * w + 64
                 ]
                 dense[w, j, pl.ds(pl.multiple_of(base + 32 * (1 - core), 32), 32), lanes] = other[
-                    i * BAND + k, :, 64 * w : 64 * w + 64
+                    s, :, 64 * w : 64 * w + 64
                 ]
 
     def block(w, j):
         b = sources[2 * view + w, j % BLOCKS]
         p, half = b // 2, b % 2
-        return jnp.concatenate([seen[p, half, :OWN], seen[3 - p, half, OWN:]], axis=0)
+        return seen[p, half]
 
     for w in range(2):
         for j in range(BLOCKS):
-            near = jnp.concatenate([block(w, j + BLOCKS - 1), block(w, j), block(w, j + 1)], axis=1)
+            wide = jnp.concatenate([block(w, j + BLOCKS - 1), block(w, j), block(w, j + 1)], axis=1)
             flat[w, :, 128 * j : 128 * j + 128] = jnp.dot(
-                near, dense[w, j], preferred_element_type=jnp.float32
+                wide, dense[w, j], preferred_element_type=jnp.float32
             ).astype(jnp.bfloat16)
 
     shape = (OWN, OWN + EDGE)
@@ -64,26 +69,28 @@
     side = lax.axis_index("gy")
     place = jnp.stack([lax.axis_index("view"), side, lax.axis_index("core")]).astype(jnp.int32)
     shard = psf_blocks.reshape(2, 32, 64).transpose(1, 0, 2).reshape(1, 32, 128)
-    edge = lax.dynamic_slice_in_dim(estimate, jnp.where(side == 0, ROWS - HALO, 0), HALO, 1)
+    along = lax.all_to_all(jnp.broadcast_to(shard, (12, 32, 128)), "z", 0, 0, tiled=True)
+    slab = estimate.reshape(PLANES, ROWS, 2, 128).transpose(2, 0, 1, 3)
+    parts = [lax.ppermute(slab, "view", [(i, i ^ k) for i in range(4)]) for k in (1, 2, 3)]
+    along, *parts = lax.optimization_barrier((along, *parts))
+    mine = lax.all_to_all(jnp.broadcast_to(along[None], (4, 12, 32, 128)), "x", 0, 0, tiled=True)
+    begin = jnp.where(side == 0, ROWS - HALO, 0)
+    edge = jnp.stack([lax.dynamic_slice_in_dim(part, begin, HALO, 2) for part in (slab, *parts)])
     mirror = [(v * 2 + g, (3 - v) * 2 + (1 - g)) for v in range(4) for g in range(2)]
-    edge = lax.ppermute(edge, ("view", "gy"), mirror)
-    across = lax.all_to_all(jnp.broadcast_to(shard, (4, 32, 128)), "x", 0, 0, tiled=True)
-    slab = jnp.concatenate([estimate.reshape(OWN, 2, 128), edge.reshape(EDGE, 2, 128)], axis=0)
-    slab = slab.transpose(1, 0, 2)
-    seen = lax.all_to_all(jnp.broadcast_to(slab[None], (4, *slab.shape)), "view", 0, 0, tiled=True)
-    mine = lax.all_to_all(jnp.broadcast_to(across[None], (12, 4, 32, 128)), "z", 0, 0, tiled=True)
-    mine = mine.reshape(48, 32, 128)
+    edge = lax.ppermute(edge, ("view", "gy"), mirror).reshape(4, 2, EDGE, 128)
+    mine, edge = lax.optimization_barrier((mine.reshape(48, 32, 128), edge))
     other = lax.ppermute(mine, "core", [(0, 1), (1, 0)])
     smem = pl.BlockSpec(memory_space=pltpu.SMEM)
     vmem = pl.BlockSpec(memory_space=pltpu.VMEM)
     ratio = pl.pallas_call(
         fused,
         out_shape=jax.ShapeDtypeStruct((2, OWN, 1024), jnp.float32),
-        in_specs=[smem] * 4 + [vmem] * 4,
+        in_specs=[smem] * 4 + [vmem] * 8,
         out_specs=vmem,
         scratch_shapes=[
             pltpu.VMEM((2, BLOCKS, 384, 128), jnp.bfloat16),
             pltpu.VMEM((2, OWN + EDGE, 1024), jnp.bfloat16),
+            pltpu.VMEM((4, 2, OWN + EDGE, 128), jnp.bfloat16),
         ],
         compiler_params=pltpu.CompilerParams(vmem_limit_bytes=32 * 1024 * 1024),
     )(
@@ -91,7 +98,8 @@
         block_source,
         psf_columns.reshape(8, 48),
         kernel_y,
-        seen,
+        *[part.reshape(2, OWN, 128) for part in (slab, *parts)],
+        edge,
         mine,
         other,
         observed.reshape(2, OWN, 1024),

time: 63.9 us -> 54.7 us (0.86)
  the two profiles are of different devices: /device:TPU:64 before, /device:TPU:1 now
where the time goes in v3:
time: 54.7 us; the launch traced here: 54.2 us
  starting transfers between devices  39.4 us (72%)
  waiting for transfers between devices  7.72 us (14%)
  Pallas kernels  3.54 us (6%)
  local copies, waits for them, and re-layouts  3.32 us (6%)
    all_to_all x1, starting transfers between devices, shards(): lax.all_to_all(jnp.broadcast_to(shard, (12, 32, 128)), 'z', 0, 0, tiled=T...  15.7 us
    ppermute x3, starting transfers between devices, shards(): lax.ppermute(slab, 'view', [(i, i ^ k) for i in range(4)])  9.34 us
    ppermute x1, starting transfers between devices, shards(): other = lax.ppermute(mine, 'core', [(0, 1), (1, 0)])  5.93 us
    ppermute x3, waiting for transfers between devices, shards(): lax.ppermute(slab, 'view', [(i, i ^ k) for i in range(4)])  4.91 us
    ppermute x1, starting transfers between devices, shards(): edge = lax.ppermute(edge, ('view', 'gy'), mirror).reshape(4, 2, EDGE, 128)  4.39 us
    all_to_all x1, starting transfers between devices, shards(): lax.all_to_all(jnp.broadcast_to(along[None], (4, 12, 32, 128)), 'x', 0, 0...  4.01 us
    pallas_call x1, Pallas kernels, shards(): pl.pallas_call(fused, out_shape=jax.ShapeDtypeStruct((2, OWN, 1024), jnp....  3.54 us
    ppermute x1, waiting for transfers between devices, shards(): edge = lax.ppermute(edge, ('view', 'gy'), mirror).reshape(4, 2, EDGE, 128)  1.47 us
  transfers between devices with their start and end apart: 7, of which 5 were waited for; matrix products, arithmetic and copies ran while one was open for 1% of the time, Pallas kernels for 0%

profile of v3, /device:TPU:1, one launch (start us, length us, event | category | flops | bytes accessed | tf_op | source)
XLA Modules:
  0.0 54.2 jit_solution(16255861234846516576)
XLA Ops:
  0.0 0.0 copy-start
  0.0 0.8 %reshape.39 = bf16[2,32,64]{2,1,0:T(8,128)(2,1)S(1)} reshape(bf16[2,2048]{1,0:T(2,128)(2,1)} %param.8) | data formatting | bytes 16384 | tf_op jit(solution)/shard_map/reshape | solution.py:71
  0.8 0.1 broadcast_in_dim.6
  0.9 0.0 copy-start.1
  0.9 0.7 %broadcast_in_dim.14 = bf16[12,32,128]{2,1,0:T(8,128)(2,1)} broadcast(bf16[32,128]{1,0:T(8,128)(2,1)S(1)} %broadcast_in_dim.6), dimensions={1,2} | broadcast | bytes 106496 | tf_op jit(solution)/shard_map/broadcast_in_dim | solution.py:72
  1.6 15.7 %all-to-all-start = ((bf16[12,32,128]{2,1,0:T(8,128)(2,1)}), bf16[12,32,128]{2,1,0:T(8,128)(2,1)S(1)}, u32[]{:S(2)}, u32[]{:S(2)}) async-start(bf16[12,32,128]{2,1,0:T(8,128)(2,1)} %broadcast_in_dim.14), calls=%async_computation | async-start | bytes 196608 | tf_op jit(solution)/shard_map/all_to_all | solution.py:72
  17.3 0.0 copy-done
  17.3 4.2 %collective-permute-start.1 = (bf16[2,4,32,128]{3,2,1,0:T(8,128)(2,1)S(1)}, bf16[2,4,32,128]{3,2,1,0:T(8,128)(2,1)S(1)}, u32[]{:S(2)}, u32[]{:S(2)}) collective-permute-start(bf16[2,4,32,128]{3,2,1,0:T(8,128)(2,1)S(1)} %get-tuple-element.17), channel_id=1, source_target_pairs={{0,4},{2,6},{4,0},{6,2},{1,5},{3,7},{5,1},{7,3},{8,12},{10,14},{12... | collective-permute-start | bytes 196616 | tf_op jit(solution)/shard_map/ppermute | solution.py:74
  21.6 3.2 %collective-permute-start = (bf16[2,4,32,128]{3,2,1,0:T(8,128)(2,1)S(1)}, bf16[2,4,32,128]{3,2,1,0:T(8,128)(2,1)S(1)}, u32[]{:S(2)}, u32[]{:S(2)}) collective-permute-start(bf16[2,4,32,128]{3,2,1,0:T(8,128)(2,1)S(1)} %get-tuple-element.17), channel_id=1, source_target_pairs={{0,2},{2,0},{4,6},{6,4},{1,3},{3,1},{5,7},{7,5},{8,10},{10,8},{12,... | collective-permute-start | bytes 196616 | tf_op jit(solution)/shard_map/ppermute | solution.py:74
  24.8 1.9 %collective-permute-start.2 = (bf16[2,4,32,128]{3,2,1,0:T(8,128)(2,1)S(1)}, bf16[2,4,32,128]{3,2,1,0:T(8,128)(2,1)S(1)}, u32[]{:S(2)}, u32[]{:S(2)}) collective-permute-start(bf16[2,4,32,128]{3,2,1,0:T(8,128)(2,1)S(1)} %get-tuple-element.17), channel_id=1, source_target_pairs={{0,6},{2,4},{4,2},{6,0},{1,7},{3,5},{5,3},{7,1},{8,14},{10,12},{12... | collective-permute-start | bytes 196616 | tf_op jit(solution)/shard_map/ppermute | solution.py:74
  26.7 0.0 collective-permute-done.1
  26.7 0.1 collective-permute-done
  26.9 4.8 %collective-permute-done.2 = bf16[2,4,32,128]{3,2,1,0:T(8,128)(2,1)S(1)} collective-permute-done((bf16[2,4,32,128]{3,2,1,0:T(8,128)(2,1)S(1)}, bf16[2,4,32,128]{3,2,1,0:T(8,128)(2,1)S(1)}, u32[]{:S(2)}, u32[]{:S(2)}) %collective-permute-start.2) | collective-permute-done | bytes 65568 | tf_op jit(solution)/shard_map/ppermute | solution.py:74
  31.6 0.0 all-to-all-done
  31.6 0.8 %broadcast_in_dim.15 = bf16[4,12,32,128]{3,2,1,0:T(8,128)(2,1)} broadcast(bf16[12,32,128]{2,1,0:T(8,128)(2,1)S(1)} %all-to-all-done), dimensions={1,2,3} | broadcast | bytes 491520 | tf_op jit(solution)/shard_map/broadcast_in_dim | solution.py:76
  32.5 4.0 %all-to-all-start.1 = ((bf16[4,12,32,128]{3,2,1,0:T(8,128)(2,1)}), bf16[4,12,32,128]{3,2,1,0:T(8,128)(2,1)S(1)}, u32[]{:S(2)}, u32[]{:S(2)}) async-start(bf16[4,12,32,128]{3,2,1,0:T(8,128)(2,1)} %broadcast_in_dim.15), calls=%async_computation.1 | async-start | bytes 786432 | tf_op jit(solution)/shard_map/all_to_all | solution.py:76
  36.6 0.0 copy-start.4
  36.6 4.4 %collective-permute-start.3 = (bf16[4,2,4,4,128]{4,3,2,1,0:T(4,128)(2,1)S(1)}, bf16[4,2,4,4,128]{4,3,2,1,0:T(4,128)(2,1)S(1)}, u32[]{:S(2)}, u32[]{:S(2)}) collective-permute-start(bf16[4,2,4,4,128]{4,3,2,1,0:T(4,128)(2,1)S(1)} %pad_maximum_fusion), channel_id=1, source_target_pairs={{0,7},{1,6},{2,5},{3,4},{4,3},{5,2},{6,1},{7,0},{8,15},{9,14},{10,... | collective-permute-start | bytes 98312 | tf_op jit(solution)/shard_map/ppermute | solution.py:80
  41.0 1.5 %collective-permute-done.3 = bf16[4,2,4,4,128]{4,3,2,1,0:T(4,128)(2,1)S(1)} collective-permute-done((bf16[4,2,4,4,128]{4,3,2,1,0:T(4,128)(2,1)S(1)}, bf16[4,2,4,4,128]{4,3,2,1,0:T(4,128)(2,1)S(1)}, u32[]{:S(2)}, u32[]{:S(2)}) %collective-permute-start.3) | collective-permute-done | bytes 32800 | tf_op jit(solution)/shard_map/ppermute | solution.py:80
  42.4 0.3 all-to-all-done.1
  42.7 5.9 %collective-permute-start.4 = (bf16[48,32,128]{2,1,0:T(8,128)(2,1)S(1)}, bf16[48,32,128]{2,1,0:T(8,128)(2,1)S(1)}, u32[]{:S(2)}, u32[]{:S(2)}) collective-permute-start(bf16[48,32,128]{2,1,0:T(8,128)(2,1)S(1)} %bitcast.36), channel_id=1, source_target_pairs={{0,8},{8,0},{1,9},{9,1},{2,10},{10,2},{3,11},{11,3},{4,12},{12,4},... | collective-permute-start | bytes 1179656 | tf_op jit(solution)/shard_map/ppermute | solution.py:82
  48.6 0.0 copy-done.4
  48.7 0.1 copy.10
  48.8 0.1 copy.14.columns
  48.8 0.1 pad_add_fusion.place
  48.9 1.1 %collective-permute-done.4.other = bf16[48,32,128]{2,1,0:T(8,128)(2,1)S(1)} collective-permute-done((bf16[48,32,128]{2,1,0:T(8,128)(2,1)S(1)}, bf16[48,32,128]{2,1,0:T(8,128)(2,1)S(1)}, u32[]{:S(2)}, u32[]{:S(2)}) %collective-permute-start.4) | collective-permute-done | bytes 393248 | tf_op jit(solution)/shard_map/ppermute | solution.py:82
  50.0 0.0 copy-start.3
  50.0 0.0 copy-start.2
  50.0 0.0 copy-done.1
  50.0 0.7 %copy-done.3 = f32[8,9]{1,0:T(8,128)S(1)} copy-done((f32[8,9]{1,0:T(8,128)S(1)}, f32[8,9]{1,0:T(8,128)}, u32[]{:S(2)}) %copy-start.3) | copy-done | bytes 312
  50.7 0.0 copy-done.2
  50.7 3.5 %shard_map.64 = f32[2,128,1024]{2,1,0:T(8,128)} custom-call(s32[3]{0:T(128)S(1)} %pad_add_fusion.place, s32[8,8]{1,0:T(8,128)S(1)} %copy-done.2, s32[8,48]{1,0:T(8,128)S(1)} %copy.14.columns, f32[8,9]{1,0:T(8,128)S(1)} %copy-done.3, bf16[2,128,128]{2,1,0:T(8,128)(2,1)S(1)} %bitcast.39, bf16[2,128,128]{2,1,0:T(8,128)(2,1)S(1)} %bitcast.40, ...), custom_call_target="tpu_custom_call" | custom-call | tf_op jit(solution)/shard_map/pallas_call | solution.py:85
  (7 shorter events, 0.1 us)
Async XLA Ops:
  0.0 17.3 %copy-start = (bf16[4,32,256]{2,1,0:T(8,128)(2,1)S(1)}, bf16[4,32,256]{2,1,0:T(8,128)(2,1)}, u32[]{:S(2)}) copy-start(bf16[4,32,256]{2,1,0:T(8,128)(2,1)} %param.6) | copy-start | bytes 196612
  0.9 49.0 %copy-start.1 = (f32[2,4,32,1024]{3,2,1,0:T(8,128)S(1)}, f32[2,4,32,1024]{3,2,1,0:T(8,128)}, u32[]{:S(2)}) copy-start(f32[2,4,32,1024]{3,2,1,0:T(8,128)} %param.7) | copy-start | bytes 3145732
  1.6 30.1 %all-to-all-start = ((bf16[12,32,128]{2,1,0:T(8,128)(2,1)}), bf16[12,32,128]{2,1,0:T(8,128)(2,1)S(1)}, u32[]{:S(2)}, u32[]{:S(2)}) async-start(bf16[12,32,128]{2,1,0:T(8,128)(2,1)} %broadcast_in_dim.14), calls=%async_computation | async-start | bytes 196608 | tf_op jit(solution)/shard_map/all_to_all | solution.py:72
  17.3 9.4 %collective-permute-start.1 = (bf16[2,4,32,128]{3,2,1,0:T(8,128)(2,1)S(1)}, bf16[2,4,32,128]{3,2,1,0:T(8,128)(2,1)S(1)}, u32[]{:S(2)}, u32[]{:S(2)}) collective-permute-start(bf16[2,4,32,128]{3,2,1,0:T(8,128)(2,1)S(1)} %get-tuple-element.17), channel_id=1, source_target_pairs={{0,4},{2,6},{4,0},{6,2},{1,5},{3,7},{5,1},{7,3},{8,12},{10,14},{12... | collective-permute-start | bytes 196616 | tf_op jit(solution)/shard_map/ppermute | solution.py:74
  21.6 5.3 %collective-permute-start = (bf16[2,4,32,128]{3,2,1,0:T(8,128)(2,1)S(1)}, bf16[2,4,32,128]{3,2,1,0:T(8,128)(2,1)S(1)}, u32[]{:S(2)}, u32[]{:S(2)}) collective-permute-start(bf16[2,4,32,128]{3,2,1,0:T(8,128)(2,1)S(1)} %get-tuple-element.17), channel_id=1, source_target_pairs={{0,2},{2,0},{4,6},{6,4},{1,3},{3,1},{5,7},{7,5},{8,10},{10,8},{12,... | collective-permute-start | bytes 196616 | tf_op jit(solution)/shard_map/ppermute | solution.py:74
  24.8 6.9 %collective-permute-start.2 = (bf16[2,4,32,128]{3,2,1,0:T(8,128)(2,1)S(1)}, bf16[2,4,32,128]{3,2,1,0:T(8,128)(2,1)S(1)}, u32[]{:S(2)}, u32[]{:S(2)}) collective-permute-start(bf16[2,4,32,128]{3,2,1,0:T(8,128)(2,1)S(1)} %get-tuple-element.17), channel_id=1, source_target_pairs={{0,6},{2,4},{4,2},{6,0},{1,7},{3,5},{5,3},{7,1},{8,14},{10,12},{12... | collective-permute-start | bytes 196616 | tf_op jit(solution)/shard_map/ppermute | solution.py:74
  32.5 10.2 %all-to-all-start.1 = ((bf16[4,12,32,128]{3,2,1,0:T(8,128)(2,1)}), bf16[4,12,32,128]{3,2,1,0:T(8,128)(2,1)S(1)}, u32[]{:S(2)}, u32[]{:S(2)}) async-start(bf16[4,12,32,128]{3,2,1,0:T(8,128)(2,1)} %broadcast_in_dim.15), calls=%async_computation.1 | async-start | bytes 786432 | tf_op jit(solution)/shard_map/all_to_all | solution.py:76
  36.6 12.1 %copy-start.4 = (s32[8,16,3]{1,0,2:T(8,128)S(1)}, s32[8,16,3]{1,0,2:T(8,128)}, u32[]{:S(2)}) copy-start(s32[8,16,3]{1,0,2:T(8,128)} %param.11) | copy-start | bytes 4612
  36.6 5.9 %collective-permute-start.3 = (bf16[4,2,4,4,128]{4,3,2,1,0:T(4,128)(2,1)S(1)}, bf16[4,2,4,4,128]{4,3,2,1,0:T(4,128)(2,1)S(1)}, u32[]{:S(2)}, u32[]{:S(2)}) collective-permute-start(bf16[4,2,4,4,128]{4,3,2,1,0:T(4,128)(2,1)S(1)} %pad_maximum_fusion), channel_id=1, source_target_pairs={{0,7},{1,6},{2,5},{3,4},{4,3},{5,2},{6,1},{7,0},{8,15},{9,14},{10,... | collective-permute-start | bytes 98312 | tf_op jit(solution)/shard_map/ppermute | solution.py:80
  42.7 7.3 %collective-permute-start.4 = (bf16[48,32,128]{2,1,0:T(8,128)(2,1)S(1)}, bf16[48,32,128]{2,1,0:T(8,128)(2,1)S(1)}, u32[]{:S(2)}, u32[]{:S(2)}) collective-permute-start(bf16[48,32,128]{2,1,0:T(8,128)(2,1)S(1)} %bitcast.36), channel_id=1, source_target_pairs={{0,8},{8,0},{1,9},{9,1},{2,10},{10,2},{3,11},{11,3},{4,12},{12,4},... | collective-permute-start | bytes 1179656 | tf_op jit(solution)/shard_map/ppermute | solution.py:82
  50.0 0.7 %copy-start.3 = (f32[8,9]{1,0:T(8,128)S(1)}, f32[8,9]{1,0:T(8,128)}, u32[]{:S(2)}) copy-start(f32[8,9]{1,0:T(8,128)} %weights.1) | copy-start | bytes 868
  50.0 0.7 %copy-start.2 = (s32[8,8]{1,0:T(8,128)S(1)}, s32[8,8]{1,0:T(8,128)}, u32[]{:S(2)}) copy-start(s32[8,8]{1,0:T(8,128)} %sources.1) | copy-start | bytes 772

commit v4 on v3

--- a/solution.py
+++ b/solution.py
@@ -10,9 +10,10 @@
 EDGE = PLANES * HALO
 BLOCKS = 8
 BAND = 3
+AHEAD = 4
 
 
-def fused(place, sources, columns, weights, own, one, two, three, edge, mine, other, observed, ratio, dense, flat, seen):
+def fused(place, numbers, weights, own, one, two, three, edge, mine, other, observed, ratio, dense, flat, seen):
     view, side, core = place[0], place[1], place[2]
     for k, part in enumerate((own, one, two, three)):
         seen[view ^ k, :, :OWN] = part[...]
@@ -22,7 +23,7 @@
         for i in range(2 * BLOCKS):
             j, half = i // 2, i % 2
             for k in range(BAND):
-                shift = (columns[2 * view + w, i * BAND + k] - (2 * j - 2)) & 15
+                shift = (numbers[w, BLOCKS + i * BAND + k] - (2 * j - 2)) & 15
                 base = shift * 64
                 lanes = pl.ds(64 * half, 64)
                 q = i * BAND + k
@@ -35,7 +36,7 @@
                 ]
 
     def block(w, j):
-        b = sources[2 * view + w, j % BLOCKS]
+        b = numbers[w, j % BLOCKS]
         p, half = b // 2, b % 2
         return seen[p, half]
 
@@ -56,7 +57,7 @@
     for w in range(2):
         mix = jnp.zeros(shape, jnp.float32)
         for t in range(2 * HALO + 1):
-            mix = jnp.where(tap == t, weights[2 * view + w, t], mix)
+            mix = jnp.where(tap == t, weights[w, t], mix)
         high = mix.astype(jnp.bfloat16)
         low = (mix - high.astype(jnp.float32)).astype(jnp.bfloat16)
         lateral = flat[w]
@@ -65,27 +66,42 @@
         ratio[w] = observed[w] / blurred
 
 
+def swap(array, k, planes):
+    return lax.ppermute(array, ("z", "view"), [(4 * z + v, 4 * z + (v ^ k)) for z in planes for v in range(4)])
+
+
 def shards(estimate, observed, psf_blocks, kernel_y, block_source, psf_columns):
     side = lax.axis_index("gy")
     place = jnp.stack([lax.axis_index("view"), side, lax.axis_index("core")]).astype(jnp.int32)
     shard = psf_blocks.reshape(2, 32, 64).transpose(1, 0, 2).reshape(1, 32, 128)
-    along = lax.all_to_all(jnp.broadcast_to(shard, (12, 32, 128)), "z", 0, 0, tiled=True)
     slab = estimate.reshape(PLANES, ROWS, 2, 128).transpose(2, 0, 1, 3)
-    parts = [lax.ppermute(slab, "view", [(i, i ^ k) for i in range(4)]) for k in (1, 2, 3)]
-    along, *parts = lax.optimization_barrier((along, *parts))
+    spread = jnp.broadcast_to(shard, (12, 32, 128))
+    ahead = swap(slab, 2, range(AHEAD))
+    ahead, spread, estimate = lax.optimization_barrier((ahead, spread, estimate))
+    slab = estimate.reshape(PLANES, ROWS, 2, 128).transpose(2, 0, 1, 3)
+    along = lax.all_to_all(spread, "z", 0, 0, tiled=True)
+    parts = [swap(slab, 1, range(12)), swap(slab, 2, range(AHEAD, 12)), swap(slab, 3, range(12))]
+    along, slab, *parts = lax.optimization_barrier((along, slab, *parts))
+    parts[1] = jnp.where(lax.axis_index("z") < AHEAD, ahead, parts[1])
     mine = lax.all_to_all(jnp.broadcast_to(along[None], (4, 12, 32, 128)), "x", 0, 0, tiled=True)
     begin = jnp.where(side == 0, ROWS - HALO, 0)
     edge = jnp.stack([lax.dynamic_slice_in_dim(part, begin, HALO, 2) for part in (slab, *parts)])
     mirror = [(v * 2 + g, (3 - v) * 2 + (1 - g)) for v in range(4) for g in range(2)]
     edge = lax.ppermute(edge, ("view", "gy"), mirror).reshape(4, 2, EDGE, 128)
-    mine, edge = lax.optimization_barrier((mine.reshape(48, 32, 128), edge))
+    mine, edge, kernel_y, block_source, psf_columns = lax.optimization_barrier(
+        (mine.reshape(48, 32, 128), edge, kernel_y, block_source, psf_columns)
+    )
+    first = 2 * lax.axis_index("view")
+    numbers = jnp.concatenate([block_source, psf_columns.reshape(8, 48)], axis=1)
+    numbers = lax.dynamic_slice_in_dim(numbers, first, 2, 0)
+    weights = lax.dynamic_slice_in_dim(kernel_y, first, 2, 0)
     other = lax.ppermute(mine, "core", [(0, 1), (1, 0)])
     smem = pl.BlockSpec(memory_space=pltpu.SMEM)
     vmem = pl.BlockSpec(memory_space=pltpu.VMEM)
     ratio = pl.pallas_call(
         fused,
         out_shape=jax.ShapeDtypeStruct((2, OWN, 1024), jnp.float32),
-        in_specs=[smem] * 4 + [vmem] * 8,
+        in_specs=[smem] * 3 + [vmem] * 8,
         out_specs=vmem,
         scratch_shapes=[
             pltpu.VMEM((2, BLOCKS, 384, 128), jnp.bfloat16),
@@ -95,9 +111,8 @@
         compiler_params=pltpu.CompilerParams(vmem_limit_bytes=32 * 1024 * 1024),
     )(
         place,
-        block_source,
-        psf_columns.reshape(8, 48),
-        kernel_y,
+        numbers,
+        weights,
         *[part.reshape(2, OWN, 128) for part in (slab, *parts)],
         edge,
         mine,

time: 54.7 us -> 53 us (0.969)
  waiting for transfers between devices: 7.72 us -> 6.72 us
  starting transfers between devices: 39.4 us -> 38.6 us
    all_to_all x1, starting transfers between devices: 15.7 us -> 10 us  [shards(): along = lax.all_to_all(spread, 'z', 0, 0, tiled=True)]
    ppermute x3 -> x4, starting transfers between devices: 9.34 us -> 12.9 us  [swap(): lax.ppermute(array, ('z', 'view'), [(4 * z + v, 4 * z + (v ^ k)) for z in...]
    ppermute x1, starting transfers between devices: 5.93 us -> 7.25 us  [shards(): other = lax.ppermute(mine, 'core', [(0, 1), (1, 0)])]
    ppermute x1, waiting for transfers between devices: 1.07 us -> 0.28 us  [shards(): other = lax.ppermute(mine, 'core', [(0, 1), (1, 0)])]
    reshape x2, local copies, waits for them, and re-layouts: 0.83 us -> 0.1 us  [shards(): shard = psf_blocks.reshape(2, 32, 64).transpose(1, 0, 2).reshape(1, 32, 128)]
    dynamic_slice x0 -> x2, local copies, waits for them, and re-layouts: none -> 0.71 us  [the longest x1 0.7 us: shards(): weights = lax.dynamic_slice_in_dim(kernel_y, first, 2, 0)]
    ppermute x3 -> x4, waiting for transfers between devices: 4.91 us -> 4.78 us  [swap(): lax.ppermute(array, ('z', 'view'), [(4 * z + v, 4 * z + (v ^ k)) for z in...]
  transfers between devices with their start and end apart: 7 -> 8, of which waited for: 5 -> 5; matrix products, arithmetic and copies ran while one was open for 1% -> 3% of each run, Pallas kernels for 0% -> 0%
where the time goes in v4:
time: 53 us; the launch traced here: 52.5 us
  starting transfers between devices  38.6 us (73%)
  waiting for transfers between devices  6.72 us (13%)
  local copies, waits for them, and re-layouts  3.46 us (7%)
  Pallas kernels  3.37 us (6%)
    ppermute x4, starting transfers between devices, swap(): lax.ppermute(array, ('z', 'view'), [(4 * z + v, 4 * z + (v ^ k)) for z in...  12.9 us
    all_to_all x1, starting transfers between devices, shards(): along = lax.all_to_all(spread, 'z', 0, 0, tiled=True)  10 us
    ppermute x1, starting transfers between devices, shards(): other = lax.ppermute(mine, 'core', [(0, 1), (1, 0)])  7.25 us
    ppermute x4, waiting for transfers between devices, swap(): lax.ppermute(array, ('z', 'view'), [(4 * z + v, 4 * z + (v ^ k)) for z in...  4.78 us
    ppermute x1, starting transfers between devices, shards(): edge = lax.ppermute(edge, ('view', 'gy'), mirror).reshape(4, 2, EDGE, 128)  4.41 us
    all_to_all x1, starting transfers between devices, shards(): lax.all_to_all(jnp.broadcast_to(along[None], (4, 12, 32, 128)), 'x', 0, 0...  4.01 us
    pallas_call x1, Pallas kernels, shards(): pl.pallas_call(fused, out_shape=jax.ShapeDtypeStruct((2, OWN, 1024), jnp....  3.37 us
    ppermute x1, waiting for transfers between devices, shards(): edge = lax.ppermute(edge, ('view', 'gy'), mirror).reshape(4, 2, EDGE, 128)  1.43 us
  transfers between devices with their start and end apart: 8, of which 5 were waited for; matrix products, arithmetic and copies ran while one was open for 3% of the time, Pallas kernels for 0%

profile of v4, /device:TPU:1, one launch (start us, length us, event | category | flops | bytes accessed | tf_op | source)
XLA Modules:
  0.0 52.5 jit_solution(14278314345329845392)
XLA Ops:
  0.0 0.0 copy-start
  0.0 0.8 %copy-done = bf16[4,32,256]{2,1,0:T(8,128)(2,1)S(1)} copy-done((bf16[4,32,256]{2,1,0:T(8,128)(2,1)S(1)}, bf16[4,32,256]{2,1,0:T(8,128)(2,1)}, u32[]{:S(2)}) %copy-start) | copy-done | bytes 65560
  0.9 5.0 %collective-permute-start = (bf16[2,4,32,128]{3,2,1,0:T(8,128)(2,1)S(1)}, bf16[2,4,32,128]{3,2,1,0:T(8,128)(2,1)S(1)}, u32[]{:S(2)}, u32[]{:S(2)}) collective-permute-start(bf16[2,4,32,128]{3,2,1,0:T(8,128)(2,1)S(1)} %bitcast_bitcast_fusion.1), channel_id=1, source_target_pairs={{0,4},{2,6},{4,0},{6,2},{64,68},{66,70},{68,64},{70,66},{128,132},... | collective-permute-start | bytes 196616 | tf_op jit(solution)/shard_map/ppermute | solution.py:70
  5.9 0.1 reshape.40
  6.0 0.1 broadcast_in_dim.6
  6.1 1.4 %collective-permute-done = bf16[2,4,32,128]{3,2,1,0:T(8,128)(2,1)S(1)} collective-permute-done((bf16[2,4,32,128]{3,2,1,0:T(8,128)(2,1)S(1)}, bf16[2,4,32,128]{3,2,1,0:T(8,128)(2,1)S(1)}, u32[]{:S(2)}, u32[]{:S(2)}) %collective-permute-start) | collective-permute-done | bytes 65568 | tf_op jit(solution)/shard_map/ppermute | solution.py:70
  7.6 0.7 %broadcast_in_dim.14 = bf16[12,32,128]{2,1,0:T(8,128)(2,1)} broadcast(bf16[32,128]{1,0:T(8,128)(2,1)S(1)} %broadcast_in_dim.6), dimensions={1,2} | broadcast | bytes 106496 | tf_op jit(solution)/shard_map/broadcast_in_dim | solution.py:78
  8.2 10.0 %all-to-all-start = ((bf16[12,32,128]{2,1,0:T(8,128)(2,1)}), bf16[12,32,128]{2,1,0:T(8,128)(2,1)S(1)}, u32[]{:S(2)}, u32[]{:S(2)}) async-start(bf16[12,32,128]{2,1,0:T(8,128)(2,1)} %broadcast_in_dim.14), calls=%async_computation | async-start | bytes 196608 | tf_op jit(solution)/shard_map/all_to_all | solution.py:82
  18.3 5.2 %collective-permute-start.3 = (bf16[2,4,32,128]{3,2,1,0:T(8,128)(2,1)S(1)}, bf16[2,4,32,128]{3,2,1,0:T(8,128)(2,1)S(1)}, u32[]{:S(2)}, u32[]{:S(2)}) collective-permute-start(bf16[2,4,32,128]{3,2,1,0:T(8,128)(2,1)S(1)} %bitcast_bitcast_fusion), channel_id=1, source_target_pairs={{0,6},{2,4},{4,2},{6,0},{64,70},{66,68},{68,66},{70,64},{128,134},... | collective-permute-start | bytes 196616 | tf_op jit(solution)/shard_map/ppermute | solution.py:70
  23.5 0.7 %collective-permute-start.2 = (bf16[2,4,32,128]{3,2,1,0:T(8,128)(2,1)S(1)}, bf16[2,4,32,128]{3,2,1,0:T(8,128)(2,1)S(1)}, u32[]{:S(2)}, u32[]{:S(2)}) collective-permute-start(bf16[2,4,32,128]{3,2,1,0:T(8,128)(2,1)S(1)} %bitcast_bitcast_fusion), channel_id=1, source_target_pairs={{256,260},{258,262},{260,256},{262,258},{320,324},{322,326},{324,3... | collective-permute-start | bytes 196616 | tf_op jit(solution)/shard_map/ppermute | solution.py:70
  24.2 1.9 %collective-permute-start.1 = (bf16[2,4,32,128]{3,2,1,0:T(8,128)(2,1)S(1)}, bf16[2,4,32,128]{3,2,1,0:T(8,128)(2,1)S(1)}, u32[]{:S(2)}, u32[]{:S(2)}) collective-permute-start(bf16[2,4,32,128]{3,2,1,0:T(8,128)(2,1)S(1)} %bitcast_bitcast_fusion), channel_id=1, source_target_pairs={{0,2},{2,0},{4,6},{6,4},{64,66},{66,64},{68,70},{70,68},{128,130},... | collective-permute-start | bytes 196616 | tf_op jit(solution)/shard_map/ppermute | solution.py:70
  26.1 0.0 collective-permute-done.3
  26.1 0.0 collective-permute-done.2
  26.1 3.3 %collective-permute-done.1 = bf16[2,4,32,128]{3,2,1,0:T(8,128)(2,1)S(1)} collective-permute-done((bf16[2,4,32,128]{3,2,1,0:T(8,128)(2,1)S(1)}, bf16[2,4,32,128]{3,2,1,0:T(8,128)(2,1)S(1)}, u32[]{:S(2)}, u32[]{:S(2)}) %collective-permute-start.1) | collective-permute-done | bytes 65568 | tf_op jit(solution)/shard_map/ppermute | solution.py:70
  29.5 0.0 all-to-all-done
  29.5 0.8 %broadcast_in_dim.15 = bf16[4,12,32,128]{3,2,1,0:T(8,128)(2,1)} broadcast(bf16[12,32,128]{2,1,0:T(8,128)(2,1)S(1)} %all-to-all-done), dimensions={1,2,3} | broadcast | bytes 491520 | tf_op jit(solution)/shard_map/broadcast_in_dim | solution.py:86
  30.3 4.0 %all-to-all-start.1 = ((bf16[4,12,32,128]{3,2,1,0:T(8,128)(2,1)}), bf16[4,12,32,128]{3,2,1,0:T(8,128)(2,1)S(1)}, u32[]{:S(2)}, u32[]{:S(2)}) async-start(bf16[4,12,32,128]{3,2,1,0:T(8,128)(2,1)} %broadcast_in_dim.15), calls=%async_computation.1 | async-start | bytes 786432 | tf_op jit(solution)/shard_map/all_to_all | solution.py:86
  34.4 4.4 %collective-permute-start.4 = (bf16[4,2,4,4,128]{4,3,2,1,0:T(4,128)(2,1)S(1)}, bf16[4,2,4,4,128]{4,3,2,1,0:T(4,128)(2,1)S(1)}, u32[]{:S(2)}, u32[]{:S(2)}) collective-permute-start(bf16[4,2,4,4,128]{4,3,2,1,0:T(4,128)(2,1)S(1)} %pad_maximum_fusion), channel_id=1, source_target_pairs={{0,7},{1,6},{2,5},{3,4},{4,3},{5,2},{6,1},{7,0},{8,15},{9,14},{10,... | collective-permute-start | bytes 98312 | tf_op jit(solution)/shard_map/ppermute | solution.py:90
  38.9 0.0 copy-start.2
  38.9 1.4 %collective-permute-done.4 = bf16[4,2,4,4,128]{4,3,2,1,0:T(4,128)(2,1)S(1)} collective-permute-done((bf16[4,2,4,4,128]{4,3,2,1,0:T(4,128)(2,1)S(1)}, bf16[4,2,4,4,128]{4,3,2,1,0:T(4,128)(2,1)S(1)}, u32[]{:S(2)}, u32[]{:S(2)}) %collective-permute-start.4) | collective-permute-done | bytes 32800 | tf_op jit(solution)/shard_map/ppermute | solution.py:90
  40.3 0.2 all-to-all-done.1
  40.5 7.3 %collective-permute-start.5 = (bf16[48,32,128]{2,1,0:T(8,128)(2,1)S(1)}, bf16[48,32,128]{2,1,0:T(8,128)(2,1)S(1)}, u32[]{:S(2)}, u32[]{:S(2)}) collective-permute-start(bf16[48,32,128]{2,1,0:T(8,128)(2,1)S(1)} %bitcast.38), channel_id=1, source_target_pairs={{0,8},{8,0},{1,9},{9,1},{2,10},{10,2},{3,11},{11,3},{4,12},{12,4},... | collective-permute-start | bytes 1179656 | tf_op jit(solution)/shard_map/ppermute | solution.py:98
  47.8 0.1 pad_add_fusion.1.place
  47.9 0.1 copy.13
  48.0 0.0 copy-start.4
  48.0 0.1 copy.14
  48.1 0.7 %constant_dynamic-slice_fusion.weights = f32[2,9]{1,0:T(2,128)S(1)} fusion(f32[8,9]{1,0:T(8,128)} %param.9, s32[]{:T(128)S(6)} %select_n.23), kind=kLoop, calls=%fused_computation.10 | loop fusion | bytes 148 | tf_op jit(solution)/shard_map/dynamic_slice | solution.py:97
  48.8 0.0 copy-done.4
  48.8 0.1 pad_add_fusion
  48.8 0.3 collective-permute-done.5.other
  49.1 0.0 copy-done.1
  49.1 3.4 %shard_map.64 = f32[2,128,1024]{2,1,0:T(8,128)} custom-call(s32[3]{0:T(128)S(1)} %pad_add_fusion.1.place, s32[2,56]{1,0:T(2,128)S(1)} %constant_dynamic-slice_fusion.1.numbers, f32[2,9]{1,0:T(2,128)S(1)} %constant_dynamic-slice_fusion.weights, bf16[2,128,128]{2,1,0:T(8,128)(2,1)S(1)} %bitcast.42, bf16[2,128,128]{2,1,0:T(8,128)(2,1)S(1)} %bitcast.44, ...), custom_call_target="tpu_custom_call" | custom-call | tf_op jit(solution)/shard_map/pallas_call | solution.py:101
  (14 shorter events, 0.2 us)
Async XLA Ops:
  0.0 0.8 %copy-start = (bf16[4,32,256]{2,1,0:T(8,128)(2,1)S(1)}, bf16[4,32,256]{2,1,0:T(8,128)(2,1)}, u32[]{:S(2)}) copy-start(bf16[4,32,256]{2,1,0:T(8,128)(2,1)} %param.6) | copy-start | bytes 196612
  0.0 5.9 %copy-start.3 = (bf16[2,2048]{1,0:T(2,128)(2,1)S(1)}, bf16[2,2048]{1,0:T(2,128)(2,1)}, u32[]{:S(2)}) copy-start(bf16[2,2048]{1,0:T(2,128)(2,1)} %param.8) | copy-start | bytes 24580
  0.9 6.7 %collective-permute-start = (bf16[2,4,32,128]{3,2,1,0:T(8,128)(2,1)S(1)}, bf16[2,4,32,128]{3,2,1,0:T(8,128)(2,1)S(1)}, u32[]{:S(2)}, u32[]{:S(2)}) collective-permute-start(bf16[2,4,32,128]{3,2,1,0:T(8,128)(2,1)S(1)} %bitcast_bitcast_fusion.1), channel_id=1, source_target_pairs={{0,4},{2,6},{4,0},{6,2},{64,68},{66,70},{68,64},{70,66},{128,132},... | collective-permute-start | bytes 196616 | tf_op jit(solution)/shard_map/ppermute | solution.py:70
  8.2 40.9 %copy-start.1 = (f32[2,4,32,1024]{3,2,1,0:T(8,128)S(1)}, f32[2,4,32,1024]{3,2,1,0:T(8,128)}, u32[]{:S(2)}) copy-start(f32[2,4,32,1024]{3,2,1,0:T(8,128)} %param.7) | copy-start | bytes 3145732
  8.2 21.3 %all-to-all-start = ((bf16[12,32,128]{2,1,0:T(8,128)(2,1)}), bf16[12,32,128]{2,1,0:T(8,128)(2,1)S(1)}, u32[]{:S(2)}, u32[]{:S(2)}) async-start(bf16[12,32,128]{2,1,0:T(8,128)(2,1)} %broadcast_in_dim.14), calls=%async_computation | async-start | bytes 196608 | tf_op jit(solution)/shard_map/all_to_all | solution.py:82
  18.3 7.9 %collective-permute-start.3 = (bf16[2,4,32,128]{3,2,1,0:T(8,128)(2,1)S(1)}, bf16[2,4,32,128]{3,2,1,0:T(8,128)(2,1)S(1)}, u32[]{:S(2)}, u32[]{:S(2)}) collective-permute-start(bf16[2,4,32,128]{3,2,1,0:T(8,128)(2,1)S(1)} %bitcast_bitcast_fusion), channel_id=1, source_target_pairs={{0,6},{2,4},{4,2},{6,0},{64,70},{66,68},{68,66},{70,64},{128,134},... | collective-permute-start | bytes 196616 | tf_op jit(solution)/shard_map/ppermute | solution.py:70
  23.5 2.6 %collective-permute-start.2 = (bf16[2,4,32,128]{3,2,1,0:T(8,128)(2,1)S(1)}, bf16[2,4,32,128]{3,2,1,0:T(8,128)(2,1)S(1)}, u32[]{:S(2)}, u32[]{:S(2)}) collective-permute-start(bf16[2,4,32,128]{3,2,1,0:T(8,128)(2,1)S(1)} %bitcast_bitcast_fusion), channel_id=1, source_target_pairs={{256,260},{258,262},{260,256},{262,258},{320,324},{322,326},{324,3... | collective-permute-start | bytes 196616 | tf_op jit(solution)/shard_map/ppermute | solution.py:70
  24.2 5.3 %collective-permute-start.1 = (bf16[2,4,32,128]{3,2,1,0:T(8,128)(2,1)S(1)}, bf16[2,4,32,128]{3,2,1,0:T(8,128)(2,1)S(1)}, u32[]{:S(2)}, u32[]{:S(2)}) collective-permute-start(bf16[2,4,32,128]{3,2,1,0:T(8,128)(2,1)S(1)} %bitcast_bitcast_fusion), channel_id=1, source_target_pairs={{0,2},{2,0},{4,6},{6,4},{64,66},{66,64},{68,70},{70,68},{128,130},... | collective-permute-start | bytes 196616 | tf_op jit(solution)/shard_map/ppermute | solution.py:70
  30.3 10.2 %all-to-all-start.1 = ((bf16[4,12,32,128]{3,2,1,0:T(8,128)(2,1)}), bf16[4,12,32,128]{3,2,1,0:T(8,128)(2,1)S(1)}, u32[]{:S(2)}, u32[]{:S(2)}) async-start(bf16[4,12,32,128]{3,2,1,0:T(8,128)(2,1)} %broadcast_in_dim.15), calls=%async_computation.1 | async-start | bytes 786432 | tf_op jit(solution)/shard_map/all_to_all | solution.py:86
  34.4 5.9 %collective-permute-start.4 = (bf16[4,2,4,4,128]{4,3,2,1,0:T(4,128)(2,1)S(1)}, bf16[4,2,4,4,128]{4,3,2,1,0:T(4,128)(2,1)S(1)}, u32[]{:S(2)}, u32[]{:S(2)}) collective-permute-start(bf16[4,2,4,4,128]{4,3,2,1,0:T(4,128)(2,1)S(1)} %pad_maximum_fusion), channel_id=1, source_target_pairs={{0,7},{1,6},{2,5},{3,4},{4,3},{5,2},{6,1},{7,0},{8,15},{9,14},{10,... | collective-permute-start | bytes 98312 | tf_op jit(solution)/shard_map/ppermute | solution.py:90
  38.9 9.0 %copy-start.2 = (s32[8,16,3]{1,0,2:T(8,128)S(1)}, s32[8,16,3]{1,0,2:T(8,128)}, u32[]{:S(2)}) copy-start(s32[8,16,3]{1,0,2:T(8,128)} %param.11) | copy-start | bytes 4612
  40.5 8.6 %collective-permute-start.5 = (bf16[48,32,128]{2,1,0:T(8,128)(2,1)S(1)}, bf16[48,32,128]{2,1,0:T(8,128)(2,1)S(1)}, u32[]{:S(2)}, u32[]{:S(2)}) collective-permute-start(bf16[48,32,128]{2,1,0:T(8,128)(2,1)S(1)} %bitcast.38), channel_id=1, source_target_pairs={{0,8},{8,0},{1,9},{9,1},{2,10},{10,2},{3,11},{11,3},{4,12},{12,4},... | collective-permute-start | bytes 1179656 | tf_op jit(solution)/shard_map/ppermute | solution.py:98
  48.0 0.8 %copy-start.4 = (s32[8,8]{1,0:T(8,128)S(1)}, s32[8,8]{1,0:T(8,128)}, u32[]{:S(2)}) copy-start(s32[8,8]{1,0:T(8,128)} %param.10) | copy-start | bytes 772

commit v5 on v4

--- a/solution.py
+++ b/solution.py
@@ -1,3 +1,6 @@
+import functools
+import itertools
+
 import jax
 import jax.numpy as jnp
 from jax import lax
@@ -10,7 +13,9 @@
 EDGE = PLANES * HALO
 BLOCKS = 8
 BAND = 3
-AHEAD = 4
+AHEAD = {2: 4, 3: 2}
+AXES = ("z", "x", "core", "view", "gy")
+SIZES = (12, 4, 2, 4, 2)
 
 
 def fused(place, numbers, weights, own, one, two, three, edge, mine, other, observed, ratio, dense, flat, seen):
@@ -66,8 +71,17 @@
         ratio[w] = observed[w] / blurred
 
 
-def swap(array, k, planes):
-    return lax.ppermute(array, ("z", "view"), [(4 * z + v, 4 * z + (v ^ k)) for z in planes for v in range(4)])
+def early(k, z, x, core, gy):
+    return (z < AHEAD.get(k, 0)) & ((z + x + core + gy) > 0)
+
+
+def swap(array, k, chosen):
+    pairs = []
+    for z, x, core, v, gy in itertools.product(*map(range, SIZES)):
+        if chosen(z, x, core, gy):
+            place = ((z * SIZES[1] + x) * SIZES[2] + core) * SIZES[3]
+            pairs.append(((place + v) * SIZES[4] + gy, (place + (v ^ k)) * SIZES[4] + gy))
+    return lax.ppermute(array, AXES, pairs)
 
 
 def shards(estimate, observed, psf_blocks, kernel_y, block_source, psf_columns):
@@ -76,13 +90,15 @@
     shard = psf_blocks.reshape(2, 32, 64).transpose(1, 0, 2).reshape(1, 32, 128)
     slab = estimate.reshape(PLANES, ROWS, 2, 128).transpose(2, 0, 1, 3)
     spread = jnp.broadcast_to(shard, (12, 32, 128))
-    ahead = swap(slab, 2, range(AHEAD))
-    ahead, spread, estimate = lax.optimization_barrier((ahead, spread, estimate))
+    ahead = [swap(slab, k, functools.partial(early, k)) for k in (2, 3)]
+    *ahead, spread, estimate = lax.optimization_barrier((*ahead, spread, estimate))
     slab = estimate.reshape(PLANES, ROWS, 2, 128).transpose(2, 0, 1, 3)
     along = lax.all_to_all(spread, "z", 0, 0, tiled=True)
-    parts = [swap(slab, 1, range(12)), swap(slab, 2, range(AHEAD, 12)), swap(slab, 3, range(12))]
+    parts = [swap(slab, k, lambda *at, k=k: not early(k, *at)) for k in (1, 2, 3)]
     along, slab, *parts = lax.optimization_barrier((along, slab, *parts))
-    parts[1] = jnp.where(lax.axis_index("z") < AHEAD, ahead, parts[1])
+    for k in (2, 3):
+        here = early(k, *(lax.axis_index(name) for name in ("z", "x", "core", "gy")))
+        parts[k - 1] = jnp.where(here, ahead[k - 2], parts[k - 1])
     mine = lax.all_to_all(jnp.broadcast_to(along[None], (4, 12, 32, 128)), "x", 0, 0, tiled=True)
     begin = jnp.where(side == 0, ROWS - HALO, 0)
     edge = jnp.stack([lax.dynamic_slice_in_dim(part, begin, HALO, 2) for part in (slab, *parts)])
@@ -123,7 +139,7 @@
 
 
 def solution(mesh):
-    fine = Mesh(mesh.devices.reshape(12, 4, 2, 4, 2), ("z", "x", "core", "view", "gy"))
+    fine = Mesh(mesh.devices.reshape(SIZES), AXES)
     gz = ("z", "x", "core")
     in_specs = (P(gz, "gy", "view"), P("view", gz, "gy", None), P("view", gz), P(), P(), P())
     out_specs = P("view", gz, "gy", None)

time: 53 us -> 53.9 us (1.017)
  the two profiles are of different devices: /device:TPU:1 before, /device:TPU:19 now
where the time goes in v5:
time: 53.9 us; the launch traced here: 53.4 us
  starting transfers between devices  37 us (69%)
  waiting for transfers between devices  9.09 us (17%)
  local copies, waits for them, and re-layouts  3.46 us (6%)
  Pallas kernels  3.37 us (6%)
    ppermute x5, starting transfers between devices, swap(): return lax.ppermute(array, AXES, pairs)  11.9 us
    ppermute x1, starting transfers between devices, shards(): other = lax.ppermute(mine, 'core', [(0, 1), (1, 0)])  7.78 us
    all_to_all x1, starting transfers between devices, shards(): along = lax.all_to_all(spread, 'z', 0, 0, tiled=True)  7.58 us
    ppermute x1, starting transfers between devices, shards(): edge = lax.ppermute(edge, ('view', 'gy'), mirror).reshape(4, 2, EDGE, 128)  5.54 us
    all_to_all x1, starting transfers between devices, shards(): lax.all_to_all(jnp.broadcast_to(along[None], (4, 12, 32, 128)), 'x', 0, 0...  4.26 us
    ppermute x5, waiting for transfers between devices, swap(): return lax.ppermute(array, AXES, pairs)  3.49 us
    pallas_call x1, Pallas kernels, shards(): pl.pallas_call(fused, out_shape=jax.ShapeDtypeStruct((2, OWN, 1024), jnp....  3.37 us
    all_to_all x1, waiting for transfers between devices, shards(): along = lax.all_to_all(spread, 'z', 0, 0, tiled=True)  3.2 us
  transfers between devices with their start and end apart: 9, of which 5 were waited for; matrix products, arithmetic and copies ran while one was open for 2% of the time, Pallas kernels for 0%

profile of v5, /device:TPU:19, one launch (start us, length us, event | category | flops | bytes accessed | tf_op | source)
XLA Modules:
  0.0 53.4 jit_solution(11808513570616131558)
XLA Ops:
  0.0 0.8 %copy-done = bf16[4,32,256]{2,1,0:T(8,128)(2,1)S(1)} copy-done((bf16[4,32,256]{2,1,0:T(8,128)(2,1)S(1)}, bf16[4,32,256]{2,1,0:T(8,128)(2,1)}, u32[]{:S(2)}) %copy-start) | copy-done | bytes 65560
  0.9 2.1 %collective-permute-start.1 = (bf16[2,4,32,128]{3,2,1,0:T(8,128)(2,1)S(1)}, bf16[2,4,32,128]{3,2,1,0:T(8,128)(2,1)S(1)}, u32[]{:S(2)}, u32[]{:S(2)}) collective-permute-start(bf16[2,4,32,128]{3,2,1,0:T(8,128)(2,1)S(1)} %bitcast_bitcast_fusion.1), channel_id=1, source_target_pairs={{1,7},{3,5},{5,3},{7,1},{8,14},{9,15},{10,12},{11,13},{12,10},{13,... | collective-permute-start | bytes 196616 | tf_op jit(solution)/shard_map/ppermute | solution.py:84
  2.9 5.1 %collective-permute-start = (bf16[2,4,32,128]{3,2,1,0:T(8,128)(2,1)S(1)}, bf16[2,4,32,128]{3,2,1,0:T(8,128)(2,1)S(1)}, u32[]{:S(2)}, u32[]{:S(2)}) collective-permute-start(bf16[2,4,32,128]{3,2,1,0:T(8,128)(2,1)S(1)} %bitcast_bitcast_fusion.1), channel_id=1, source_target_pairs={{1,5},{3,7},{5,1},{7,3},{8,12},{9,13},{10,14},{11,15},{12,8},{13,9... | collective-permute-start | bytes 196616 | tf_op jit(solution)/shard_map/ppermute | solution.py:84
  8.1 0.1 reshape.40
  8.2 0.1 broadcast_in_dim.6
  8.3 0.0 collective-permute-done.1
  8.3 1.4 %collective-permute-done = bf16[2,4,32,128]{3,2,1,0:T(8,128)(2,1)S(1)} collective-permute-done((bf16[2,4,32,128]{3,2,1,0:T(8,128)(2,1)S(1)}, bf16[2,4,32,128]{3,2,1,0:T(8,128)(2,1)S(1)}, u32[]{:S(2)}, u32[]{:S(2)}) %collective-permute-start) | collective-permute-done | bytes 65568 | tf_op jit(solution)/shard_map/ppermute | solution.py:84
  9.7 0.7 %broadcast_in_dim.14 = bf16[12,32,128]{2,1,0:T(8,128)(2,1)} broadcast(bf16[32,128]{1,0:T(8,128)(2,1)S(1)} %broadcast_in_dim.6), dimensions={1,2} | broadcast | bytes 106496 | tf_op jit(solution)/shard_map/broadcast_in_dim | solution.py:92
  10.4 7.6 %all-to-all-start = ((bf16[12,32,128]{2,1,0:T(8,128)(2,1)}), bf16[12,32,128]{2,1,0:T(8,128)(2,1)S(1)}, u32[]{:S(2)}, u32[]{:S(2)}) async-start(bf16[12,32,128]{2,1,0:T(8,128)(2,1)} %broadcast_in_dim.14), calls=%async_computation | async-start | bytes 196608 | tf_op jit(solution)/shard_map/all_to_all | solution.py:96
  18.0 0.0 copy-start.1
  18.0 0.8 %collective-permute-start.4 = (bf16[2,4,32,128]{3,2,1,0:T(8,128)(2,1)S(1)}, bf16[2,4,32,128]{3,2,1,0:T(8,128)(2,1)S(1)}, u32[]{:S(2)}, u32[]{:S(2)}) collective-permute-start(bf16[2,4,32,128]{3,2,1,0:T(8,128)(2,1)S(1)} %bitcast_bitcast_fusion), channel_id=1, source_target_pairs={{0,6},{2,4},{4,2},{6,0},{128,134},{129,135},{130,132},{131,133},{1... | collective-permute-start | bytes 196616 | tf_op jit(solution)/shard_map/ppermute | solution.py:84
  18.8 0.7 %collective-permute-start.3 = (bf16[2,4,32,128]{3,2,1,0:T(8,128)(2,1)S(1)}, bf16[2,4,32,128]{3,2,1,0:T(8,128)(2,1)S(1)}, u32[]{:S(2)}, u32[]{:S(2)}) collective-permute-start(bf16[2,4,32,128]{3,2,1,0:T(8,128)(2,1)S(1)} %bitcast_bitcast_fusion), channel_id=1, source_target_pairs={{0,4},{2,6},{4,0},{6,2},{256,260},{257,261},{258,262},{259,263},{2... | collective-permute-start | bytes 196616 | tf_op jit(solution)/shard_map/ppermute | solution.py:84
  19.5 3.2 %collective-permute-start.2 = (bf16[2,4,32,128]{3,2,1,0:T(8,128)(2,1)S(1)}, bf16[2,4,32,128]{3,2,1,0:T(8,128)(2,1)S(1)}, u32[]{:S(2)}, u32[]{:S(2)}) collective-permute-start(bf16[2,4,32,128]{3,2,1,0:T(8,128)(2,1)S(1)} %bitcast_bitcast_fusion), channel_id=1, source_target_pairs={{0,2},{1,3},{2,0},{3,1},{4,6},{5,7},{6,4},{7,5},{8,10},{9,11},{10,... | collective-permute-start | bytes 196616 | tf_op jit(solution)/shard_map/ppermute | solution.py:84
  22.7 0.0 collective-permute-done.4
  22.7 0.0 collective-permute-done.3
  22.7 2.0 %collective-permute-done.2 = bf16[2,4,32,128]{3,2,1,0:T(8,128)(2,1)S(1)} collective-permute-done((bf16[2,4,32,128]{3,2,1,0:T(8,128)(2,1)S(1)}, bf16[2,4,32,128]{3,2,1,0:T(8,128)(2,1)S(1)}, u32[]{:S(2)}, u32[]{:S(2)}) %collective-permute-start.2) | collective-permute-done | bytes 65568 | tf_op jit(solution)/shard_map/ppermute | solution.py:84
  24.8 3.2 %all-to-all-done = bf16[12,32,128]{2,1,0:T(8,128)(2,1)S(1)} async-done(((bf16[12,32,128]{2,1,0:T(8,128)(2,1)}), bf16[12,32,128]{2,1,0:T(8,128)(2,1)S(1)}, u32[]{:S(2)}, u32[]{:S(2)}) %all-to-all-start) | async-done | bytes 98336 | tf_op jit(solution)/shard_map/all_to_all | solution.py:96
  28.0 0.8 %broadcast_in_dim.15 = bf16[4,12,32,128]{3,2,1,0:T(8,128)(2,1)} broadcast(bf16[12,32,128]{2,1,0:T(8,128)(2,1)S(1)} %all-to-all-done), dimensions={1,2,3} | broadcast | bytes 491520 | tf_op jit(solution)/shard_map/broadcast_in_dim | solution.py:102
  28.8 4.3 %all-to-all-start.1 = ((bf16[4,12,32,128]{3,2,1,0:T(8,128)(2,1)}), bf16[4,12,32,128]{3,2,1,0:T(8,128)(2,1)S(1)}, u32[]{:S(2)}, u32[]{:S(2)}) async-start(bf16[4,12,32,128]{3,2,1,0:T(8,128)(2,1)} %broadcast_in_dim.15), calls=%async_computation.1 | async-start | bytes 786432 | tf_op jit(solution)/shard_map/all_to_all | solution.py:102
  33.2 0.0 copy-start.2
  33.2 5.5 %collective-permute-start.5 = (bf16[4,2,4,4,128]{4,3,2,1,0:T(4,128)(2,1)S(1)}, bf16[4,2,4,4,128]{4,3,2,1,0:T(4,128)(2,1)S(1)}, u32[]{:S(2)}, u32[]{:S(2)}) collective-permute-start(bf16[4,2,4,4,128]{4,3,2,1,0:T(4,128)(2,1)S(1)} %pad_maximum_fusion), channel_id=1, source_target_pairs={{0,7},{1,6},{2,5},{3,4},{4,3},{5,2},{6,1},{7,0},{8,15},{9,14},{10,... | collective-permute-start | bytes 98312 | tf_op jit(solution)/shard_map/ppermute | solution.py:106
  38.8 2.1 %collective-permute-done.5 = bf16[4,2,4,4,128]{4,3,2,1,0:T(4,128)(2,1)S(1)} collective-permute-done((bf16[4,2,4,4,128]{4,3,2,1,0:T(4,128)(2,1)S(1)}, bf16[4,2,4,4,128]{4,3,2,1,0:T(4,128)(2,1)S(1)}, u32[]{:S(2)}, u32[]{:S(2)}) %collective-permute-start.5) | collective-permute-done | bytes 32800 | tf_op jit(solution)/shard_map/ppermute | solution.py:106
  40.9 0.0 all-to-all-done.1
  40.9 7.8 %collective-permute-start.6 = (bf16[48,32,128]{2,1,0:T(8,128)(2,1)S(1)}, bf16[48,32,128]{2,1,0:T(8,128)(2,1)S(1)}, u32[]{:S(2)}, u32[]{:S(2)}) collective-permute-start(bf16[48,32,128]{2,1,0:T(8,128)(2,1)S(1)} %bitcast.38), channel_id=1, source_target_pairs={{0,8},{8,0},{1,9},{9,1},{2,10},{10,2},{3,11},{11,3},{4,12},{12,4},... | collective-permute-start | bytes 1179656 | tf_op jit(solution)/shard_map/ppermute | solution.py:114
  48.7 0.1 pad_add_fusion.1.place
  48.7 0.1 copy.13
  48.8 0.0 copy-start.4
  48.9 0.1 copy.14
  48.9 0.7 %constant_dynamic-slice_fusion.weights = f32[2,9]{1,0:T(2,128)S(1)} fusion(f32[8,9]{1,0:T(8,128)} %param.9, s32[]{:T(128)S(6)} %select_n.31), kind=kLoop, calls=%fused_computation.11 | loop fusion | bytes 148 | tf_op jit(solution)/shard_map/dynamic_slice | solution.py:113
  49.6 0.1 pad_add_fusion
  49.7 0.3 collective-permute-done.6.other
  50.0 3.4 %shard_map.64 = f32[2,128,1024]{2,1,0:T(8,128)} custom-call(s32[3]{0:T(128)S(1)} %pad_add_fusion.1.place, s32[2,56]{1,0:T(2,128)S(1)} %constant_dynamic-slice_fusion.1.numbers, f32[2,9]{1,0:T(2,128)S(1)} %constant_dynamic-slice_fusion.weights, bf16[2,128,128]{2,1,0:T(8,128)(2,1)S(1)} %bitcast.41, bf16[2,128,128]{2,1,0:T(8,128)(2,1)S(1)} %bitcast.44, ...), custom_call_target="tpu_custom_call" | custom-call | tf_op jit(solution)/shard_map/pallas_call | solution.py:117
  (16 shorter events, 0.2 us)
Async XLA Ops:
  0.0 0.8 %copy-start = (bf16[4,32,256]{2,1,0:T(8,128)(2,1)S(1)}, bf16[4,32,256]{2,1,0:T(8,128)(2,1)}, u32[]{:S(2)}) copy-start(bf16[4,32,256]{2,1,0:T(8,128)(2,1)} %param.6) | copy-start | bytes 196612
  0.0 8.1 %copy-start.3 = (bf16[2,2048]{1,0:T(2,128)(2,1)S(1)}, bf16[2,2048]{1,0:T(2,128)(2,1)}, u32[]{:S(2)}) copy-start(bf16[2,2048]{1,0:T(2,128)(2,1)} %param.8) | copy-start | bytes 24580
  0.9 7.4 %collective-permute-start.1 = (bf16[2,4,32,128]{3,2,1,0:T(8,128)(2,1)S(1)}, bf16[2,4,32,128]{3,2,1,0:T(8,128)(2,1)S(1)}, u32[]{:S(2)}, u32[]{:S(2)}) collective-permute-start(bf16[2,4,32,128]{3,2,1,0:T(8,128)(2,1)S(1)} %bitcast_bitcast_fusion.1), channel_id=1, source_target_pairs={{1,7},{3,5},{5,3},{7,1},{8,14},{9,15},{10,12},{11,13},{12,10},{13,... | collective-permute-start | bytes 196616 | tf_op jit(solution)/shard_map/ppermute | solution.py:84
  2.9 6.8 %collective-permute-start = (bf16[2,4,32,128]{3,2,1,0:T(8,128)(2,1)S(1)}, bf16[2,4,32,128]{3,2,1,0:T(8,128)(2,1)S(1)}, u32[]{:S(2)}, u32[]{:S(2)}) collective-permute-start(bf16[2,4,32,128]{3,2,1,0:T(8,128)(2,1)S(1)} %bitcast_bitcast_fusion.1), channel_id=1, source_target_pairs={{1,5},{3,7},{5,1},{7,3},{8,12},{9,13},{10,14},{11,15},{12,8},{13,9... | collective-permute-start | bytes 196616 | tf_op jit(solution)/shard_map/ppermute | solution.py:84
  10.4 17.6 %all-to-all-start = ((bf16[12,32,128]{2,1,0:T(8,128)(2,1)}), bf16[12,32,128]{2,1,0:T(8,128)(2,1)S(1)}, u32[]{:S(2)}, u32[]{:S(2)}) async-start(bf16[12,32,128]{2,1,0:T(8,128)(2,1)} %broadcast_in_dim.14), calls=%async_computation | async-start | bytes 196608 | tf_op jit(solution)/shard_map/all_to_all | solution.py:96
  18.0 32.0 %copy-start.1 = (f32[2,4,32,1024]{3,2,1,0:T(8,128)S(1)}, f32[2,4,32,1024]{3,2,1,0:T(8,128)}, u32[]{:S(2)}) copy-start(f32[2,4,32,1024]{3,2,1,0:T(8,128)} %param.7) | copy-start | bytes 3145732
  18.0 4.7 %collective-permute-start.4 = (bf16[2,4,32,128]{3,2,1,0:T(8,128)(2,1)S(1)}, bf16[2,4,32,128]{3,2,1,0:T(8,128)(2,1)S(1)}, u32[]{:S(2)}, u32[]{:S(2)}) collective-permute-start(bf16[2,4,32,128]{3,2,1,0:T(8,128)(2,1)S(1)} %bitcast_bitcast_fusion), channel_id=1, source_target_pairs={{0,6},{2,4},{4,2},{6,0},{128,134},{129,135},{130,132},{131,133},{1... | collective-permute-start | bytes 196616 | tf_op jit(solution)/shard_map/ppermute | solution.py:84
  18.8 3.9 %collective-permute-start.3 = (bf16[2,4,32,128]{3,2,1,0:T(8,128)(2,1)S(1)}, bf16[2,4,32,128]{3,2,1,0:T(8,128)(2,1)S(1)}, u32[]{:S(2)}, u32[]{:S(2)}) collective-permute-start(bf16[2,4,32,128]{3,2,1,0:T(8,128)(2,1)S(1)} %bitcast_bitcast_fusion), channel_id=1, source_target_pairs={{0,4},{2,6},{4,0},{6,2},{256,260},{257,261},{258,262},{259,263},{2... | collective-permute-start | bytes 196616 | tf_op jit(solution)/shard_map/ppermute | solution.py:84
  19.5 5.3 %collective-permute-start.2 = (bf16[2,4,32,128]{3,2,1,0:T(8,128)(2,1)S(1)}, bf16[2,4,32,128]{3,2,1,0:T(8,128)(2,1)S(1)}, u32[]{:S(2)}, u32[]{:S(2)}) collective-permute-start(bf16[2,4,32,128]{3,2,1,0:T(8,128)(2,1)S(1)} %bitcast_bitcast_fusion), channel_id=1, source_target_pairs={{0,2},{1,3},{2,0},{3,1},{4,6},{5,7},{6,4},{7,5},{8,10},{9,11},{10,... | collective-permute-start | bytes 196616 | tf_op jit(solution)/shard_map/ppermute | solution.py:84
  28.8 12.1 %all-to-all-start.1 = ((bf16[4,12,32,128]{3,2,1,0:T(8,128)(2,1)}), bf16[4,12,32,128]{3,2,1,0:T(8,128)(2,1)S(1)}, u32[]{:S(2)}, u32[]{:S(2)}) async-start(bf16[4,12,32,128]{3,2,1,0:T(8,128)(2,1)} %broadcast_in_dim.15), calls=%async_computation.1 | async-start | bytes 786432 | tf_op jit(solution)/shard_map/all_to_all | solution.py:102
  33.2 15.5 %copy-start.2 = (s32[8,16,3]{1,0,2:T(8,128)S(1)}, s32[8,16,3]{1,0,2:T(8,128)}, u32[]{:S(2)}) copy-start(s32[8,16,3]{1,0,2:T(8,128)} %param.11) | copy-start | bytes 4612
  33.2 7.7 %collective-permute-start.5 = (bf16[4,2,4,4,128]{4,3,2,1,0:T(4,128)(2,1)S(1)}, bf16[4,2,4,4,128]{4,3,2,1,0:T(4,128)(2,1)S(1)}, u32[]{:S(2)}, u32[]{:S(2)}) collective-permute-start(bf16[4,2,4,4,128]{4,3,2,1,0:T(4,128)(2,1)S(1)} %pad_maximum_fusion), channel_id=1, source_target_pairs={{0,7},{1,6},{2,5},{3,4},{4,3},{5,2},{6,1},{7,0},{8,15},{9,14},{10,... | collective-permute-start | bytes 98312 | tf_op jit(solution)/shard_map/ppermute | solution.py:106
  40.9 9.1 %collective-permute-start.6 = (bf16[48,32,128]{2,1,0:T(8,128)(2,1)S(1)}, bf16[48,32,128]{2,1,0:T(8,128)(2,1)S(1)}, u32[]{:S(2)}, u32[]{:S(2)}) collective-permute-start(bf16[48,32,128]{2,1,0:T(8,128)(2,1)S(1)} %bitcast.38), channel_id=1, source_target_pairs={{0,8},{8,0},{1,9},{9,1},{2,10},{10,2},{3,11},{11,3},{4,12},{12,4},... | collective-permute-start | bytes 1179656 | tf_op jit(solution)/shard_map/ppermute | solution.py:114
  48.8 0.8 %copy-start.4 = (s32[8,8]{1,0:T(8,128)S(1)}, s32[8,8]{1,0:T(8,128)}, u32[]{:S(2)}) copy-start(s32[8,8]{1,0:T(8,128)} %param.10) | copy-start | bytes 772

commit v6 on v4

--- a/solution.py
+++ b/solution.py
@@ -1,3 +1,5 @@
+import itertools
+
 import jax
 import jax.numpy as jnp
 from jax import lax
@@ -10,14 +12,17 @@
 EDGE = PLANES * HALO
 BLOCKS = 8
 BAND = 3
-AHEAD = 4
+AHEAD = 5
+AXES = ("z", "x", "core", "view", "gy")
+SIZES = (12, 4, 2, 4, 2)
 
 
-def fused(place, numbers, weights, own, one, two, three, edge, mine, other, observed, ratio, dense, flat, seen):
+def fused(place, numbers, weights, near, far, edge, mine, other, observed, ratio, dense, flat, seen):
     view, side, core = place[0], place[1], place[2]
-    for k, part in enumerate((own, one, two, three)):
-        seen[view ^ k, :, :OWN] = part[...]
-        seen[view ^ 3 ^ k, :, OWN:] = edge[k]
+    parts = (near.at[0], near.at[1], far.at[0], far.at[1])
+    for n, k in enumerate((0, 2, 1, 3)):
+        seen[view ^ k, :, :OWN] = parts[n][:, :OWN]
+        seen[view ^ k ^ 3, :, OWN:] = jnp.where(place[3] == 1, parts[n][:, OWN:], edge[n])
     dense[...] = jnp.zeros_like(dense)
     for w in range(2):
         for i in range(2 * BLOCKS):
@@ -37,8 +42,7 @@
 
     def block(w, j):
         b = numbers[w, j % BLOCKS]
-        p, half = b // 2, b % 2
-        return seen[p, half]
+        return seen[b // 2, b % 2]
 
     for w in range(2):
         for j in range(BLOCKS):
@@ -66,28 +70,46 @@
         ratio[w] = observed[w] / blurred
 
 
-def swap(array, k, planes):
-    return lax.ppermute(array, ("z", "view"), [(4 * z + v, 4 * z + (v ^ k)) for z in planes for v in range(4)])
+def early(z, x, core):
+    return (z < AHEAD) & ((z + x + core) > 0)
+
+
+def permute(array, route, chosen=lambda *at: True):
+    pairs = []
+    for z, x, core, v, gy in itertools.product(*map(range, SIZES)):
+        if chosen(z, x, core):
+            to, across = route(v, gy)
+            base = ((z * SIZES[1] + x) * SIZES[2] + core) * SIZES[3]
+            pairs.append(((base + v) * SIZES[4] + gy, (base + to) * SIZES[4] + across))
+    return lax.ppermute(array, AXES, pairs)
+
+
+def mirror(v, gy):
+    return 3 - v, 1 - gy
 
 
 def shards(estimate, observed, psf_blocks, kernel_y, block_source, psf_columns):
     side = lax.axis_index("gy")
-    place = jnp.stack([lax.axis_index("view"), side, lax.axis_index("core")]).astype(jnp.int32)
+    place = [lax.axis_index("view"), side, lax.axis_index("core"), early(*map(lax.axis_index, AXES[:3]))]
+    place = jnp.stack([jnp.asarray(entry, jnp.int32) for entry in place])
     shard = psf_blocks.reshape(2, 32, 64).transpose(1, 0, 2).reshape(1, 32, 128)
-    slab = estimate.reshape(PLANES, ROWS, 2, 128).transpose(2, 0, 1, 3)
     spread = jnp.broadcast_to(shard, (12, 32, 128))
-    ahead = swap(slab, 2, range(AHEAD))
+    begin = jnp.where(side == 0, ROWS - HALO, 0)
+    ahead = permute(lax.dynamic_slice_in_dim(estimate, begin, HALO, 1), mirror, early)
     ahead, spread, estimate = lax.optimization_barrier((ahead, spread, estimate))
-    slab = estimate.reshape(PLANES, ROWS, 2, 128).transpose(2, 0, 1, 3)
     along = lax.all_to_all(spread, "z", 0, 0, tiled=True)
-    parts = [swap(slab, 1, range(12)), swap(slab, 2, range(AHEAD, 12)), swap(slab, 3, range(12))]
-    along, slab, *parts = lax.optimization_barrier((along, slab, *parts))
-    parts[1] = jnp.where(lax.axis_index("z") < AHEAD, ahead, parts[1])
+    slab = jnp.concatenate([estimate.reshape(OWN, 2, 128), ahead.reshape(EDGE, 2, 128)], axis=0)
+    slab = slab.transpose(1, 0, 2)
+    two = permute(slab, lambda v, gy: (v ^ 2, gy))
+    along, near = lax.optimization_barrier((along, jnp.stack([slab, two])))
     mine = lax.all_to_all(jnp.broadcast_to(along[None], (4, 12, 32, 128)), "x", 0, 0, tiled=True)
-    begin = jnp.where(side == 0, ROWS - HALO, 0)
-    edge = jnp.stack([lax.dynamic_slice_in_dim(part, begin, HALO, 2) for part in (slab, *parts)])
-    mirror = [(v * 2 + g, (3 - v) * 2 + (1 - g)) for v in range(4) for g in range(2)]
-    edge = lax.ppermute(edge, ("view", "gy"), mirror).reshape(4, 2, EDGE, 128)
+    far = permute(near, lambda v, gy: (v ^ 1, gy))
+    near, far = lax.optimization_barrier((near, far))
+    rows = [part.reshape(2, 2, 18, 8, 128) for part in (near, far)]
+    upper = jnp.concatenate([part[:, :, 0:16:4, :HALO] for part in rows])
+    lower = jnp.concatenate([part[:, :, 3:16:4, HALO:] for part in rows])
+    rows = jnp.where(side == 0, lower, upper)
+    edge = permute(rows, mirror, lambda *at: not early(*at)).reshape(4, 2, EDGE, 128)
     mine, edge, kernel_y, block_source, psf_columns = lax.optimization_barrier(
         (mine.reshape(48, 32, 128), edge, kernel_y, block_source, psf_columns)
     )
@@ -101,19 +123,20 @@
     ratio = pl.pallas_call(
         fused,
         out_shape=jax.ShapeDtypeStruct((2, OWN, 1024), jnp.float32),
-        in_specs=[smem] * 3 + [vmem] * 8,
+        in_specs=[smem] * 3 + [vmem] * 6,
         out_specs=vmem,
         scratch_shapes=[
             pltpu.VMEM((2, BLOCKS, 384, 128), jnp.bfloat16),
             pltpu.VMEM((2, OWN + EDGE, 1024), jnp.bfloat16),
             pltpu.VMEM((4, 2, OWN + EDGE, 128), jnp.bfloat16),
         ],
-        compiler_params=pltpu.CompilerParams(vmem_limit_bytes=32 * 1024 * 1024),
+        compiler_params=pltpu.CompilerParams(vmem_limit_bytes=16 * 1024 * 1024),
     )(
         place,
         numbers,
         weights,
-        *[part.reshape(2, OWN, 128) for part in (slab, *parts)],
+        near,
+        far,
         edge,
         mine,
         other,
@@ -123,7 +146,7 @@
 
 
 def solution(mesh):
-    fine = Mesh(mesh.devices.reshape(12, 4, 2, 4, 2), ("z", "x", "core", "view", "gy"))
+    fine = Mesh(mesh.devices.reshape(SIZES), AXES)
     gz = ("z", "x", "core")
     in_specs = (P(gz, "gy", "view"), P("view", gz, "gy", None), P("view", gz), P(), P(), P())
     out_specs = P("view", gz, "gy", None)

time: 53 us -> 56.2 us (1.060)
  waiting for transfers between devices: 6.72 us -> 11 us
  starting transfers between devices: 38.6 us -> 37.7 us
    all_to_all x1, waiting for transfers between devices: 0.23 us -> 5.43 us  [shards(): lax.all_to_all(jnp.broadcast_to(along[None], (4, 12, 32, 128)), 'x', 0, 0...]
    ppermute x5 -> x4, waiting for transfers between devices: 6.2 us -> 2.84 us  [permute(): return lax.ppermute(array, AXES, pairs)]
    all_to_all x1, waiting for transfers between devices: 0.01 us -> 2.36 us  [shards(): along = lax.all_to_all(spread, 'z', 0, 0, tiled=True)]
    dynamic_slice x0 -> x1, local copies, waits for them, and re-layouts: none -> 0.75 us  [shards(): lax.dynamic_slice_in_dim(estimate, begin, HALO, 1)]
    dynamic_slice x1, local copies, waits for them, and re-layouts: 0.7 us -> 0.01 us  [shards(): weights = lax.dynamic_slice_in_dim(kernel_y, first, 2, 0)]
    ppermute x5 -> x4, starting transfers between devices: 17.3 us -> 16.7 us  [permute(): return lax.ppermute(array, AXES, pairs)]
  transfers between devices with their start and end apart: 8 -> 7, of which waited for: 5 -> 5; matrix products, arithmetic and copies ran while one was open for 3% -> 3% of each run, Pallas kernels for 0% -> 0%
where the time goes in v6:
time: 56.2 us; the launch traced here: 55.8 us
  starting transfers between devices  37.7 us (67%)
  waiting for transfers between devices  11 us (20%)
  Pallas kernels  3.37 us (6%)
  local copies, waits for them, and re-layouts  3.3 us (6%)
    ppermute x4, starting transfers between devices, permute(): return lax.ppermute(array, AXES, pairs)  16.7 us
    all_to_all x1, starting transfers between devices, shards(): along = lax.all_to_all(spread, 'z', 0, 0, tiled=True)  10.2 us
    ppermute x1, starting transfers between devices, shards(): other = lax.ppermute(mine, 'core', [(0, 1), (1, 0)])  6.84 us
    all_to_all x1, waiting for transfers between devices, shards(): lax.all_to_all(jnp.broadcast_to(along[None], (4, 12, 32, 128)), 'x', 0, 0...  5.43 us
    all_to_all x1, starting transfers between devices, shards(): lax.all_to_all(jnp.broadcast_to(along[None], (4, 12, 32, 128)), 'x', 0, 0...  4.01 us
    pallas_call x1, Pallas kernels, shards(): pl.pallas_call(fused, out_shape=jax.ShapeDtypeStruct((2, OWN, 1024), jnp....  3.37 us
    ppermute x4, waiting for transfers between devices, permute(): return lax.ppermute(array, AXES, pairs)  2.84 us
    all_to_all x1, waiting for transfers between devices, shards(): along = lax.all_to_all(spread, 'z', 0, 0, tiled=True)  2.36 us
  transfers between devices with their start and end apart: 7, of which 5 were waited for; matrix products, arithmetic and copies ran while one was open for 3% of the time, Pallas kernels for 0%

profile of v6, /device:TPU:1, one launch (start us, length us, event | category | flops | bytes accessed | tf_op | source)
XLA Modules:
  0.0 55.8 jit_solution(11670708938794377744)
XLA Ops:
  0.0 0.0 copy-start
  0.0 0.8 %constant_dynamic-slice_fusion.2 = bf16[4,4,256]{2,1,0:T(4,128)(2,1)S(1)} fusion(bf16[4,32,256]{2,1,0:T(8,128)(2,1)} %param.6, s32[]{:T(128)S(6)} %select_n.17), kind=kLoop, calls=%fused_computation.8 | loop fusion | bytes 16388 | tf_op jit(solution)/shard_map/dynamic_slice | solution.py:98
  0.8 5.9 %collective-permute-start = (bf16[4,4,256]{2,1,0:T(4,128)(2,1)S(1)}, bf16[4,4,256]{2,1,0:T(4,128)(2,1)S(1)}, u32[]{:S(2)}, u32[]{:S(2)}) collective-permute-start(bf16[4,4,256]{2,1,0:T(4,128)(2,1)S(1)} %constant_dynamic-slice_fusion.2), channel_id=1, source_target_pairs={{8,15},{9,14},{10,13},{11,12},{12,11},{13,10},{14,9},{15,8},{16,23... | collective-permute-start | bytes 24584 | tf_op jit(solution)/shard_map/ppermute | solution.py:84
  6.7 0.0 copy-done.4
  6.7 0.1 reshape.33
  6.8 0.1 broadcast_in_dim.6
  6.9 0.8 %collective-permute-done = bf16[4,4,256]{2,1,0:T(4,128)(2,1)S(1)} collective-permute-done((bf16[4,4,256]{2,1,0:T(4,128)(2,1)S(1)}, bf16[4,4,256]{2,1,0:T(4,128)(2,1)S(1)}, u32[]{:S(2)}, u32[]{:S(2)}) %collective-permute-start) | collective-permute-done | bytes 8224 | tf_op jit(solution)/shard_map/ppermute | solution.py:84
  7.7 0.7 %broadcast_in_dim.14 = bf16[12,32,128]{2,1,0:T(8,128)(2,1)} broadcast(bf16[32,128]{1,0:T(8,128)(2,1)S(1)} %broadcast_in_dim.6), dimensions={1,2} | broadcast | bytes 106496 | tf_op jit(solution)/shard_map/broadcast_in_dim | solution.py:96
  8.4 10.2 %all-to-all-start = ((bf16[12,32,128]{2,1,0:T(8,128)(2,1)}), bf16[12,32,128]{2,1,0:T(8,128)(2,1)S(1)}, u32[]{:S(2)}, u32[]{:S(2)}) async-start(bf16[12,32,128]{2,1,0:T(8,128)(2,1)} %broadcast_in_dim.14), calls=%async_computation | async-start | bytes 196608 | tf_op jit(solution)/shard_map/all_to_all | solution.py:100
  18.6 0.0 copy-done.2
  18.6 0.0 copy-start.1
  18.6 5.6 %collective-permute-start.1 = (bf16[2,144,128]{2,1,0:T(8,128)(2,1)S(1)}, bf16[2,144,128]{2,1,0:T(8,128)(2,1)S(1)}, u32[]{:S(2)}, u32[]{:S(2)}) collective-permute-start(bf16[2,144,128]{2,1,0:T(8,128)(2,1)S(1)} %bitcast.25), channel_id=1, source_target_pairs={{0,4},{1,5},{2,6},{3,7},{4,0},{5,1},{6,2},{7,3},{8,12},{9,13},{10,... | collective-permute-start | bytes 221192 | tf_op jit(solution)/shard_map/ppermute | solution.py:84
  24.3 2.0 %collective-permute-done.1 = bf16[2,144,128]{2,1,0:T(8,128)(2,1)S(1)} collective-permute-done((bf16[2,144,128]{2,1,0:T(8,128)(2,1)S(1)}, bf16[2,144,128]{2,1,0:T(8,128)(2,1)S(1)}, u32[]{:S(2)}, u32[]{:S(2)}) %collective-permute-start.1) | collective-permute-done | bytes 73760 | tf_op jit(solution)/shard_map/ppermute | solution.py:84
  26.3 2.4 %all-to-all-done = bf16[12,32,128]{2,1,0:T(8,128)(2,1)S(1)} async-done(((bf16[12,32,128]{2,1,0:T(8,128)(2,1)}), bf16[12,32,128]{2,1,0:T(8,128)(2,1)S(1)}, u32[]{:S(2)}, u32[]{:S(2)}) %all-to-all-start) | async-done | bytes 98336 | tf_op jit(solution)/shard_map/all_to_all | solution.py:100
  28.7 4.5 %collective-permute-start.2 = (bf16[2,2,144,128]{3,2,1,0:T(8,128)(2,1)S(1)}, bf16[2,2,144,128]{3,2,1,0:T(8,128)(2,1)S(1)}, u32[]{:S(2)}, u32[]{:S(2)}) collective-permute-start(bf16[2,2,144,128]{3,2,1,0:T(8,128)(2,1)S(1)} %pad_maximum_fusion.near), channel_id=1, source_target_pairs={{0,2},{1,3},{2,0},{3,1},{4,6},{5,7},{6,4},{7,5},{8,10},{9,11},{10,... | collective-permute-start | bytes 442376 | tf_op jit(solution)/shard_map/ppermute | solution.py:84
  33.2 0.8 %broadcast_in_dim.15 = bf16[4,12,32,128]{3,2,1,0:T(8,128)(2,1)} broadcast(bf16[12,32,128]{2,1,0:T(8,128)(2,1)S(1)} %all-to-all-done), dimensions={1,2,3} | broadcast | bytes 491520 | tf_op jit(solution)/shard_map/broadcast_in_dim | solution.py:105
  34.0 4.0 %all-to-all-start.1 = ((bf16[4,12,32,128]{3,2,1,0:T(8,128)(2,1)}), bf16[4,12,32,128]{3,2,1,0:T(8,128)(2,1)S(1)}, u32[]{:S(2)}, u32[]{:S(2)}) async-start(bf16[4,12,32,128]{3,2,1,0:T(8,128)(2,1)} %broadcast_in_dim.15), calls=%async_computation.1 | async-start | bytes 786432 | tf_op jit(solution)/shard_map/all_to_all | solution.py:105
  38.0 0.0 collective-permute-done.2.far
  38.1 0.7 %collective-permute-start.3 = (bf16[4,2,4,4,128]{4,3,2,1,0:T(4,128)(2,1)S(1)}, bf16[4,2,4,4,128]{4,3,2,1,0:T(4,128)(2,1)S(1)}, u32[]{:S(2)}, u32[]{:S(2)}) collective-permute-start(bf16[4,2,4,4,128]{4,3,2,1,0:T(4,128)(2,1)S(1)} %maximum_select_fusion), channel_id=1, source_target_pairs={{0,7},{1,6},{2,5},{3,4},{4,3},{5,2},{6,1},{7,0},{320,327},{321,326... | collective-permute-start | bytes 98312 | tf_op jit(solution)/shard_map/ppermute | solution.py:84
  38.8 0.0 copy-start.3
  38.8 0.0 collective-permute-done.3
  38.8 5.4 %all-to-all-done.1 = bf16[4,12,32,128]{3,2,1,0:T(8,128)(2,1)S(1)} async-done(((bf16[4,12,32,128]{3,2,1,0:T(8,128)(2,1)}), bf16[4,12,32,128]{3,2,1,0:T(8,128)(2,1)S(1)}, u32[]{:S(2)}, u32[]{:S(2)}) %all-to-all-start.1) | async-done | bytes 393248 | tf_op jit(solution)/shard_map/all_to_all | solution.py:105
  44.2 6.8 %collective-permute-start.4 = (bf16[48,32,128]{2,1,0:T(8,128)(2,1)S(1)}, bf16[48,32,128]{2,1,0:T(8,128)(2,1)S(1)}, u32[]{:S(2)}, u32[]{:S(2)}) collective-permute-start(bf16[48,32,128]{2,1,0:T(8,128)(2,1)S(1)} %bitcast.19), channel_id=1, source_target_pairs={{0,8},{8,0},{1,9},{9,1},{2,10},{10,2},{3,11},{11,3},{4,12},{12,4},... | collective-permute-start | bytes 1179656 | tf_op jit(solution)/shard_map/ppermute | solution.py:120
  51.1 0.1 pad_add_fusion.1.place
  51.1 0.1 copy.11
  51.2 0.0 copy-start.5
  51.3 0.1 copy.12
  51.3 0.0 copy-done
  51.3 0.6 %copy-done.5 = s32[8,8]{1,0:T(8,128)S(1)} copy-done((s32[8,8]{1,0:T(8,128)S(1)}, s32[8,8]{1,0:T(8,128)}, u32[]{:S(2)}) %copy-start.5) | copy-done | bytes 280
  51.9 0.1 pad_add_fusion
  52.0 0.4 collective-permute-done.4.other
  52.4 3.4 %shard_map.64 = f32[2,128,1024]{2,1,0:T(8,128)} custom-call(s32[4]{0:T(128)S(1)} %pad_add_fusion.1.place, s32[2,56]{1,0:T(2,128)S(1)} %constant_dynamic-slice_fusion.1.numbers, f32[2,9]{1,0:T(2,128)S(1)} %constant_dynamic-slice_fusion.weights, bf16[2,2,144,128]{3,2,1,0:T(8,128)(2,1)S(1)} %pad_maximum_fusion.near, ...), custom_call_target="tpu_custom_call" | custom-call | tf_op jit(solution)/shard_map/pallas_call | solution.py:123
  (15 shorter events, 0.2 us)
Async XLA Ops:
  0.0 51.3 %copy-start = (f32[8,9]{1,0:T(8,128)S(1)}, f32[8,9]{1,0:T(8,128)}, u32[]{:S(2)}) copy-start(f32[8,9]{1,0:T(8,128)} %param.9) | copy-start | bytes 868
  0.0 6.7 %copy-start.4 = (bf16[2,2048]{1,0:T(2,128)(2,1)S(1)}, bf16[2,2048]{1,0:T(2,128)(2,1)}, u32[]{:S(2)}) copy-start(bf16[2,2048]{1,0:T(2,128)(2,1)} %param.8) | copy-start | bytes 24580
  0.8 6.9 %collective-permute-start = (bf16[4,4,256]{2,1,0:T(4,128)(2,1)S(1)}, bf16[4,4,256]{2,1,0:T(4,128)(2,1)S(1)}, u32[]{:S(2)}, u32[]{:S(2)}) collective-permute-start(bf16[4,4,256]{2,1,0:T(4,128)(2,1)S(1)} %constant_dynamic-slice_fusion.2), channel_id=1, source_target_pairs={{8,15},{9,14},{10,13},{11,12},{12,11},{13,10},{14,9},{15,8},{16,23... | collective-permute-start | bytes 24584 | tf_op jit(solution)/shard_map/ppermute | solution.py:84
  8.4 10.2 %copy-start.2 = (bf16[4,32,256]{2,1,0:T(8,128)(2,1)S(1)}, bf16[4,32,256]{2,1,0:T(8,128)(2,1)}, u32[]{:S(2)}) copy-start(bf16[4,32,256]{2,1,0:T(8,128)(2,1)} %param.6) | copy-start | bytes 196612
  8.4 20.3 %all-to-all-start = ((bf16[12,32,128]{2,1,0:T(8,128)(2,1)}), bf16[12,32,128]{2,1,0:T(8,128)(2,1)S(1)}, u32[]{:S(2)}, u32[]{:S(2)}) async-start(bf16[12,32,128]{2,1,0:T(8,128)(2,1)} %broadcast_in_dim.14), calls=%async_computation | async-start | bytes 196608 | tf_op jit(solution)/shard_map/all_to_all | solution.py:100
  18.6 33.8 %copy-start.1 = (f32[2,4,32,1024]{3,2,1,0:T(8,128)S(1)}, f32[2,4,32,1024]{3,2,1,0:T(8,128)}, u32[]{:S(2)}) copy-start(f32[2,4,32,1024]{3,2,1,0:T(8,128)} %param.7) | copy-start | bytes 3145732
  18.6 7.7 %collective-permute-start.1 = (bf16[2,144,128]{2,1,0:T(8,128)(2,1)S(1)}, bf16[2,144,128]{2,1,0:T(8,128)(2,1)S(1)}, u32[]{:S(2)}, u32[]{:S(2)}) collective-permute-start(bf16[2,144,128]{2,1,0:T(8,128)(2,1)S(1)} %bitcast.25), channel_id=1, source_target_pairs={{0,4},{1,5},{2,6},{3,7},{4,0},{5,1},{6,2},{7,3},{8,12},{9,13},{10,... | collective-permute-start | bytes 221192 | tf_op jit(solution)/shard_map/ppermute | solution.py:84
  28.7 9.3 %collective-permute-start.2 = (bf16[2,2,144,128]{3,2,1,0:T(8,128)(2,1)S(1)}, bf16[2,2,144,128]{3,2,1,0:T(8,128)(2,1)S(1)}, u32[]{:S(2)}, u32[]{:S(2)}) collective-permute-start(bf16[2,2,144,128]{3,2,1,0:T(8,128)(2,1)S(1)} %pad_maximum_fusion.near), channel_id=1, source_target_pairs={{0,2},{1,3},{2,0},{3,1},{4,6},{5,7},{6,4},{7,5},{8,10},{9,11},{10,... | collective-permute-start | bytes 442376 | tf_op jit(solution)/shard_map/ppermute | solution.py:84
  34.0 10.2 %all-to-all-start.1 = ((bf16[4,12,32,128]{3,2,1,0:T(8,128)(2,1)}), bf16[4,12,32,128]{3,2,1,0:T(8,128)(2,1)S(1)}, u32[]{:S(2)}, u32[]{:S(2)}) async-start(bf16[4,12,32,128]{3,2,1,0:T(8,128)(2,1)} %broadcast_in_dim.15), calls=%async_computation.1 | async-start | bytes 786432 | tf_op jit(solution)/shard_map/all_to_all | solution.py:105
  38.1 0.7 %collective-permute-start.3 = (bf16[4,2,4,4,128]{4,3,2,1,0:T(4,128)(2,1)S(1)}, bf16[4,2,4,4,128]{4,3,2,1,0:T(4,128)(2,1)S(1)}, u32[]{:S(2)}, u32[]{:S(2)}) collective-permute-start(bf16[4,2,4,4,128]{4,3,2,1,0:T(4,128)(2,1)S(1)} %maximum_select_fusion), channel_id=1, source_target_pairs={{0,7},{1,6},{2,5},{3,4},{4,3},{5,2},{6,1},{7,0},{320,327},{321,326... | collective-permute-start | bytes 98312 | tf_op jit(solution)/shard_map/ppermute | solution.py:84
  38.8 12.4 %copy-start.3 = (s32[8,16,3]{1,0,2:T(8,128)S(1)}, s32[8,16,3]{1,0,2:T(8,128)}, u32[]{:S(2)}) copy-start(s32[8,16,3]{1,0,2:T(8,128)} %param.11) | copy-start | bytes 4612
  44.2 8.2 %collective-permute-start.4 = (bf16[48,32,128]{2,1,0:T(8,128)(2,1)S(1)}, bf16[48,32,128]{2,1,0:T(8,128)(2,1)S(1)}, u32[]{:S(2)}, u32[]{:S(2)}) collective-permute-start(bf16[48,32,128]{2,1,0:T(8,128)(2,1)S(1)} %bitcast.19), channel_id=1, source_target_pairs={{0,8},{8,0},{1,9},{9,1},{2,10},{10,2},{3,11},{11,3},{4,12},{12,4},... | collective-permute-start | bytes 1179656 | tf_op jit(solution)/shard_map/ppermute | solution.py:120
  51.2 0.7 %copy-start.5 = (s32[8,8]{1,0:T(8,128)S(1)}, s32[8,8]{1,0:T(8,128)}, u32[]{:S(2)}) copy-start(s32[8,8]{1,0:T(8,128)} %param.10) | copy-start | bytes 772

commit v7 on v6

--- a/solution.py
+++ b/solution.py
@@ -70,14 +70,14 @@
         ratio[w] = observed[w] / blurred
 
 
-def early(z, x, core):
-    return (z < AHEAD) & ((z + x + core) > 0)
+def early(z):
+    return z < AHEAD
 
 
-def permute(array, route, chosen=lambda *at: True):
+def permute(array, route, chosen=lambda z: True):
     pairs = []
     for z, x, core, v, gy in itertools.product(*map(range, SIZES)):
-        if chosen(z, x, core):
+        if chosen(z):
             to, across = route(v, gy)
             base = ((z * SIZES[1] + x) * SIZES[2] + core) * SIZES[3]
             pairs.append(((base + v) * SIZES[4] + gy, (base + to) * SIZES[4] + across))
@@ -90,7 +90,7 @@
 
 def shards(estimate, observed, psf_blocks, kernel_y, block_source, psf_columns):
     side = lax.axis_index("gy")
-    place = [lax.axis_index("view"), side, lax.axis_index("core"), early(*map(lax.axis_index, AXES[:3]))]
+    place = [lax.axis_index("view"), side, lax.axis_index("core"), early(lax.axis_index("z"))]
     place = jnp.stack([jnp.asarray(entry, jnp.int32) for entry in place])
     shard = psf_blocks.reshape(2, 32, 64).transpose(1, 0, 2).reshape(1, 32, 128)
     spread = jnp.broadcast_to(shard, (12, 32, 128))
@@ -104,15 +104,16 @@
     along, near = lax.optimization_barrier((along, jnp.stack([slab, two])))
     mine = lax.all_to_all(jnp.broadcast_to(along[None], (4, 12, 32, 128)), "x", 0, 0, tiled=True)
     far = permute(near, lambda v, gy: (v ^ 1, gy))
-    near, far = lax.optimization_barrier((near, far))
+    mine, near, far = lax.optimization_barrier((mine, near, far))
     rows = [part.reshape(2, 2, 18, 8, 128) for part in (near, far)]
     upper = jnp.concatenate([part[:, :, 0:16:4, :HALO] for part in rows])
     lower = jnp.concatenate([part[:, :, 3:16:4, HALO:] for part in rows])
     rows = jnp.where(side == 0, lower, upper)
-    edge = permute(rows, mirror, lambda *at: not early(*at)).reshape(4, 2, EDGE, 128)
-    mine, edge, kernel_y, block_source, psf_columns = lax.optimization_barrier(
-        (mine.reshape(48, 32, 128), edge, kernel_y, block_source, psf_columns)
-    )
+    edge = permute(rows, mirror, lambda z: not early(z)).reshape(4, 2, EDGE, 128)
+    mine = mine.reshape(48, 32, 128)
+    kernel_y, block_source, psf_columns = lax.optimization_barrier(
+        (kernel_y, block_source, psf_columns, mine)
+    )[:3]
     first = 2 * lax.axis_index("view")
     numbers = jnp.concatenate([block_source, psf_columns.reshape(8, 48)], axis=1)
     numbers = lax.dynamic_slice_in_dim(numbers, first, 2, 0)

time: 56.2 us -> 52.6 us (0.936)
  waiting for transfers between devices: 11 us -> 7.87 us
  local copies, waits for them, and re-layouts: 3.3 us -> 2.7 us
    all_to_all x1, waiting for transfers between devices: 5.43 us -> 0.01 us  [shards(): lax.all_to_all(jnp.broadcast_to(along[None], (4, 12, 32, 128)), 'x', 0, 0...]
    ppermute x4, waiting for transfers between devices: 2.84 us -> 4.96 us  [permute(): return lax.ppermute(array, AXES, pairs)]
    unnamed x13, local copies, waits for them, and re-layouts: 0.65 us -> 0.04 us
  transfers between devices with their start and end apart: 7 -> 7, of which waited for: 5 -> 5; matrix products, arithmetic and copies ran while one was open for 3% -> 1% of each run, Pallas kernels for 0% -> 0%
where the time goes in v7:
time: 52.6 us; the launch traced here: 52.1 us
  starting transfers between devices  37.8 us (72%)
  waiting for transfers between devices  7.87 us (15%)
  Pallas kernels  3.37 us (6%)
  local copies, waits for them, and re-layouts  2.7 us (5%)
    ppermute x4, starting transfers between devices, permute(): return lax.ppermute(array, AXES, pairs)  16.7 us
    all_to_all x1, starting transfers between devices, shards(): along = lax.all_to_all(spread, 'z', 0, 0, tiled=True)  10.2 us
    ppermute x1, starting transfers between devices, shards(): other = lax.ppermute(mine, 'core', [(0, 1), (1, 0)])  6.9 us
    ppermute x4, waiting for transfers between devices, permute(): return lax.ppermute(array, AXES, pairs)  4.96 us
    all_to_all x1, starting transfers between devices, shards(): lax.all_to_all(jnp.broadcast_to(along[None], (4, 12, 32, 128)), 'x', 0, 0...  4.01 us
    pallas_call x1, Pallas kernels, shards(): pl.pallas_call(fused, out_shape=jax.ShapeDtypeStruct((2, OWN, 1024), jnp....  3.37 us
    all_to_all x1, waiting for transfers between devices, shards(): along = lax.all_to_all(spread, 'z', 0, 0, tiled=True)  2.66 us
  transfers between devices with their start and end apart: 7, of which 5 were waited for; matrix products, arithmetic and copies ran while one was open for 1% of the time, Pallas kernels for 0%

profile of v7, /device:TPU:1, one launch (start us, length us, event | category | flops | bytes accessed | tf_op | source)
XLA Modules:
  0.0 52.1 jit_solution(5052993432851281697)
XLA Ops:
  0.0 0.0 copy-start
  0.0 0.8 %constant_dynamic-slice_fusion.2 = bf16[4,4,256]{2,1,0:T(4,128)(2,1)S(1)} fusion(bf16[4,32,256]{2,1,0:T(8,128)(2,1)} %param.6, s32[]{:T(128)S(6)} %select_n.17), kind=kLoop, calls=%fused_computation.8 | loop fusion | bytes 16388 | tf_op jit(solution)/shard_map/dynamic_slice | solution.py:98
  0.8 5.9 %collective-permute-start = (bf16[4,4,256]{2,1,0:T(4,128)(2,1)S(1)}, bf16[4,4,256]{2,1,0:T(4,128)(2,1)S(1)}, u32[]{:S(2)}, u32[]{:S(2)}) collective-permute-start(bf16[4,4,256]{2,1,0:T(4,128)(2,1)S(1)} %constant_dynamic-slice_fusion.2), channel_id=1, source_target_pairs={{0,7},{1,6},{2,5},{3,4},{4,3},{5,2},{6,1},{7,0},{8,15},{9,14},{10,... | collective-permute-start | bytes 24584 | tf_op jit(solution)/shard_map/ppermute | solution.py:84
  6.7 0.0 copy-done.4
  6.7 0.1 reshape.33
  6.8 0.1 broadcast_in_dim.6
  6.9 0.8 %collective-permute-done = bf16[4,4,256]{2,1,0:T(4,128)(2,1)S(1)} collective-permute-done((bf16[4,4,256]{2,1,0:T(4,128)(2,1)S(1)}, bf16[4,4,256]{2,1,0:T(4,128)(2,1)S(1)}, u32[]{:S(2)}, u32[]{:S(2)}) %collective-permute-start) | collective-permute-done | bytes 8224 | tf_op jit(solution)/shard_map/ppermute | solution.py:84
  7.7 0.7 %broadcast_in_dim.14 = bf16[12,32,128]{2,1,0:T(8,128)(2,1)} broadcast(bf16[32,128]{1,0:T(8,128)(2,1)S(1)} %broadcast_in_dim.6), dimensions={1,2} | broadcast | bytes 106496 | tf_op jit(solution)/shard_map/broadcast_in_dim | solution.py:96
  8.4 10.2 %all-to-all-start = ((bf16[12,32,128]{2,1,0:T(8,128)(2,1)}), bf16[12,32,128]{2,1,0:T(8,128)(2,1)S(1)}, u32[]{:S(2)}, u32[]{:S(2)}) async-start(bf16[12,32,128]{2,1,0:T(8,128)(2,1)} %broadcast_in_dim.14), calls=%async_computation | async-start | bytes 196608 | tf_op jit(solution)/shard_map/all_to_all | solution.py:100
  18.6 0.0 copy-done.2
  18.6 0.0 copy-start.1
  18.6 5.6 %collective-permute-start.1 = (bf16[2,144,128]{2,1,0:T(8,128)(2,1)S(1)}, bf16[2,144,128]{2,1,0:T(8,128)(2,1)S(1)}, u32[]{:S(2)}, u32[]{:S(2)}) collective-permute-start(bf16[2,144,128]{2,1,0:T(8,128)(2,1)S(1)} %bitcast.25), channel_id=1, source_target_pairs={{0,4},{1,5},{2,6},{3,7},{4,0},{5,1},{6,2},{7,3},{8,12},{9,13},{10,... | collective-permute-start | bytes 221192 | tf_op jit(solution)/shard_map/ppermute | solution.py:84
  24.3 1.7 %collective-permute-done.1 = bf16[2,144,128]{2,1,0:T(8,128)(2,1)S(1)} collective-permute-done((bf16[2,144,128]{2,1,0:T(8,128)(2,1)S(1)}, bf16[2,144,128]{2,1,0:T(8,128)(2,1)S(1)}, u32[]{:S(2)}, u32[]{:S(2)}) %collective-permute-start.1) | collective-permute-done | bytes 73760 | tf_op jit(solution)/shard_map/ppermute | solution.py:84
  26.0 2.7 %all-to-all-done = bf16[12,32,128]{2,1,0:T(8,128)(2,1)S(1)} async-done(((bf16[12,32,128]{2,1,0:T(8,128)(2,1)}), bf16[12,32,128]{2,1,0:T(8,128)(2,1)S(1)}, u32[]{:S(2)}, u32[]{:S(2)}) %all-to-all-start) | async-done | bytes 98336 | tf_op jit(solution)/shard_map/all_to_all | solution.py:100
  28.7 0.8 %broadcast_in_dim.15 = bf16[4,12,32,128]{3,2,1,0:T(8,128)(2,1)} broadcast(bf16[12,32,128]{2,1,0:T(8,128)(2,1)S(1)} %all-to-all-done), dimensions={1,2,3} | broadcast | bytes 491520 | tf_op jit(solution)/shard_map/broadcast_in_dim | solution.py:105
  29.5 4.0 %all-to-all-start.1 = ((bf16[4,12,32,128]{3,2,1,0:T(8,128)(2,1)}), bf16[4,12,32,128]{3,2,1,0:T(8,128)(2,1)S(1)}, u32[]{:S(2)}, u32[]{:S(2)}) async-start(bf16[4,12,32,128]{3,2,1,0:T(8,128)(2,1)} %broadcast_in_dim.15), calls=%async_computation.1 | async-start | bytes 786432 | tf_op jit(solution)/shard_map/all_to_all | solution.py:105
  33.5 4.5 %collective-permute-start.2 = (bf16[2,2,144,128]{3,2,1,0:T(8,128)(2,1)S(1)}, bf16[2,2,144,128]{3,2,1,0:T(8,128)(2,1)S(1)}, u32[]{:S(2)}, u32[]{:S(2)}) collective-permute-start(bf16[2,2,144,128]{3,2,1,0:T(8,128)(2,1)S(1)} %pad_maximum_fusion.near), channel_id=1, source_target_pairs={{0,2},{1,3},{2,0},{3,1},{4,6},{5,7},{6,4},{7,5},{8,10},{9,11},{10,... | collective-permute-start | bytes 442376 | tf_op jit(solution)/shard_map/ppermute | solution.py:84
  38.0 0.0 copy-start.3
  38.0 0.1 pad_add_fusion.1.place
  38.1 2.4 %collective-permute-done.2.far = bf16[2,2,144,128]{3,2,1,0:T(8,128)(2,1)S(1)} collective-permute-done((bf16[2,2,144,128]{3,2,1,0:T(8,128)(2,1)S(1)}, bf16[2,2,144,128]{3,2,1,0:T(8,128)(2,1)S(1)}, u32[]{:S(2)}, u32[]{:S(2)}) %collective-permute-start.2) | collective-permute-done | bytes 147488 | tf_op jit(solution)/shard_map/ppermute | solution.py:84
  40.5 0.0 all-to-all-done.1
  40.5 6.9 %collective-permute-start.4 = (bf16[48,32,128]{2,1,0:T(8,128)(2,1)S(1)}, bf16[48,32,128]{2,1,0:T(8,128)(2,1)S(1)}, u32[]{:S(2)}, u32[]{:S(2)}) collective-permute-start(bf16[48,32,128]{2,1,0:T(8,128)(2,1)S(1)} %bitcast.19), channel_id=1, source_target_pairs={{0,8},{8,0},{1,9},{9,1},{2,10},{10,2},{3,11},{11,3},{4,12},{12,4},... | collective-permute-start | bytes 1179656 | tf_op jit(solution)/shard_map/ppermute | solution.py:121
  47.4 0.1 copy.11
  47.5 0.1 copy.12
  47.6 0.0 copy-start.5
  47.7 0.7 %collective-permute-start.3 = (bf16[4,2,4,4,128]{4,3,2,1,0:T(4,128)(2,1)S(1)}, bf16[4,2,4,4,128]{4,3,2,1,0:T(4,128)(2,1)S(1)}, u32[]{:S(2)}, u32[]{:S(2)}) collective-permute-start(bf16[4,2,4,4,128]{4,3,2,1,0:T(4,128)(2,1)S(1)} %maximum_select_fusion), channel_id=1, source_target_pairs={{320,327},{321,326},{322,325},{323,324},{324,323},{325,322},{326,3... | collective-permute-start | bytes 98312 | tf_op jit(solution)/shard_map/ppermute | solution.py:84
  48.4 0.0 copy-done.5
  48.4 0.1 pad_add_fusion
  48.5 0.0 collective-permute-done.3
  48.5 0.2 collective-permute-done.4.other
  48.7 0.0 copy-done.1
  48.7 3.4 %shard_map.64 = f32[2,128,1024]{2,1,0:T(8,128)} custom-call(s32[4]{0:T(128)S(1)} %pad_add_fusion.1.place, s32[2,56]{1,0:T(2,128)S(1)} %constant_dynamic-slice_fusion.1.numbers, f32[2,9]{1,0:T(2,128)S(1)} %constant_dynamic-slice_fusion.weights, bf16[2,2,144,128]{3,2,1,0:T(8,128)(2,1)S(1)} %pad_maximum_fusion.near, ...), custom_call_target="tpu_custom_call" | custom-call | tf_op jit(solution)/shard_map/pallas_call | solution.py:124
  (15 shorter events, 0.2 us)
Async XLA Ops:
  0.0 48.4 %copy-start = (f32[8,9]{1,0:T(8,128)S(1)}, f32[8,9]{1,0:T(8,128)}, u32[]{:S(2)}) copy-start(f32[8,9]{1,0:T(8,128)} %param.9) | copy-start | bytes 868
  0.0 6.7 %copy-start.4 = (bf16[2,2048]{1,0:T(2,128)(2,1)S(1)}, bf16[2,2048]{1,0:T(2,128)(2,1)}, u32[]{:S(2)}) copy-start(bf16[2,2048]{1,0:T(2,128)(2,1)} %param.8) | copy-start | bytes 24580
  0.8 6.9 %collective-permute-start = (bf16[4,4,256]{2,1,0:T(4,128)(2,1)S(1)}, bf16[4,4,256]{2,1,0:T(4,128)(2,1)S(1)}, u32[]{:S(2)}, u32[]{:S(2)}) collective-permute-start(bf16[4,4,256]{2,1,0:T(4,128)(2,1)S(1)} %constant_dynamic-slice_fusion.2), channel_id=1, source_target_pairs={{0,7},{1,6},{2,5},{3,4},{4,3},{5,2},{6,1},{7,0},{8,15},{9,14},{10,... | collective-permute-start | bytes 24584 | tf_op jit(solution)/shard_map/ppermute | solution.py:84
  8.4 10.2 %copy-start.2 = (bf16[4,32,256]{2,1,0:T(8,128)(2,1)S(1)}, bf16[4,32,256]{2,1,0:T(8,128)(2,1)}, u32[]{:S(2)}) copy-start(bf16[4,32,256]{2,1,0:T(8,128)(2,1)} %param.6) | copy-start | bytes 196612
  8.4 20.3 %all-to-all-start = ((bf16[12,32,128]{2,1,0:T(8,128)(2,1)}), bf16[12,32,128]{2,1,0:T(8,128)(2,1)S(1)}, u32[]{:S(2)}, u32[]{:S(2)}) async-start(bf16[12,32,128]{2,1,0:T(8,128)(2,1)} %broadcast_in_dim.14), calls=%async_computation | async-start | bytes 196608 | tf_op jit(solution)/shard_map/all_to_all | solution.py:100
  18.6 30.1 %copy-start.1 = (f32[2,4,32,1024]{3,2,1,0:T(8,128)S(1)}, f32[2,4,32,1024]{3,2,1,0:T(8,128)}, u32[]{:S(2)}) copy-start(f32[2,4,32,1024]{3,2,1,0:T(8,128)} %param.7) | copy-start | bytes 3145732
  18.6 7.4 %collective-permute-start.1 = (bf16[2,144,128]{2,1,0:T(8,128)(2,1)S(1)}, bf16[2,144,128]{2,1,0:T(8,128)(2,1)S(1)}, u32[]{:S(2)}, u32[]{:S(2)}) collective-permute-start(bf16[2,144,128]{2,1,0:T(8,128)(2,1)S(1)} %bitcast.25), channel_id=1, source_target_pairs={{0,4},{1,5},{2,6},{3,7},{4,0},{5,1},{6,2},{7,3},{8,12},{9,13},{10,... | collective-permute-start | bytes 221192 | tf_op jit(solution)/shard_map/ppermute | solution.py:84
  29.5 11.0 %all-to-all-start.1 = ((bf16[4,12,32,128]{3,2,1,0:T(8,128)(2,1)}), bf16[4,12,32,128]{3,2,1,0:T(8,128)(2,1)S(1)}, u32[]{:S(2)}, u32[]{:S(2)}) async-start(bf16[4,12,32,128]{3,2,1,0:T(8,128)(2,1)} %broadcast_in_dim.15), calls=%async_computation.1 | async-start | bytes 786432 | tf_op jit(solution)/shard_map/all_to_all | solution.py:105
  33.5 7.0 %collective-permute-start.2 = (bf16[2,2,144,128]{3,2,1,0:T(8,128)(2,1)S(1)}, bf16[2,2,144,128]{3,2,1,0:T(8,128)(2,1)S(1)}, u32[]{:S(2)}, u32[]{:S(2)}) collective-permute-start(bf16[2,2,144,128]{3,2,1,0:T(8,128)(2,1)S(1)} %pad_maximum_fusion.near), channel_id=1, source_target_pairs={{0,2},{1,3},{2,0},{3,1},{4,6},{5,7},{6,4},{7,5},{8,10},{9,11},{10,... | collective-permute-start | bytes 442376 | tf_op jit(solution)/shard_map/ppermute | solution.py:84
  38.0 9.4 %copy-start.3 = (s32[8,16,3]{1,0,2:T(8,128)S(1)}, s32[8,16,3]{1,0,2:T(8,128)}, u32[]{:S(2)}) copy-start(s32[8,16,3]{1,0,2:T(8,128)} %param.11) | copy-start | bytes 4612
  40.5 8.2 %collective-permute-start.4 = (bf16[48,32,128]{2,1,0:T(8,128)(2,1)S(1)}, bf16[48,32,128]{2,1,0:T(8,128)(2,1)S(1)}, u32[]{:S(2)}, u32[]{:S(2)}) collective-permute-start(bf16[48,32,128]{2,1,0:T(8,128)(2,1)S(1)} %bitcast.19), channel_id=1, source_target_pairs={{0,8},{8,0},{1,9},{9,1},{2,10},{10,2},{3,11},{11,3},{4,12},{12,4},... | collective-permute-start | bytes 1179656 | tf_op jit(solution)/shard_map/ppermute | solution.py:121
  47.6 0.8 %copy-start.5 = (s32[8,8]{1,0:T(8,128)S(1)}, s32[8,8]{1,0:T(8,128)}, u32[]{:S(2)}) copy-start(s32[8,8]{1,0:T(8,128)} %param.10) | copy-start | bytes 772
  47.7 0.8 %collective-permute-start.3 = (bf16[4,2,4,4,128]{4,3,2,1,0:T(4,128)(2,1)S(1)}, bf16[4,2,4,4,128]{4,3,2,1,0:T(4,128)(2,1)S(1)}, u32[]{:S(2)}, u32[]{:S(2)}) collective-permute-start(bf16[4,2,4,4,128]{4,3,2,1,0:T(4,128)(2,1)S(1)} %maximum_select_fusion), channel_id=1, source_target_pairs={{320,327},{321,326},{322,325},{323,324},{324,323},{325,322},{326,3... | collective-permute-start | bytes 98312 | tf_op jit(solution)/shard_map/ppermute | solution.py:84

commit v8 on v7

--- a/solution.py
+++ b/solution.py
@@ -17,12 +17,11 @@
 SIZES = (12, 4, 2, 4, 2)
 
 
-def fused(place, numbers, weights, near, far, edge, mine, other, observed, ratio, dense, flat, seen):
+def fused(place, numbers, weights, own, one, two, three, edge, mine, other, observed, ratio, dense, flat, seen):
     view, side, core = place[0], place[1], place[2]
-    parts = (near.at[0], near.at[1], far.at[0], far.at[1])
-    for n, k in enumerate((0, 2, 1, 3)):
-        seen[view ^ k, :, :OWN] = parts[n][:, :OWN]
-        seen[view ^ k ^ 3, :, OWN:] = jnp.where(place[3] == 1, parts[n][:, OWN:], edge[n])
+    for k, part in enumerate((own, one, two, three)):
+        seen[view ^ k, :, :OWN] = part[:, :OWN]
+        seen[view ^ k ^ 3, :, OWN:] = jnp.where(place[3] == 1, part[:, OWN:], edge[k])
     dense[...] = jnp.zeros_like(dense)
     for w in range(2):
         for i in range(2 * BLOCKS):
@@ -101,13 +100,15 @@
     slab = jnp.concatenate([estimate.reshape(OWN, 2, 128), ahead.reshape(EDGE, 2, 128)], axis=0)
     slab = slab.transpose(1, 0, 2)
     two = permute(slab, lambda v, gy: (v ^ 2, gy))
-    along, near = lax.optimization_barrier((along, jnp.stack([slab, two])))
-    mine = lax.all_to_all(jnp.broadcast_to(along[None], (4, 12, 32, 128)), "x", 0, 0, tiled=True)
-    far = permute(near, lambda v, gy: (v ^ 1, gy))
-    mine, near, far = lax.optimization_barrier((mine, near, far))
-    rows = [part.reshape(2, 2, 18, 8, 128) for part in (near, far)]
-    upper = jnp.concatenate([part[:, :, 0:16:4, :HALO] for part in rows])
-    lower = jnp.concatenate([part[:, :, 3:16:4, HALO:] for part in rows])
+    three = permute(slab, lambda v, gy: (v ^ 3, gy))
+    one = permute(slab, lambda v, gy: (v ^ 1, gy))
+    along, two, three = lax.optimization_barrier((along, two, three))
+    spread, one = lax.optimization_barrier((jnp.broadcast_to(along[None], (4, 12, 32, 128)), one))
+    mine = lax.all_to_all(spread, "x", 0, 0, tiled=True)
+    mine, slab, one, two, three = lax.optimization_barrier((mine, slab, one, two, three))
+    rows = [part.reshape(2, 18, 8, 128) for part in (slab, one, two, three)]
+    upper = jnp.stack([part[:, 0:16:4, :HALO] for part in rows])
+    lower = jnp.stack([part[:, 3:16:4, HALO:] for part in rows])
     rows = jnp.where(side == 0, lower, upper)
     edge = permute(rows, mirror, lambda z: not early(z)).reshape(4, 2, EDGE, 128)
     mine = mine.reshape(48, 32, 128)
@@ -124,7 +125,7 @@
     ratio = pl.pallas_call(
         fused,
         out_shape=jax.ShapeDtypeStruct((2, OWN, 1024), jnp.float32),
-        in_specs=[smem] * 3 + [vmem] * 6,
+        in_specs=[smem] * 3 + [vmem] * 8,
         out_specs=vmem,
         scratch_shapes=[
             pltpu.VMEM((2, BLOCKS, 384, 128), jnp.bfloat16),
@@ -136,8 +137,10 @@
         place,
         numbers,
         weights,
-        near,
-        far,
+        slab,
+        one,
+        two,
+        three,
         edge,
         mine,
         other,

time: 52.6 us -> 56.4 us (1.072)
  the two profiles are of different devices: /device:TPU:1 before, /device:TPU:328 now
where the time goes in v8:
time: 56.4 us; the launch traced here: 55.9 us
  starting transfers between devices  34.7 us (62%)
  waiting for transfers between devices  14.6 us (26%)
  Pallas kernels  3.37 us (6%)
  local copies, waits for them, and re-layouts  2.71 us (5%)
    ppermute x5, starting transfers between devices, permute(): return lax.ppermute(array, AXES, pairs)  15.3 us
    all_to_all x1, starting transfers between devices, shards(): along = lax.all_to_all(spread, 'z', 0, 0, tiled=True)  14.1 us
    ppermute x5, waiting for transfers between devices, permute(): return lax.ppermute(array, AXES, pairs)  7.37 us
    all_to_all x1, waiting for transfers between devices, shards(): mine = lax.all_to_all(spread, 'x', 0, 0, tiled=True)  7.24 us
    all_to_all x1, starting transfers between devices, shards(): mine = lax.all_to_all(spread, 'x', 0, 0, tiled=True)  3.46 us
    pallas_call x1, Pallas kernels, shards(): pl.pallas_call(fused, out_shape=jax.ShapeDtypeStruct((2, OWN, 1024), jnp....  3.37 us
    ppermute x1, starting transfers between devices, shards(): other = lax.ppermute(mine, 'core', [(0, 1), (1, 0)])  1.91 us
  transfers between devices with their start and end apart: 8, of which 4 were waited for; matrix products, arithmetic and copies ran while one was open for 1% of the time, Pallas kernels for 0%

profile of v8, /device:TPU:328, one launch (start us, length us, event | category | flops | bytes accessed | tf_op | source)
XLA Modules:
  0.0 55.9 jit_solution(6739851480640812788)
XLA Ops:
  0.0 0.0 copy-start
  0.0 0.8 %constant_dynamic-slice_fusion.2 = bf16[4,4,256]{2,1,0:T(4,128)(2,1)S(1)} fusion(bf16[4,32,256]{2,1,0:T(8,128)(2,1)} %param.6, s32[]{:T(128)S(6)} %select_n.17), kind=kLoop, calls=%fused_computation.14 | loop fusion | bytes 16388 | tf_op jit(solution)/shard_map/dynamic_slice | solution.py:97
  0.8 0.6 %collective-permute-start = (bf16[4,4,256]{2,1,0:T(4,128)(2,1)S(1)}, bf16[4,4,256]{2,1,0:T(4,128)(2,1)S(1)}, u32[]{:S(2)}, u32[]{:S(2)}) collective-permute-start(bf16[4,4,256]{2,1,0:T(4,128)(2,1)S(1)} %constant_dynamic-slice_fusion.2), channel_id=1, source_target_pairs={{0,7},{1,6},{2,5},{3,4},{4,3},{5,2},{6,1},{7,0},{8,15},{9,14},{10,... | collective-permute-start | bytes 24584 | tf_op jit(solution)/shard_map/ppermute | solution.py:83
  1.4 0.1 reshape.39
  1.5 0.1 broadcast_in_dim.6
  1.6 0.0 collective-permute-done
  1.6 0.7 %broadcast_in_dim.14 = bf16[12,32,128]{2,1,0:T(8,128)(2,1)} broadcast(bf16[32,128]{1,0:T(8,128)(2,1)S(1)} %broadcast_in_dim.6), dimensions={1,2} | broadcast | bytes 106496 | tf_op jit(solution)/shard_map/broadcast_in_dim | solution.py:95
  2.3 14.1 %all-to-all-start = ((bf16[12,32,128]{2,1,0:T(8,128)(2,1)}), bf16[12,32,128]{2,1,0:T(8,128)(2,1)S(1)}, u32[]{:S(2)}, u32[]{:S(2)}) async-start(bf16[12,32,128]{2,1,0:T(8,128)(2,1)} %broadcast_in_dim.14), calls=%async_computation | async-start | bytes 196608 | tf_op jit(solution)/shard_map/all_to_all | solution.py:99
  16.4 0.0 copy-start.1
  16.5 3.6 %collective-permute-start.2 = (bf16[2,144,128]{2,1,0:T(8,128)(2,1)S(1)}, bf16[2,144,128]{2,1,0:T(8,128)(2,1)S(1)}, u32[]{:S(2)}, u32[]{:S(2)}) collective-permute-start(bf16[2,144,128]{2,1,0:T(8,128)(2,1)S(1)} %maximum_bitcast_fusion.own), channel_id=1, source_target_pairs={{0,6},{1,7},{2,4},{3,5},{4,2},{5,3},{6,0},{7,1},{8,14},{9,15},{10,... | collective-permute-start | bytes 221192 | tf_op jit(solution)/shard_map/ppermute | solution.py:83
  20.1 3.5 %collective-permute-start.1 = (bf16[2,144,128]{2,1,0:T(8,128)(2,1)S(1)}, bf16[2,144,128]{2,1,0:T(8,128)(2,1)S(1)}, u32[]{:S(2)}, u32[]{:S(2)}) collective-permute-start(bf16[2,144,128]{2,1,0:T(8,128)(2,1)S(1)} %maximum_bitcast_fusion.own), channel_id=1, source_target_pairs={{0,4},{1,5},{2,6},{3,7},{4,0},{5,1},{6,2},{7,3},{8,12},{9,13},{10,... | collective-permute-start | bytes 221192 | tf_op jit(solution)/shard_map/ppermute | solution.py:83
  23.6 2.3 %collective-permute-start.3 = (bf16[2,144,128]{2,1,0:T(8,128)(2,1)S(1)}, bf16[2,144,128]{2,1,0:T(8,128)(2,1)S(1)}, u32[]{:S(2)}, u32[]{:S(2)}) collective-permute-start(bf16[2,144,128]{2,1,0:T(8,128)(2,1)S(1)} %maximum_bitcast_fusion.own), channel_id=1, source_target_pairs={{0,2},{1,3},{2,0},{3,1},{4,6},{5,7},{6,4},{7,5},{8,10},{9,11},{10,... | collective-permute-start | bytes 221192 | tf_op jit(solution)/shard_map/ppermute | solution.py:83
  25.9 0.0 collective-permute-done.2.three
  25.9 1.5 %collective-permute-done.1.two = bf16[2,144,128]{2,1,0:T(8,128)(2,1)S(1)} collective-permute-done((bf16[2,144,128]{2,1,0:T(8,128)(2,1)S(1)}, bf16[2,144,128]{2,1,0:T(8,128)(2,1)S(1)}, u32[]{:S(2)}, u32[]{:S(2)}) %collective-permute-start.1) | collective-permute-done | bytes 73760 | tf_op jit(solution)/shard_map/ppermute | solution.py:83
  27.4 0.0 all-to-all-done
  27.4 2.5 %collective-permute-done.3.one = bf16[2,144,128]{2,1,0:T(8,128)(2,1)S(1)} collective-permute-done((bf16[2,144,128]{2,1,0:T(8,128)(2,1)S(1)}, bf16[2,144,128]{2,1,0:T(8,128)(2,1)S(1)}, u32[]{:S(2)}, u32[]{:S(2)}) %collective-permute-start.3) | collective-permute-done | bytes 73760 | tf_op jit(solution)/shard_map/ppermute | solution.py:83
  29.8 0.8 %broadcast_in_dim.15 = bf16[4,12,32,128]{3,2,1,0:T(8,128)(2,1)} broadcast(bf16[12,32,128]{2,1,0:T(8,128)(2,1)S(1)} %all-to-all-done), dimensions={1,2,3} | broadcast | bytes 491520 | tf_op jit(solution)/shard_map/broadcast_in_dim | solution.py:106
  30.6 3.5 %all-to-all-start.1 = ((bf16[4,12,32,128]{3,2,1,0:T(8,128)(2,1)}), bf16[4,12,32,128]{3,2,1,0:T(8,128)(2,1)S(1)}, u32[]{:S(2)}, u32[]{:S(2)}) async-start(bf16[4,12,32,128]{3,2,1,0:T(8,128)(2,1)} %broadcast_in_dim.15), calls=%async_computation.1 | async-start | bytes 786432 | tf_op jit(solution)/shard_map/all_to_all | solution.py:107
  34.1 0.0 copy-start.3
  34.1 0.1 pad_add_fusion.1.place
  34.2 7.2 %all-to-all-done.1 = bf16[4,12,32,128]{3,2,1,0:T(8,128)(2,1)S(1)} async-done(((bf16[4,12,32,128]{3,2,1,0:T(8,128)(2,1)}), bf16[4,12,32,128]{3,2,1,0:T(8,128)(2,1)S(1)}, u32[]{:S(2)}, u32[]{:S(2)}) %all-to-all-start.1) | async-done | bytes 393248 | tf_op jit(solution)/shard_map/all_to_all | solution.py:107
  41.4 1.9 %collective-permute-start.5 = (bf16[48,32,128]{2,1,0:T(8,128)(2,1)S(1)}, bf16[48,32,128]{2,1,0:T(8,128)(2,1)S(1)}, u32[]{:S(2)}, u32[]{:S(2)}) collective-permute-start(bf16[48,32,128]{2,1,0:T(8,128)(2,1)S(1)} %bitcast.35), channel_id=1, source_target_pairs={{0,8},{8,0},{1,9},{9,1},{2,10},{10,2},{3,11},{11,3},{4,12},{12,4},... | collective-permute-start | bytes 1179656 | tf_op jit(solution)/shard_map/ppermute | solution.py:122
  43.4 0.0 copy-done.3
  43.4 0.1 copy.11
  43.5 0.1 copy.12
  43.6 0.0 copy-start.5
  43.6 0.1 maximum_select_fusion
  43.7 5.3 %collective-permute-start.4 = (bf16[4,2,4,4,128]{4,3,2,1,0:T(4,128)(2,1)S(1)}, bf16[4,2,4,4,128]{4,3,2,1,0:T(4,128)(2,1)S(1)}, u32[]{:S(2)}, u32[]{:S(2)}) collective-permute-start(bf16[4,2,4,4,128]{4,3,2,1,0:T(4,128)(2,1)S(1)} %maximum_select_fusion), channel_id=1, source_target_pairs={{320,327},{321,326},{322,325},{323,324},{324,323},{325,322},{326,3... | collective-permute-start | bytes 98312 | tf_op jit(solution)/shard_map/ppermute | solution.py:83
  49.0 0.1 pad_add_fusion
  49.1 3.4 %collective-permute-done.4 = bf16[4,2,4,4,128]{4,3,2,1,0:T(4,128)(2,1)S(1)} collective-permute-done((bf16[4,2,4,4,128]{4,3,2,1,0:T(4,128)(2,1)S(1)}, bf16[4,2,4,4,128]{4,3,2,1,0:T(4,128)(2,1)S(1)}, u32[]{:S(2)}, u32[]{:S(2)}) %collective-permute-start.4) | collective-permute-done | bytes 32800 | tf_op jit(solution)/shard_map/ppermute | solution.py:83
  52.5 0.0 collective-permute-done.5.other
  52.5 3.4 %shard_map.64 = f32[2,128,1024]{2,1,0:T(8,128)} custom-call(s32[4]{0:T(128)S(1)} %pad_add_fusion.1.place, s32[2,56]{1,0:T(2,128)S(1)} %constant_dynamic-slice_fusion.1.numbers, f32[2,9]{1,0:T(2,128)S(1)} %constant_dynamic-slice_fusion.weights, bf16[2,144,128]{2,1,0:T(8,128)(2,1)S(1)} %maximum_bitcast_fusion.own, ...), custom_call_target="tpu_custom_call" | custom-call | tf_op jit(solution)/shard_map/pallas_call | solution.py:125
  (18 shorter events, 0.2 us)
Async XLA Ops:
  0.0 48.9 %copy-start = (f32[8,9]{1,0:T(8,128)S(1)}, f32[8,9]{1,0:T(8,128)}, u32[]{:S(2)}) copy-start(f32[8,9]{1,0:T(8,128)} %param.9) | copy-start | bytes 868
  0.0 1.4 %copy-start.4 = (bf16[2,2048]{1,0:T(2,128)(2,1)S(1)}, bf16[2,2048]{1,0:T(2,128)(2,1)}, u32[]{:S(2)}) copy-start(bf16[2,2048]{1,0:T(2,128)(2,1)} %param.8) | copy-start | bytes 24580
  0.8 0.9 %collective-permute-start = (bf16[4,4,256]{2,1,0:T(4,128)(2,1)S(1)}, bf16[4,4,256]{2,1,0:T(4,128)(2,1)S(1)}, u32[]{:S(2)}, u32[]{:S(2)}) collective-permute-start(bf16[4,4,256]{2,1,0:T(4,128)(2,1)S(1)} %constant_dynamic-slice_fusion.2), channel_id=1, source_target_pairs={{0,7},{1,6},{2,5},{3,4},{4,3},{5,2},{6,1},{7,0},{8,15},{9,14},{10,... | collective-permute-start | bytes 24584 | tf_op jit(solution)/shard_map/ppermute | solution.py:83
  2.3 14.1 %copy-start.2 = (bf16[4,32,256]{2,1,0:T(8,128)(2,1)S(1)}, bf16[4,32,256]{2,1,0:T(8,128)(2,1)}, u32[]{:S(2)}) copy-start(bf16[4,32,256]{2,1,0:T(8,128)(2,1)} %param.6) | copy-start | bytes 196612
  2.3 25.1 %all-to-all-start = ((bf16[12,32,128]{2,1,0:T(8,128)(2,1)}), bf16[12,32,128]{2,1,0:T(8,128)(2,1)S(1)}, u32[]{:S(2)}, u32[]{:S(2)}) async-start(bf16[12,32,128]{2,1,0:T(8,128)(2,1)} %broadcast_in_dim.14), calls=%async_computation | async-start | bytes 196608 | tf_op jit(solution)/shard_map/all_to_all | solution.py:99
  16.4 36.1 %copy-start.1 = (f32[2,4,32,1024]{3,2,1,0:T(8,128)S(1)}, f32[2,4,32,1024]{3,2,1,0:T(8,128)}, u32[]{:S(2)}) copy-start(f32[2,4,32,1024]{3,2,1,0:T(8,128)} %param.7) | copy-start | bytes 3145732
  16.5 9.4 %collective-permute-start.2 = (bf16[2,144,128]{2,1,0:T(8,128)(2,1)S(1)}, bf16[2,144,128]{2,1,0:T(8,128)(2,1)S(1)}, u32[]{:S(2)}, u32[]{:S(2)}) collective-permute-start(bf16[2,144,128]{2,1,0:T(8,128)(2,1)S(1)} %maximum_bitcast_fusion.own), channel_id=1, source_target_pairs={{0,6},{1,7},{2,4},{3,5},{4,2},{5,3},{6,0},{7,1},{8,14},{9,15},{10,... | collective-permute-start | bytes 221192 | tf_op jit(solution)/shard_map/ppermute | solution.py:83
  20.1 7.2 %collective-permute-start.1 = (bf16[2,144,128]{2,1,0:T(8,128)(2,1)S(1)}, bf16[2,144,128]{2,1,0:T(8,128)(2,1)S(1)}, u32[]{:S(2)}, u32[]{:S(2)}) collective-permute-start(bf16[2,144,128]{2,1,0:T(8,128)(2,1)S(1)} %maximum_bitcast_fusion.own), channel_id=1, source_target_pairs={{0,4},{1,5},{2,6},{3,7},{4,0},{5,1},{6,2},{7,3},{8,12},{9,13},{10,... | collective-permute-start | bytes 221192 | tf_op jit(solution)/shard_map/ppermute | solution.py:83
  23.6 6.2 %collective-permute-start.3 = (bf16[2,144,128]{2,1,0:T(8,128)(2,1)S(1)}, bf16[2,144,128]{2,1,0:T(8,128)(2,1)S(1)}, u32[]{:S(2)}, u32[]{:S(2)}) collective-permute-start(bf16[2,144,128]{2,1,0:T(8,128)(2,1)S(1)} %maximum_bitcast_fusion.own), channel_id=1, source_target_pairs={{0,2},{1,3},{2,0},{3,1},{4,6},{5,7},{6,4},{7,5},{8,10},{9,11},{10,... | collective-permute-start | bytes 221192 | tf_op jit(solution)/shard_map/ppermute | solution.py:83
  30.6 10.8 %all-to-all-start.1 = ((bf16[4,12,32,128]{3,2,1,0:T(8,128)(2,1)}), bf16[4,12,32,128]{3,2,1,0:T(8,128)(2,1)S(1)}, u32[]{:S(2)}, u32[]{:S(2)}) async-start(bf16[4,12,32,128]{3,2,1,0:T(8,128)(2,1)} %broadcast_in_dim.15), calls=%async_computation.1 | async-start | bytes 786432 | tf_op jit(solution)/shard_map/all_to_all | solution.py:107
  34.1 9.3 %copy-start.3 = (s32[8,16,3]{1,0,2:T(8,128)S(1)}, s32[8,16,3]{1,0,2:T(8,128)}, u32[]{:S(2)}) copy-start(s32[8,16,3]{1,0,2:T(8,128)} %param.11) | copy-start | bytes 4612
  41.4 11.0 %collective-permute-start.5 = (bf16[48,32,128]{2,1,0:T(8,128)(2,1)S(1)}, bf16[48,32,128]{2,1,0:T(8,128)(2,1)S(1)}, u32[]{:S(2)}, u32[]{:S(2)}) collective-permute-start(bf16[48,32,128]{2,1,0:T(8,128)(2,1)S(1)} %bitcast.35), channel_id=1, source_target_pairs={{0,8},{8,0},{1,9},{9,1},{2,10},{10,2},{3,11},{11,3},{4,12},{12,4},... | collective-permute-start | bytes 1179656 | tf_op jit(solution)/shard_map/ppermute | solution.py:122
  43.6 5.4 %copy-start.5 = (s32[8,8]{1,0:T(8,128)S(1)}, s32[8,8]{1,0:T(8,128)}, u32[]{:S(2)}) copy-start(s32[8,8]{1,0:T(8,128)} %param.10) | copy-start | bytes 772
  43.7 8.8 %collective-permute-start.4 = (bf16[4,2,4,4,128]{4,3,2,1,0:T(4,128)(2,1)S(1)}, bf16[4,2,4,4,128]{4,3,2,1,0:T(4,128)(2,1)S(1)}, u32[]{:S(2)}, u32[]{:S(2)}) collective-permute-start(bf16[4,2,4,4,128]{4,3,2,1,0:T(4,128)(2,1)S(1)} %maximum_select_fusion), channel_id=1, source_target_pairs={{320,327},{321,326},{322,325},{323,324},{324,323},{325,322},{326,3... | collective-permute-start | bytes 98312 | tf_op jit(solution)/shard_map/ppermute | solution.py:83

commit v9 on v8

--- a/solution.py
+++ b/solution.py
@@ -12,7 +12,7 @@
 EDGE = PLANES * HALO
 BLOCKS = 8
 BAND = 3
-AHEAD = 5
+AHEAD = 7
 AXES = ("z", "x", "core", "view", "gy")
 SIZES = (12, 4, 2, 4, 2)
 
@@ -94,17 +94,21 @@
     shard = psf_blocks.reshape(2, 32, 64).transpose(1, 0, 2).reshape(1, 32, 128)
     spread = jnp.broadcast_to(shard, (12, 32, 128))
     begin = jnp.where(side == 0, ROWS - HALO, 0)
-    ahead = permute(lax.dynamic_slice_in_dim(estimate, begin, HALO, 1), mirror, early)
+    ahead = lax.dynamic_slice_in_dim(estimate, begin, HALO, 1)
     ahead, spread, estimate = lax.optimization_barrier((ahead, spread, estimate))
+    ahead = permute(ahead, mirror, early)
+    ahead, block_source, psf_columns = lax.optimization_barrier((ahead, block_source, psf_columns))
+    first = 2 * lax.axis_index("view")
+    numbers = jnp.concatenate([block_source, psf_columns.reshape(8, 48)], axis=1)
+    numbers = lax.dynamic_slice_in_dim(numbers, first, 2, 0)
     along = lax.all_to_all(spread, "z", 0, 0, tiled=True)
     slab = jnp.concatenate([estimate.reshape(OWN, 2, 128), ahead.reshape(EDGE, 2, 128)], axis=0)
     slab = slab.transpose(1, 0, 2)
     two = permute(slab, lambda v, gy: (v ^ 2, gy))
     three = permute(slab, lambda v, gy: (v ^ 3, gy))
+    along, two, three, slab, numbers = lax.optimization_barrier((along, two, three, slab, numbers))
+    mine = lax.all_to_all(jnp.broadcast_to(along[None], (4, 12, 32, 128)), "x", 0, 0, tiled=True)
     one = permute(slab, lambda v, gy: (v ^ 1, gy))
-    along, two, three = lax.optimization_barrier((along, two, three))
-    spread, one = lax.optimization_barrier((jnp.broadcast_to(along[None], (4, 12, 32, 128)), one))
-    mine = lax.all_to_all(spread, "x", 0, 0, tiled=True)
     mine, slab, one, two, three = lax.optimization_barrier((mine, slab, one, two, three))
     rows = [part.reshape(2, 18, 8, 128) for part in (slab, one, two, three)]
     upper = jnp.stack([part[:, 0:16:4, :HALO] for part in rows])
@@ -112,12 +116,7 @@
     rows = jnp.where(side == 0, lower, upper)
     edge = permute(rows, mirror, lambda z: not early(z)).reshape(4, 2, EDGE, 128)
     mine = mine.reshape(48, 32, 128)
-    kernel_y, block_source, psf_columns = lax.optimization_barrier(
-        (kernel_y, block_source, psf_columns, mine)
-    )[:3]
-    first = 2 * lax.axis_index("view")
-    numbers = jnp.concatenate([block_source, psf_columns.reshape(8, 48)], axis=1)
-    numbers = lax.dynamic_slice_in_dim(numbers, first, 2, 0)
+    kernel_y, _ = lax.optimization_barrier((kernel_y, mine))
     weights = lax.dynamic_slice_in_dim(kernel_y, first, 2, 0)
     other = lax.ppermute(mine, "core", [(0, 1), (1, 0)])
     smem = pl.BlockSpec(memory_space=pltpu.SMEM)

time: 56.4 us -> 55.6 us (0.986)
  the two profiles are of different devices: /device:TPU:328 before, /device:TPU:1 now
where the time goes in v9:
time: 55.6 us; the launch traced here: 55.2 us
  starting transfers between devices  39.7 us (71%)
  waiting for transfers between devices  8.98 us (16%)
  Pallas kernels  3.38 us (6%)
  local copies, waits for them, and re-layouts  2.68 us (5%)
    ppermute x5, starting transfers between devices, permute(): return lax.ppermute(array, AXES, pairs)  15.7 us
    all_to_all x1, starting transfers between devices, shards(): along = lax.all_to_all(spread, 'z', 0, 0, tiled=True)  14.3 us
    ppermute x5, waiting for transfers between devices, permute(): return lax.ppermute(array, AXES, pairs)  7.32 us
    ppermute x1, starting transfers between devices, shards(): other = lax.ppermute(mine, 'core', [(0, 1), (1, 0)])  5.7 us
    all_to_all x1, starting transfers between devices, shards(): lax.all_to_all(jnp.broadcast_to(along[None], (4, 12, 32, 128)), 'x', 0, 0...  4.01 us
    pallas_call x1, Pallas kernels, shards(): pl.pallas_call(fused, out_shape=jax.ShapeDtypeStruct((2, OWN, 1024), jnp....  3.38 us
    all_to_all x1, waiting for transfers between devices, shards(): lax.all_to_all(jnp.broadcast_to(along[None], (4, 12, 32, 128)), 'x', 0, 0...  1.15 us
  transfers between devices with their start and end apart: 8, of which 4 were waited for; matrix products, arithmetic and copies ran while one was open for 1% of the time, Pallas kernels for 0%

profile of v9, /device:TPU:1, one launch (start us, length us, event | category | flops | bytes accessed | tf_op | source)
XLA Modules:
  0.0 55.2 jit_solution(13080337772492451660)
XLA Ops:
  0.0 0.0 copy-start
  0.0 0.8 %reshape.39 = bf16[2,32,64]{2,1,0:T(8,128)(2,1)S(1)} reshape(bf16[2,2048]{1,0:T(2,128)(2,1)} %param.8) | data formatting | bytes 16384 | tf_op jit(solution)/shard_map/reshape | solution.py:94
  0.8 0.1 broadcast_in_dim.6
  0.9 0.0 copy-done.2
  0.9 0.7 %broadcast_in_dim.14 = bf16[12,32,128]{2,1,0:T(8,128)(2,1)} broadcast(bf16[32,128]{1,0:T(8,128)(2,1)S(1)} %broadcast_in_dim.6), dimensions={1,2} | broadcast | bytes 106496 | tf_op jit(solution)/shard_map/broadcast_in_dim | solution.py:95
  1.6 5.9 %collective-permute-start = (bf16[4,4,256]{2,1,0:T(4,128)(2,1)S(1)}, bf16[4,4,256]{2,1,0:T(4,128)(2,1)S(1)}, u32[]{:S(2)}, u32[]{:S(2)}) collective-permute-start(bf16[4,4,256]{2,1,0:T(4,128)(2,1)S(1)} %constant_dynamic-slice_fusion.2), channel_id=1, source_target_pairs={{0,7},{1,6},{2,5},{3,4},{4,3},{5,2},{6,1},{7,0},{8,15},{9,14},{10,... | collective-permute-start | bytes 24584 | tf_op jit(solution)/shard_map/ppermute | solution.py:83
  7.5 14.3 %all-to-all-start = ((bf16[12,32,128]{2,1,0:T(8,128)(2,1)}), bf16[12,32,128]{2,1,0:T(8,128)(2,1)S(1)}, u32[]{:S(2)}, u32[]{:S(2)}) async-start(bf16[12,32,128]{2,1,0:T(8,128)(2,1)} %broadcast_in_dim.14), calls=%async_computation | async-start | bytes 196608 | tf_op jit(solution)/shard_map/all_to_all | solution.py:104
  21.8 0.0 copy-start.4
  21.8 0.0 copy-start.3
  21.8 0.0 copy-start.1
  21.9 0.0 collective-permute-done
  21.9 4.7 %collective-permute-start.2 = (bf16[2,144,128]{2,1,0:T(8,128)(2,1)S(1)}, bf16[2,144,128]{2,1,0:T(8,128)(2,1)S(1)}, u32[]{:S(2)}, u32[]{:S(2)}) collective-permute-start(bf16[2,144,128]{2,1,0:T(8,128)(2,1)S(1)} %maximum_bitcast_fusion.own), channel_id=1, source_target_pairs={{0,6},{1,7},{2,4},{3,5},{4,2},{5,3},{6,0},{7,1},{8,14},{9,15},{10,... | collective-permute-start | bytes 221192 | tf_op jit(solution)/shard_map/ppermute | solution.py:83
  26.6 2.4 %collective-permute-start.1 = (bf16[2,144,128]{2,1,0:T(8,128)(2,1)S(1)}, bf16[2,144,128]{2,1,0:T(8,128)(2,1)S(1)}, u32[]{:S(2)}, u32[]{:S(2)}) collective-permute-start(bf16[2,144,128]{2,1,0:T(8,128)(2,1)S(1)} %maximum_bitcast_fusion.own), channel_id=1, source_target_pairs={{0,4},{1,5},{2,6},{3,7},{4,0},{5,1},{6,2},{7,3},{8,12},{9,13},{10,... | collective-permute-start | bytes 221192 | tf_op jit(solution)/shard_map/ppermute | solution.py:83
  29.1 0.0 copy-done.3
  29.1 0.1 copy.11
  29.2 0.1 copy.12
  29.2 0.1 pad_add_fusion
  29.3 0.0 collective-permute-done.2.three
  29.3 4.4 %collective-permute-done.1.two = bf16[2,144,128]{2,1,0:T(8,128)(2,1)S(1)} collective-permute-done((bf16[2,144,128]{2,1,0:T(8,128)(2,1)S(1)}, bf16[2,144,128]{2,1,0:T(8,128)(2,1)S(1)}, u32[]{:S(2)}, u32[]{:S(2)}) %collective-permute-start.1) | collective-permute-done | bytes 73760 | tf_op jit(solution)/shard_map/ppermute | solution.py:83
  33.7 0.0 all-to-all-done
  33.7 0.8 %broadcast_in_dim.15 = bf16[4,12,32,128]{3,2,1,0:T(8,128)(2,1)} broadcast(bf16[12,32,128]{2,1,0:T(8,128)(2,1)S(1)} %all-to-all-done), dimensions={1,2,3} | broadcast | bytes 491520 | tf_op jit(solution)/shard_map/broadcast_in_dim | solution.py:110
  34.5 4.0 %all-to-all-start.1 = ((bf16[4,12,32,128]{3,2,1,0:T(8,128)(2,1)}), bf16[4,12,32,128]{3,2,1,0:T(8,128)(2,1)S(1)}, u32[]{:S(2)}, u32[]{:S(2)}) async-start(bf16[4,12,32,128]{3,2,1,0:T(8,128)(2,1)} %broadcast_in_dim.15), calls=%async_computation.1 | async-start | bytes 786432 | tf_op jit(solution)/shard_map/all_to_all | solution.py:110
  38.5 2.1 %collective-permute-start.3 = (bf16[2,144,128]{2,1,0:T(8,128)(2,1)S(1)}, bf16[2,144,128]{2,1,0:T(8,128)(2,1)S(1)}, u32[]{:S(2)}, u32[]{:S(2)}) collective-permute-start(bf16[2,144,128]{2,1,0:T(8,128)(2,1)S(1)} %maximum_bitcast_fusion.own), channel_id=1, source_target_pairs={{0,2},{1,3},{2,0},{3,1},{4,6},{5,7},{6,4},{7,5},{8,10},{9,11},{10,... | collective-permute-start | bytes 221192 | tf_op jit(solution)/shard_map/ppermute | solution.py:83
  40.6 0.1 pad_add_fusion.1.place
  40.7 2.9 %collective-permute-done.3.one = bf16[2,144,128]{2,1,0:T(8,128)(2,1)S(1)} collective-permute-done((bf16[2,144,128]{2,1,0:T(8,128)(2,1)S(1)}, bf16[2,144,128]{2,1,0:T(8,128)(2,1)S(1)}, u32[]{:S(2)}, u32[]{:S(2)}) %collective-permute-start.3) | collective-permute-done | bytes 73760 | tf_op jit(solution)/shard_map/ppermute | solution.py:83
  43.6 1.1 %all-to-all-done.1 = bf16[4,12,32,128]{3,2,1,0:T(8,128)(2,1)S(1)} async-done(((bf16[4,12,32,128]{3,2,1,0:T(8,128)(2,1)}), bf16[4,12,32,128]{3,2,1,0:T(8,128)(2,1)S(1)}, u32[]{:S(2)}, u32[]{:S(2)}) %all-to-all-start.1) | async-done | bytes 393248 | tf_op jit(solution)/shard_map/all_to_all | solution.py:110
  44.8 5.7 %collective-permute-start.5 = (bf16[48,32,128]{2,1,0:T(8,128)(2,1)S(1)}, bf16[48,32,128]{2,1,0:T(8,128)(2,1)S(1)}, u32[]{:S(2)}, u32[]{:S(2)}) collective-permute-start(bf16[48,32,128]{2,1,0:T(8,128)(2,1)S(1)} %bitcast.35), channel_id=1, source_target_pairs={{0,8},{8,0},{1,9},{9,1},{2,10},{10,2},{3,11},{11,3},{4,12},{12,4},... | collective-permute-start | bytes 1179656 | tf_op jit(solution)/shard_map/ppermute | solution.py:121
  50.5 0.1 maximum_select_fusion
  50.6 0.7 %collective-permute-start.4 = (bf16[4,2,4,4,128]{4,3,2,1,0:T(4,128)(2,1)S(1)}, bf16[4,2,4,4,128]{4,3,2,1,0:T(4,128)(2,1)S(1)}, u32[]{:S(2)}, u32[]{:S(2)}) collective-permute-start(bf16[4,2,4,4,128]{4,3,2,1,0:T(4,128)(2,1)S(1)} %maximum_select_fusion), channel_id=1, source_target_pairs={{448,455},{449,454},{450,453},{451,452},{452,451},{453,450},{454,4... | collective-permute-start | bytes 98312 | tf_op jit(solution)/shard_map/ppermute | solution.py:83
  51.3 0.0 collective-permute-done.4
  51.3 0.5 collective-permute-done.5.other
  51.8 3.4 %shard_map.64 = f32[2,128,1024]{2,1,0:T(8,128)} custom-call(s32[4]{0:T(128)S(1)} %pad_add_fusion.1.place, s32[2,56]{1,0:T(2,128)S(1)} %constant_dynamic-slice_fusion.1.numbers, f32[2,9]{1,0:T(2,128)S(1)} %constant_dynamic-slice_fusion.weights, bf16[2,144,128]{2,1,0:T(8,128)(2,1)S(1)} %maximum_bitcast_fusion.own, ...), custom_call_target="tpu_custom_call" | custom-call | tf_op jit(solution)/shard_map/pallas_call | solution.py:124
  (16 shorter events, 0.2 us)
Async XLA Ops:
  0.0 51.3 %copy-start = (f32[8,9]{1,0:T(8,128)S(1)}, f32[8,9]{1,0:T(8,128)}, u32[]{:S(2)}) copy-start(f32[8,9]{1,0:T(8,128)} %param.9) | copy-start | bytes 868
  0.0 0.9 %copy-start.2 = (bf16[4,32,256]{2,1,0:T(8,128)(2,1)S(1)}, bf16[4,32,256]{2,1,0:T(8,128)(2,1)}, u32[]{:S(2)}) copy-start(bf16[4,32,256]{2,1,0:T(8,128)(2,1)} %param.6) | copy-start | bytes 196612
  1.6 20.3 %collective-permute-start = (bf16[4,4,256]{2,1,0:T(4,128)(2,1)S(1)}, bf16[4,4,256]{2,1,0:T(4,128)(2,1)S(1)}, u32[]{:S(2)}, u32[]{:S(2)}) collective-permute-start(bf16[4,4,256]{2,1,0:T(4,128)(2,1)S(1)} %constant_dynamic-slice_fusion.2), channel_id=1, source_target_pairs={{0,7},{1,6},{2,5},{3,4},{4,3},{5,2},{6,1},{7,0},{8,15},{9,14},{10,... | collective-permute-start | bytes 24584 | tf_op jit(solution)/shard_map/ppermute | solution.py:83
  7.5 26.2 %all-to-all-start = ((bf16[12,32,128]{2,1,0:T(8,128)(2,1)}), bf16[12,32,128]{2,1,0:T(8,128)(2,1)S(1)}, u32[]{:S(2)}, u32[]{:S(2)}) async-start(bf16[12,32,128]{2,1,0:T(8,128)(2,1)} %broadcast_in_dim.14), calls=%async_computation | async-start | bytes 196608 | tf_op jit(solution)/shard_map/all_to_all | solution.py:104
  21.8 7.4 %copy-start.4 = (s32[8,8]{1,0:T(8,128)S(1)}, s32[8,8]{1,0:T(8,128)}, u32[]{:S(2)}) copy-start(s32[8,8]{1,0:T(8,128)} %param.10) | copy-start | bytes 772
  21.8 7.2 %copy-start.3 = (s32[8,16,3]{1,0,2:T(8,128)S(1)}, s32[8,16,3]{1,0,2:T(8,128)}, u32[]{:S(2)}) copy-start(s32[8,16,3]{1,0,2:T(8,128)} %param.11) | copy-start | bytes 4612
  21.8 30.0 %copy-start.1 = (f32[2,4,32,1024]{3,2,1,0:T(8,128)S(1)}, f32[2,4,32,1024]{3,2,1,0:T(8,128)}, u32[]{:S(2)}) copy-start(f32[2,4,32,1024]{3,2,1,0:T(8,128)} %param.7) | copy-start | bytes 3145732
  21.9 7.4 %collective-permute-start.2 = (bf16[2,144,128]{2,1,0:T(8,128)(2,1)S(1)}, bf16[2,144,128]{2,1,0:T(8,128)(2,1)S(1)}, u32[]{:S(2)}, u32[]{:S(2)}) collective-permute-start(bf16[2,144,128]{2,1,0:T(8,128)(2,1)S(1)} %maximum_bitcast_fusion.own), channel_id=1, source_target_pairs={{0,6},{1,7},{2,4},{3,5},{4,2},{5,3},{6,0},{7,1},{8,14},{9,15},{10,... | collective-permute-start | bytes 221192 | tf_op jit(solution)/shard_map/ppermute | solution.py:83
  26.6 7.1 %collective-permute-start.1 = (bf16[2,144,128]{2,1,0:T(8,128)(2,1)S(1)}, bf16[2,144,128]{2,1,0:T(8,128)(2,1)S(1)}, u32[]{:S(2)}, u32[]{:S(2)}) collective-permute-start(bf16[2,144,128]{2,1,0:T(8,128)(2,1)S(1)} %maximum_bitcast_fusion.own), channel_id=1, source_target_pairs={{0,4},{1,5},{2,6},{3,7},{4,0},{5,1},{6,2},{7,3},{8,12},{9,13},{10,... | collective-permute-start | bytes 221192 | tf_op jit(solution)/shard_map/ppermute | solution.py:83
  34.5 10.2 %all-to-all-start.1 = ((bf16[4,12,32,128]{3,2,1,0:T(8,128)(2,1)}), bf16[4,12,32,128]{3,2,1,0:T(8,128)(2,1)S(1)}, u32[]{:S(2)}, u32[]{:S(2)}) async-start(bf16[4,12,32,128]{3,2,1,0:T(8,128)(2,1)} %broadcast_in_dim.15), calls=%async_computation.1 | async-start | bytes 786432 | tf_op jit(solution)/shard_map/all_to_all | solution.py:110
  38.5 5.1 %collective-permute-start.3 = (bf16[2,144,128]{2,1,0:T(8,128)(2,1)S(1)}, bf16[2,144,128]{2,1,0:T(8,128)(2,1)S(1)}, u32[]{:S(2)}, u32[]{:S(2)}) collective-permute-start(bf16[2,144,128]{2,1,0:T(8,128)(2,1)S(1)} %maximum_bitcast_fusion.own), channel_id=1, source_target_pairs={{0,2},{1,3},{2,0},{3,1},{4,6},{5,7},{6,4},{7,5},{8,10},{9,11},{10,... | collective-permute-start | bytes 221192 | tf_op jit(solution)/shard_map/ppermute | solution.py:83
  44.8 7.0 %collective-permute-start.5 = (bf16[48,32,128]{2,1,0:T(8,128)(2,1)S(1)}, bf16[48,32,128]{2,1,0:T(8,128)(2,1)S(1)}, u32[]{:S(2)}, u32[]{:S(2)}) collective-permute-start(bf16[48,32,128]{2,1,0:T(8,128)(2,1)S(1)} %bitcast.35), channel_id=1, source_target_pairs={{0,8},{8,0},{1,9},{9,1},{2,10},{10,2},{3,11},{11,3},{4,12},{12,4},... | collective-permute-start | bytes 1179656 | tf_op jit(solution)/shard_map/ppermute | solution.py:121
  50.6 0.7 %collective-permute-start.4 = (bf16[4,2,4,4,128]{4,3,2,1,0:T(4,128)(2,1)S(1)}, bf16[4,2,4,4,128]{4,3,2,1,0:T(4,128)(2,1)S(1)}, u32[]{:S(2)}, u32[]{:S(2)}) collective-permute-start(bf16[4,2,4,4,128]{4,3,2,1,0:T(4,128)(2,1)S(1)} %maximum_select_fusion), channel_id=1, source_target_pairs={{448,455},{449,454},{450,453},{451,452},{452,451},{453,450},{454,4... | collective-permute-start | bytes 98312 | tf_op jit(solution)/shard_map/ppermute | solution.py:83

commit v10 on v9

--- a/solution.py
+++ b/solution.py
@@ -12,24 +12,25 @@
 EDGE = PLANES * HALO
 BLOCKS = 8
 BAND = 3
-AHEAD = 7
+AHEAD = 5
 AXES = ("z", "x", "core", "view", "gy")
 SIZES = (12, 4, 2, 4, 2)
 
 
-def fused(place, numbers, weights, own, one, two, three, edge, mine, other, observed, ratio, dense, flat, seen):
+def fused(place, numbers, weights, own, one, two, three, edge, mine, other, observed, ratio, dense, seen, done, sems):
     view, side, core = place[0], place[1], place[2]
     for k, part in enumerate((own, one, two, three)):
         seen[view ^ k, :, :OWN] = part[:, :OWN]
         seen[view ^ k ^ 3, :, OWN:] = jnp.where(place[3] == 1, part[:, OWN:], edge[k])
-    dense[...] = jnp.zeros_like(dense)
-    for w in range(2):
+
+    def build(w):
+        dense[w] = jnp.zeros_like(dense[w])
         for i in range(2 * BLOCKS):
-            j, half = i // 2, i % 2
+            j, quarter = i // 4, i % 4
             for k in range(BAND):
-                shift = (numbers[w, BLOCKS + i * BAND + k] - (2 * j - 2)) & 15
+                shift = (numbers[w, BLOCKS + i * BAND + k] - (4 * j - 2)) & 15
                 base = shift * 64
-                lanes = pl.ds(64 * half, 64)
+                lanes = pl.ds(64 * quarter, 64)
                 q = i * BAND + k
                 s = q % 4 * 12 + q // 4
                 dense[w, j, pl.ds(pl.multiple_of(base + 32 * core, 32), 32), lanes] = mine[
@@ -39,16 +40,11 @@
                     s, :, 64 * w : 64 * w + 64
                 ]
 
+    build(0)
+
     def block(w, j):
         b = numbers[w, j % BLOCKS]
         return seen[b // 2, b % 2]
-
-    for w in range(2):
-        for j in range(BLOCKS):
-            wide = jnp.concatenate([block(w, j + BLOCKS - 1), block(w, j), block(w, j + 1)], axis=1)
-            flat[w, :, 128 * j : 128 * j + 128] = jnp.dot(
-                wide, dense[w, j], preferred_element_type=jnp.float32
-            ).astype(jnp.bfloat16)
 
     shape = (OWN, OWN + EDGE)
     row = lax.broadcasted_iota(jnp.int32, shape, 0)
@@ -57,16 +53,40 @@
     spot = jnp.where(col < OWN, col & (ROWS - 1), (outer & (HALO - 1)) + jnp.where(side == 0, ROWS, -HALO))
     plane = jnp.where(col < OWN, col >> 5, outer >> 2)
     tap = jnp.where(plane == (row >> 5), spot - (row & (ROWS - 1)) + HALO, -1)
+    mixes = []
     for w in range(2):
         mix = jnp.zeros(shape, jnp.float32)
         for t in range(2 * HALO + 1):
             mix = jnp.where(tap == t, weights[w, t], mix)
         high = mix.astype(jnp.bfloat16)
         low = (mix - high.astype(jnp.float32)).astype(jnp.bfloat16)
-        lateral = flat[w]
-        blurred = jnp.dot(high, lateral, preferred_element_type=jnp.float32)
-        blurred = blurred + jnp.dot(low, lateral, preferred_element_type=jnp.float32)
-        ratio[w] = observed[w] / blurred
+        mixes.append((high, low))
+
+    copies = []
+
+    def lateral(n):
+        w, j = n // 4, n % 4
+        wide = jnp.concatenate([block(w, 2 * j + BLOCKS + s) for s in (-1, 0, 1, 2)], axis=1)
+        return jnp.dot(wide, dense[w, j], preferred_element_type=jnp.float32).astype(jnp.bfloat16)
+
+    def finish(n, rows):
+        w, j = n // 4, n % 4
+        lanes = slice(256 * j, 256 * j + 256)
+        blurred = jnp.dot(mixes[w][0], rows, preferred_element_type=jnp.float32)
+        blurred = blurred + jnp.dot(mixes[w][1], rows, preferred_element_type=jnp.float32)
+        done[w, :, lanes] = observed[w, :, lanes] / blurred
+        copies.append(pltpu.make_async_copy(done.at[w, :, lanes], ratio.at[w, :, lanes], sems.at[n]))
+        copies[-1].start()
+
+    rows = lateral(0)
+    for n in range(8):
+        if n == 0:
+            build(1)
+        after = lateral(n + 1) if n < 7 else None
+        finish(n, rows)
+        rows = after
+    for copy in copies:
+        copy.wait()
 
 
 def early(z):
@@ -125,11 +145,12 @@
         fused,
         out_shape=jax.ShapeDtypeStruct((2, OWN, 1024), jnp.float32),
         in_specs=[smem] * 3 + [vmem] * 8,
-        out_specs=vmem,
+        out_specs=pl.BlockSpec(memory_space=pl.ANY),
         scratch_shapes=[
-            pltpu.VMEM((2, BLOCKS, 384, 128), jnp.bfloat16),
-            pltpu.VMEM((2, OWN + EDGE, 1024), jnp.bfloat16),
+            pltpu.VMEM((2, BLOCKS // 2, 512, 256), jnp.bfloat16),
             pltpu.VMEM((4, 2, OWN + EDGE, 128), jnp.bfloat16),
+            pltpu.VMEM((2, OWN, 1024), jnp.float32),
+            pltpu.SemaphoreType.DMA((8,)),
         ],
         compiler_params=pltpu.CompilerParams(vmem_limit_bytes=16 * 1024 * 1024),
     )(

time: 55.6 us -> 51.8 us (0.932)
  the two profiles are of different devices: /device:TPU:1 before, /device:TPU:321 now
where the time goes in v10:
time: 51.8 us; the launch traced here: 51.4 us
  starting transfers between devices  35.3 us (68%)
  waiting for transfers between devices  10.2 us (20%)
  Pallas kernels  2.76 us (5%)
  local copies, waits for them, and re-layouts  2.68 us (5%)
    ppermute x5, starting transfers between devices, permute(): return lax.ppermute(array, AXES, pairs)  14.7 us
    all_to_all x1, starting transfers between devices, shards(): along = lax.all_to_all(spread, 'z', 0, 0, tiled=True)  10.6 us
    ppermute x5, waiting for transfers between devices, permute(): return lax.ppermute(array, AXES, pairs)  9.04 us
    ppermute x1, starting transfers between devices, shards(): other = lax.ppermute(mine, 'core', [(0, 1), (1, 0)])  6.09 us
    all_to_all x1, starting transfers between devices, shards(): lax.all_to_all(jnp.broadcast_to(along[None], (4, 12, 32, 128)), 'x', 0, 0...  4.01 us
    pallas_call x1, Pallas kernels, shards(): pl.pallas_call(fused, out_shape=jax.ShapeDtypeStruct((2, OWN, 1024), jnp....  2.76 us
    all_to_all x1, waiting for transfers between devices, shards(): lax.all_to_all(jnp.broadcast_to(along[None], (4, 12, 32, 128)), 'x', 0, 0...  1.15 us
  transfers between devices with their start and end apart: 8, of which 4 were waited for; matrix products, arithmetic and copies ran while one was open for 1% of the time, Pallas kernels for 0%

profile of v10, /device:TPU:321, one launch (start us, length us, event | category | flops | bytes accessed | tf_op | source)
XLA Modules:
  0.0 51.4 jit_solution(2139404686169058527)
XLA Ops:
  0.0 0.0 copy-start
  0.0 0.8 %reshape.39 = bf16[2,32,64]{2,1,0:T(8,128)(2,1)S(1)} reshape(bf16[2,2048]{1,0:T(2,128)(2,1)} %param.8) | data formatting | bytes 16384 | tf_op jit(solution)/shard_map/reshape | solution.py:114
  0.8 0.1 broadcast_in_dim.6
  0.9 0.0 copy-done.2
  0.9 0.7 %broadcast_in_dim.14 = bf16[12,32,128]{2,1,0:T(8,128)(2,1)} broadcast(bf16[32,128]{1,0:T(8,128)(2,1)S(1)} %broadcast_in_dim.6), dimensions={1,2} | broadcast | bytes 106496 | tf_op jit(solution)/shard_map/broadcast_in_dim | solution.py:115
  1.6 0.6 %collective-permute-start = (bf16[4,4,256]{2,1,0:T(4,128)(2,1)S(1)}, bf16[4,4,256]{2,1,0:T(4,128)(2,1)S(1)}, u32[]{:S(2)}, u32[]{:S(2)}) collective-permute-start(bf16[4,4,256]{2,1,0:T(4,128)(2,1)S(1)} %constant_dynamic-slice_fusion.2), channel_id=1, source_target_pairs={{0,7},{1,6},{2,5},{3,4},{4,3},{5,2},{6,1},{7,0},{8,15},{9,14},{10,... | collective-permute-start | bytes 24584 | tf_op jit(solution)/shard_map/ppermute | solution.py:103
  2.3 10.6 %all-to-all-start = ((bf16[12,32,128]{2,1,0:T(8,128)(2,1)}), bf16[12,32,128]{2,1,0:T(8,128)(2,1)S(1)}, u32[]{:S(2)}, u32[]{:S(2)}) async-start(bf16[12,32,128]{2,1,0:T(8,128)(2,1)} %broadcast_in_dim.14), calls=%async_computation | async-start | bytes 196608 | tf_op jit(solution)/shard_map/all_to_all | solution.py:124
  12.9 0.0 copy-start.1
  12.9 0.0 collective-permute-done
  13.0 5.4 %collective-permute-start.2 = (bf16[2,144,128]{2,1,0:T(8,128)(2,1)S(1)}, bf16[2,144,128]{2,1,0:T(8,128)(2,1)S(1)}, u32[]{:S(2)}, u32[]{:S(2)}) collective-permute-start(bf16[2,144,128]{2,1,0:T(8,128)(2,1)S(1)} %maximum_bitcast_fusion.own), channel_id=1, source_target_pairs={{0,6},{1,7},{2,4},{3,5},{4,2},{5,3},{6,0},{7,1},{8,14},{9,15},{10,... | collective-permute-start | bytes 221192 | tf_op jit(solution)/shard_map/ppermute | solution.py:103
  18.3 1.9 %collective-permute-start.1 = (bf16[2,144,128]{2,1,0:T(8,128)(2,1)S(1)}, bf16[2,144,128]{2,1,0:T(8,128)(2,1)S(1)}, u32[]{:S(2)}, u32[]{:S(2)}) collective-permute-start(bf16[2,144,128]{2,1,0:T(8,128)(2,1)S(1)} %maximum_bitcast_fusion.own), channel_id=1, source_target_pairs={{0,4},{1,5},{2,6},{3,7},{4,0},{5,1},{6,2},{7,3},{8,12},{9,13},{10,... | collective-permute-start | bytes 221192 | tf_op jit(solution)/shard_map/ppermute | solution.py:103
  20.3 0.0 copy-done.3
  20.3 0.1 copy.11
  20.4 0.1 copy.12
  20.4 0.0 copy-done.4
  20.4 0.1 pad_add_fusion
  20.5 0.0 collective-permute-done.2.three
  20.5 3.8 %collective-permute-done.1.two = bf16[2,144,128]{2,1,0:T(8,128)(2,1)S(1)} collective-permute-done((bf16[2,144,128]{2,1,0:T(8,128)(2,1)S(1)}, bf16[2,144,128]{2,1,0:T(8,128)(2,1)S(1)}, u32[]{:S(2)}, u32[]{:S(2)}) %collective-permute-start.1) | collective-permute-done | bytes 73760 | tf_op jit(solution)/shard_map/ppermute | solution.py:103
  24.3 0.0 all-to-all-done
  24.3 0.8 %broadcast_in_dim.15 = bf16[4,12,32,128]{3,2,1,0:T(8,128)(2,1)} broadcast(bf16[12,32,128]{2,1,0:T(8,128)(2,1)S(1)} %all-to-all-done), dimensions={1,2,3} | broadcast | bytes 491520 | tf_op jit(solution)/shard_map/broadcast_in_dim | solution.py:130
  25.2 4.0 %all-to-all-start.1 = ((bf16[4,12,32,128]{3,2,1,0:T(8,128)(2,1)}), bf16[4,12,32,128]{3,2,1,0:T(8,128)(2,1)S(1)}, u32[]{:S(2)}, u32[]{:S(2)}) async-start(bf16[4,12,32,128]{3,2,1,0:T(8,128)(2,1)} %broadcast_in_dim.15), calls=%async_computation.1 | async-start | bytes 786432 | tf_op jit(solution)/shard_map/all_to_all | solution.py:130
  29.2 2.4 %collective-permute-start.3 = (bf16[2,144,128]{2,1,0:T(8,128)(2,1)S(1)}, bf16[2,144,128]{2,1,0:T(8,128)(2,1)S(1)}, u32[]{:S(2)}, u32[]{:S(2)}) collective-permute-start(bf16[2,144,128]{2,1,0:T(8,128)(2,1)S(1)} %maximum_bitcast_fusion.own), channel_id=1, source_target_pairs={{0,2},{1,3},{2,0},{3,1},{4,6},{5,7},{6,4},{7,5},{8,10},{9,11},{10,... | collective-permute-start | bytes 221192 | tf_op jit(solution)/shard_map/ppermute | solution.py:103
  31.6 0.1 pad_add_fusion.1.place
  31.7 2.6 %collective-permute-done.3.one = bf16[2,144,128]{2,1,0:T(8,128)(2,1)S(1)} collective-permute-done((bf16[2,144,128]{2,1,0:T(8,128)(2,1)S(1)}, bf16[2,144,128]{2,1,0:T(8,128)(2,1)S(1)}, u32[]{:S(2)}, u32[]{:S(2)}) %collective-permute-start.3) | collective-permute-done | bytes 73760 | tf_op jit(solution)/shard_map/ppermute | solution.py:103
  34.2 1.1 %all-to-all-done.1 = bf16[4,12,32,128]{3,2,1,0:T(8,128)(2,1)S(1)} async-done(((bf16[4,12,32,128]{3,2,1,0:T(8,128)(2,1)}), bf16[4,12,32,128]{3,2,1,0:T(8,128)(2,1)S(1)}, u32[]{:S(2)}, u32[]{:S(2)}) %all-to-all-start.1) | async-done | bytes 393248 | tf_op jit(solution)/shard_map/all_to_all | solution.py:130
  35.4 6.1 %collective-permute-start.5 = (bf16[48,32,128]{2,1,0:T(8,128)(2,1)S(1)}, bf16[48,32,128]{2,1,0:T(8,128)(2,1)S(1)}, u32[]{:S(2)}, u32[]{:S(2)}) collective-permute-start(bf16[48,32,128]{2,1,0:T(8,128)(2,1)S(1)} %bitcast.35), channel_id=1, source_target_pairs={{0,8},{8,0},{1,9},{9,1},{2,10},{10,2},{3,11},{11,3},{4,12},{12,4},... | collective-permute-start | bytes 1179656 | tf_op jit(solution)/shard_map/ppermute | solution.py:141
  41.5 0.1 maximum_select_fusion
  41.6 4.3 %collective-permute-start.4 = (bf16[4,2,4,4,128]{4,3,2,1,0:T(4,128)(2,1)S(1)}, bf16[4,2,4,4,128]{4,3,2,1,0:T(4,128)(2,1)S(1)}, u32[]{:S(2)}, u32[]{:S(2)}) collective-permute-start(bf16[4,2,4,4,128]{4,3,2,1,0:T(4,128)(2,1)S(1)} %maximum_select_fusion), channel_id=1, source_target_pairs={{320,327},{321,326},{322,325},{323,324},{324,323},{325,322},{326,3... | collective-permute-start | bytes 98312 | tf_op jit(solution)/shard_map/ppermute | solution.py:103
  46.0 2.6 %collective-permute-done.4 = bf16[4,2,4,4,128]{4,3,2,1,0:T(4,128)(2,1)S(1)} collective-permute-done((bf16[4,2,4,4,128]{4,3,2,1,0:T(4,128)(2,1)S(1)}, bf16[4,2,4,4,128]{4,3,2,1,0:T(4,128)(2,1)S(1)}, u32[]{:S(2)}, u32[]{:S(2)}) %collective-permute-start.4) | collective-permute-done | bytes 32800 | tf_op jit(solution)/shard_map/ppermute | solution.py:103
  48.6 0.0 collective-permute-done.5.other
  48.6 0.0 copy-done.1
  48.6 2.8 %shard_map.64 = f32[2,128,1024]{2,1,0:T(8,128)} custom-call(s32[4]{0:T(128)S(1)} %pad_add_fusion.1.place, s32[2,56]{1,0:T(2,128)S(1)} %constant_dynamic-slice_fusion.1.numbers, f32[2,9]{1,0:T(2,128)S(1)} %constant_dynamic-slice_fusion.weights, bf16[2,144,128]{2,1,0:T(8,128)(2,1)S(1)} %maximum_bitcast_fusion.own, ...), custom_call_target="tpu_custom_call" | custom-call | tf_op jit(solution)/shard_map/pallas_call | solution.py:144
  (16 shorter events, 0.2 us)
Async XLA Ops:
  0.0 45.9 %copy-start = (f32[8,9]{1,0:T(8,128)S(1)}, f32[8,9]{1,0:T(8,128)}, u32[]{:S(2)}) copy-start(f32[8,9]{1,0:T(8,128)} %param.9) | copy-start | bytes 868
  0.0 0.9 %copy-start.2 = (bf16[4,32,256]{2,1,0:T(8,128)(2,1)S(1)}, bf16[4,32,256]{2,1,0:T(8,128)(2,1)}, u32[]{:S(2)}) copy-start(bf16[4,32,256]{2,1,0:T(8,128)(2,1)} %param.6) | copy-start | bytes 196612
  1.6 11.3 %collective-permute-start = (bf16[4,4,256]{2,1,0:T(4,128)(2,1)S(1)}, bf16[4,4,256]{2,1,0:T(4,128)(2,1)S(1)}, u32[]{:S(2)}, u32[]{:S(2)}) collective-permute-start(bf16[4,4,256]{2,1,0:T(4,128)(2,1)S(1)} %constant_dynamic-slice_fusion.2), channel_id=1, source_target_pairs={{0,7},{1,6},{2,5},{3,4},{4,3},{5,2},{6,1},{7,0},{8,15},{9,14},{10,... | collective-permute-start | bytes 24584 | tf_op jit(solution)/shard_map/ppermute | solution.py:103
  2.3 22.1 %all-to-all-start = ((bf16[12,32,128]{2,1,0:T(8,128)(2,1)}), bf16[12,32,128]{2,1,0:T(8,128)(2,1)S(1)}, u32[]{:S(2)}, u32[]{:S(2)}) async-start(bf16[12,32,128]{2,1,0:T(8,128)(2,1)} %broadcast_in_dim.14), calls=%async_computation | async-start | bytes 196608 | tf_op jit(solution)/shard_map/all_to_all | solution.py:124
  12.9 7.6 %copy-start.4 = (s32[8,8]{1,0:T(8,128)S(1)}, s32[8,8]{1,0:T(8,128)}, u32[]{:S(2)}) copy-start(s32[8,8]{1,0:T(8,128)} %param.10) | copy-start | bytes 772
  12.9 7.4 %copy-start.3 = (s32[8,16,3]{1,0,2:T(8,128)S(1)}, s32[8,16,3]{1,0,2:T(8,128)}, u32[]{:S(2)}) copy-start(s32[8,16,3]{1,0,2:T(8,128)} %param.11) | copy-start | bytes 4612
  12.9 35.8 %copy-start.1 = (f32[2,4,32,1024]{3,2,1,0:T(8,128)S(1)}, f32[2,4,32,1024]{3,2,1,0:T(8,128)}, u32[]{:S(2)}) copy-start(f32[2,4,32,1024]{3,2,1,0:T(8,128)} %param.7) | copy-start | bytes 3145732
  13.0 7.6 %collective-permute-start.2 = (bf16[2,144,128]{2,1,0:T(8,128)(2,1)S(1)}, bf16[2,144,128]{2,1,0:T(8,128)(2,1)S(1)}, u32[]{:S(2)}, u32[]{:S(2)}) collective-permute-start(bf16[2,144,128]{2,1,0:T(8,128)(2,1)S(1)} %maximum_bitcast_fusion.own), channel_id=1, source_target_pairs={{0,6},{1,7},{2,4},{3,5},{4,2},{5,3},{6,0},{7,1},{8,14},{9,15},{10,... | collective-permute-start | bytes 221192 | tf_op jit(solution)/shard_map/ppermute | solution.py:103
  18.3 6.0 %collective-permute-start.1 = (bf16[2,144,128]{2,1,0:T(8,128)(2,1)S(1)}, bf16[2,144,128]{2,1,0:T(8,128)(2,1)S(1)}, u32[]{:S(2)}, u32[]{:S(2)}) collective-permute-start(bf16[2,144,128]{2,1,0:T(8,128)(2,1)S(1)} %maximum_bitcast_fusion.own), channel_id=1, source_target_pairs={{0,4},{1,5},{2,6},{3,7},{4,0},{5,1},{6,2},{7,3},{8,12},{9,13},{10,... | collective-permute-start | bytes 221192 | tf_op jit(solution)/shard_map/ppermute | solution.py:103
  25.2 10.2 %all-to-all-start.1 = ((bf16[4,12,32,128]{3,2,1,0:T(8,128)(2,1)}), bf16[4,12,32,128]{3,2,1,0:T(8,128)(2,1)S(1)}, u32[]{:S(2)}, u32[]{:S(2)}) async-start(bf16[4,12,32,128]{3,2,1,0:T(8,128)(2,1)} %broadcast_in_dim.15), calls=%async_computation.1 | async-start | bytes 786432 | tf_op jit(solution)/shard_map/all_to_all | solution.py:130
  29.2 5.1 %collective-permute-start.3 = (bf16[2,144,128]{2,1,0:T(8,128)(2,1)S(1)}, bf16[2,144,128]{2,1,0:T(8,128)(2,1)S(1)}, u32[]{:S(2)}, u32[]{:S(2)}) collective-permute-start(bf16[2,144,128]{2,1,0:T(8,128)(2,1)S(1)} %maximum_bitcast_fusion.own), channel_id=1, source_target_pairs={{0,2},{1,3},{2,0},{3,1},{4,6},{5,7},{6,4},{7,5},{8,10},{9,11},{10,... | collective-permute-start | bytes 221192 | tf_op jit(solution)/shard_map/ppermute | solution.py:103
  35.4 13.2 %collective-permute-start.5 = (bf16[48,32,128]{2,1,0:T(8,128)(2,1)S(1)}, bf16[48,32,128]{2,1,0:T(8,128)(2,1)S(1)}, u32[]{:S(2)}, u32[]{:S(2)}) collective-permute-start(bf16[48,32,128]{2,1,0:T(8,128)(2,1)S(1)} %bitcast.35), channel_id=1, source_target_pairs={{0,8},{8,0},{1,9},{9,1},{2,10},{10,2},{3,11},{11,3},{4,12},{12,4},... | collective-permute-start | bytes 1179656 | tf_op jit(solution)/shard_map/ppermute | solution.py:141
  41.6 7.0 %collective-permute-start.4 = (bf16[4,2,4,4,128]{4,3,2,1,0:T(4,128)(2,1)S(1)}, bf16[4,2,4,4,128]{4,3,2,1,0:T(4,128)(2,1)S(1)}, u32[]{:S(2)}, u32[]{:S(2)}) collective-permute-start(bf16[4,2,4,4,128]{4,3,2,1,0:T(4,128)(2,1)S(1)} %maximum_select_fusion), channel_id=1, source_target_pairs={{320,327},{321,326},{322,325},{323,324},{324,323},{325,322},{326,3... | collective-permute-start | bytes 98312 | tf_op jit(solution)/shard_map/ppermute | solution.py:103

commit v11 on v10

--- a/solution.py
+++ b/solution.py
@@ -12,7 +12,7 @@
 EDGE = PLANES * HALO
 BLOCKS = 8
 BAND = 3
-AHEAD = 5
+AHEAD = 6
 AXES = ("z", "x", "core", "view", "gy")
 SIZES = (12, 4, 2, 4, 2)
 
@@ -125,10 +125,10 @@
     slab = jnp.concatenate([estimate.reshape(OWN, 2, 128), ahead.reshape(EDGE, 2, 128)], axis=0)
     slab = slab.transpose(1, 0, 2)
     two = permute(slab, lambda v, gy: (v ^ 2, gy))
+    one = permute(slab, lambda v, gy: (v ^ 1, gy))
+    along, one, two, slab, numbers = lax.optimization_barrier((along, one, two, slab, numbers))
+    mine = lax.all_to_all(jnp.broadcast_to(along[None], (4, 12, 32, 128)), "x", 0, 0, tiled=True)
     three = permute(slab, lambda v, gy: (v ^ 3, gy))
-    along, two, three, slab, numbers = lax.optimization_barrier((along, two, three, slab, numbers))
-    mine = lax.all_to_all(jnp.broadcast_to(along[None], (4, 12, 32, 128)), "x", 0, 0, tiled=True)
-    one = permute(slab, lambda v, gy: (v ^ 1, gy))
     mine, slab, one, two, three = lax.optimization_barrier((mine, slab, one, two, three))
     rows = [part.reshape(2, 18, 8, 128) for part in (slab, one, two, three)]
     upper = jnp.stack([part[:, 0:16:4, :HALO] for part in rows])

time: 51.8 us -> 52 us (level)
  the two profiles are of different devices: /device:TPU:321 before, /device:TPU:1 now
where the time goes in v11:
time: 52 us; the launch traced here: 51.6 us
  starting transfers between devices  39.5 us (76%)
  waiting for transfers between devices  6.14 us (12%)
  Pallas kernels  2.76 us (5%)
  local copies, waits for them, and re-layouts  2.68 us (5%)
    ppermute x5, starting transfers between devices, permute(): return lax.ppermute(array, AXES, pairs)  17.8 us
    all_to_all x1, starting transfers between devices, shards(): along = lax.all_to_all(spread, 'z', 0, 0, tiled=True)  11.9 us
    ppermute x1, starting transfers between devices, shards(): other = lax.ppermute(mine, 'core', [(0, 1), (1, 0)])  5.91 us
    ppermute x5, waiting for transfers between devices, permute(): return lax.ppermute(array, AXES, pairs)  5.63 us
    all_to_all x1, starting transfers between devices, shards(): lax.all_to_all(jnp.broadcast_to(along[None], (4, 12, 32, 128)), 'x', 0, 0...  4.01 us
    pallas_call x1, Pallas kernels, shards(): pl.pallas_call(fused, out_shape=jax.ShapeDtypeStruct((2, OWN, 1024), jnp....  2.76 us
  transfers between devices with their start and end apart: 8, of which 3 were waited for; matrix products, arithmetic and copies ran while one was open for 1% of the time, Pallas kernels for 0%

profile of v11, /device:TPU:1, one launch (start us, length us, event | category | flops | bytes accessed | tf_op | source)
XLA Modules:
  0.0 51.6 jit_solution(1579964073718944990)
XLA Ops:
  0.0 0.0 copy-start
  0.0 0.8 %reshape.39 = bf16[2,32,64]{2,1,0:T(8,128)(2,1)S(1)} reshape(bf16[2,2048]{1,0:T(2,128)(2,1)} %param.8) | data formatting | bytes 16384 | tf_op jit(solution)/shard_map/reshape | solution.py:114
  0.8 0.1 broadcast_in_dim.6
  0.9 0.0 copy-done.2
  0.9 0.7 %broadcast_in_dim.14 = bf16[12,32,128]{2,1,0:T(8,128)(2,1)} broadcast(bf16[32,128]{1,0:T(8,128)(2,1)S(1)} %broadcast_in_dim.6), dimensions={1,2} | broadcast | bytes 106496 | tf_op jit(solution)/shard_map/broadcast_in_dim | solution.py:115
  1.6 5.9 %collective-permute-start = (bf16[4,4,256]{2,1,0:T(4,128)(2,1)S(1)}, bf16[4,4,256]{2,1,0:T(4,128)(2,1)S(1)}, u32[]{:S(2)}, u32[]{:S(2)}) collective-permute-start(bf16[4,4,256]{2,1,0:T(4,128)(2,1)S(1)} %constant_dynamic-slice_fusion.2), channel_id=1, source_target_pairs={{0,7},{1,6},{2,5},{3,4},{4,3},{5,2},{6,1},{7,0},{8,15},{9,14},{10,... | collective-permute-start | bytes 24584 | tf_op jit(solution)/shard_map/ppermute | solution.py:103
  7.5 11.9 %all-to-all-start = ((bf16[12,32,128]{2,1,0:T(8,128)(2,1)}), bf16[12,32,128]{2,1,0:T(8,128)(2,1)S(1)}, u32[]{:S(2)}, u32[]{:S(2)}) async-start(bf16[12,32,128]{2,1,0:T(8,128)(2,1)} %broadcast_in_dim.14), calls=%async_computation | async-start | bytes 196608 | tf_op jit(solution)/shard_map/all_to_all | solution.py:124
  19.4 0.0 copy-start.4
  19.4 0.0 copy-start.3
  19.4 0.0 copy-start.1
  19.5 0.0 collective-permute-done
  19.5 4.8 %collective-permute-start.2 = (bf16[2,144,128]{2,1,0:T(8,128)(2,1)S(1)}, bf16[2,144,128]{2,1,0:T(8,128)(2,1)S(1)}, u32[]{:S(2)}, u32[]{:S(2)}) collective-permute-start(bf16[2,144,128]{2,1,0:T(8,128)(2,1)S(1)} %maximum_bitcast_fusion.own), channel_id=1, source_target_pairs={{0,4},{1,5},{2,6},{3,7},{4,0},{5,1},{6,2},{7,3},{8,12},{9,13},{10,... | collective-permute-start | bytes 221192 | tf_op jit(solution)/shard_map/ppermute | solution.py:103
  24.3 2.1 %collective-permute-start.1 = (bf16[2,144,128]{2,1,0:T(8,128)(2,1)S(1)}, bf16[2,144,128]{2,1,0:T(8,128)(2,1)S(1)}, u32[]{:S(2)}, u32[]{:S(2)}) collective-permute-start(bf16[2,144,128]{2,1,0:T(8,128)(2,1)S(1)} %maximum_bitcast_fusion.own), channel_id=1, source_target_pairs={{0,2},{1,3},{2,0},{3,1},{4,6},{5,7},{6,4},{7,5},{8,10},{9,11},{10,... | collective-permute-start | bytes 221192 | tf_op jit(solution)/shard_map/ppermute | solution.py:103
  26.4 0.1 copy.11
  26.5 0.1 copy.12
  26.6 0.1 pad_add_fusion
  26.7 0.0 collective-permute-done.2.two
  26.7 3.0 %collective-permute-done.1.one = bf16[2,144,128]{2,1,0:T(8,128)(2,1)S(1)} collective-permute-done((bf16[2,144,128]{2,1,0:T(8,128)(2,1)S(1)}, bf16[2,144,128]{2,1,0:T(8,128)(2,1)S(1)}, u32[]{:S(2)}, u32[]{:S(2)}) %collective-permute-start.1) | collective-permute-done | bytes 73760 | tf_op jit(solution)/shard_map/ppermute | solution.py:103
  29.7 0.0 all-to-all-done
  29.7 0.8 %broadcast_in_dim.15 = bf16[4,12,32,128]{3,2,1,0:T(8,128)(2,1)} broadcast(bf16[12,32,128]{2,1,0:T(8,128)(2,1)S(1)} %all-to-all-done), dimensions={1,2,3} | broadcast | bytes 491520 | tf_op jit(solution)/shard_map/broadcast_in_dim | solution.py:130
  30.5 4.0 %all-to-all-start.1 = ((bf16[4,12,32,128]{3,2,1,0:T(8,128)(2,1)}), bf16[4,12,32,128]{3,2,1,0:T(8,128)(2,1)S(1)}, u32[]{:S(2)}, u32[]{:S(2)}) async-start(bf16[4,12,32,128]{3,2,1,0:T(8,128)(2,1)} %broadcast_in_dim.15), calls=%async_computation.1 | async-start | bytes 786432 | tf_op jit(solution)/shard_map/all_to_all | solution.py:130
  34.5 4.3 %collective-permute-start.3 = (bf16[2,144,128]{2,1,0:T(8,128)(2,1)S(1)}, bf16[2,144,128]{2,1,0:T(8,128)(2,1)S(1)}, u32[]{:S(2)}, u32[]{:S(2)}) collective-permute-start(bf16[2,144,128]{2,1,0:T(8,128)(2,1)S(1)} %maximum_bitcast_fusion.own), channel_id=1, source_target_pairs={{0,6},{1,7},{2,4},{3,5},{4,2},{5,3},{6,0},{7,1},{8,14},{9,15},{10,... | collective-permute-start | bytes 221192 | tf_op jit(solution)/shard_map/ppermute | solution.py:103
  38.9 0.1 pad_add_fusion.1.place
  38.9 2.6 %collective-permute-done.3.three = bf16[2,144,128]{2,1,0:T(8,128)(2,1)S(1)} collective-permute-done((bf16[2,144,128]{2,1,0:T(8,128)(2,1)S(1)}, bf16[2,144,128]{2,1,0:T(8,128)(2,1)S(1)}, u32[]{:S(2)}, u32[]{:S(2)}) %collective-permute-start.3) | collective-permute-done | bytes 73760 | tf_op jit(solution)/shard_map/ppermute | solution.py:103
  41.5 0.0 all-to-all-done.1
  41.5 5.9 %collective-permute-start.5 = (bf16[48,32,128]{2,1,0:T(8,128)(2,1)S(1)}, bf16[48,32,128]{2,1,0:T(8,128)(2,1)S(1)}, u32[]{:S(2)}, u32[]{:S(2)}) collective-permute-start(bf16[48,32,128]{2,1,0:T(8,128)(2,1)S(1)} %bitcast.35), channel_id=1, source_target_pairs={{0,8},{8,0},{1,9},{9,1},{2,10},{10,2},{3,11},{11,3},{4,12},{12,4},... | collective-permute-start | bytes 1179656 | tf_op jit(solution)/shard_map/ppermute | solution.py:141
  47.5 0.1 maximum_select_fusion
  47.6 0.7 %collective-permute-start.4 = (bf16[4,2,4,4,128]{4,3,2,1,0:T(4,128)(2,1)S(1)}, bf16[4,2,4,4,128]{4,3,2,1,0:T(4,128)(2,1)S(1)}, u32[]{:S(2)}, u32[]{:S(2)}) collective-permute-start(bf16[4,2,4,4,128]{4,3,2,1,0:T(4,128)(2,1)S(1)} %maximum_select_fusion), channel_id=1, source_target_pairs={{384,391},{385,390},{386,389},{387,388},{388,387},{389,386},{390,3... | collective-permute-start | bytes 98312 | tf_op jit(solution)/shard_map/ppermute | solution.py:103
  48.3 0.0 collective-permute-done.4
  48.3 0.5 collective-permute-done.5.other
  48.8 0.0 copy-done.1
  48.8 2.8 %shard_map.64 = f32[2,128,1024]{2,1,0:T(8,128)} custom-call(s32[4]{0:T(128)S(1)} %pad_add_fusion.1.place, s32[2,56]{1,0:T(2,128)S(1)} %constant_dynamic-slice_fusion.1.numbers, f32[2,9]{1,0:T(2,128)S(1)} %constant_dynamic-slice_fusion.weights, bf16[2,144,128]{2,1,0:T(8,128)(2,1)S(1)} %maximum_bitcast_fusion.own, ...), custom_call_target="tpu_custom_call" | custom-call | tf_op jit(solution)/shard_map/pallas_call | solution.py:144
  (16 shorter events, 0.2 us)
Async XLA Ops:
  0.0 48.2 %copy-start = (f32[8,9]{1,0:T(8,128)S(1)}, f32[8,9]{1,0:T(8,128)}, u32[]{:S(2)}) copy-start(f32[8,9]{1,0:T(8,128)} %param.9) | copy-start | bytes 868
  0.0 0.9 %copy-start.2 = (bf16[4,32,256]{2,1,0:T(8,128)(2,1)S(1)}, bf16[4,32,256]{2,1,0:T(8,128)(2,1)}, u32[]{:S(2)}) copy-start(bf16[4,32,256]{2,1,0:T(8,128)(2,1)} %param.6) | copy-start | bytes 196612
  1.6 17.9 %collective-permute-start = (bf16[4,4,256]{2,1,0:T(4,128)(2,1)S(1)}, bf16[4,4,256]{2,1,0:T(4,128)(2,1)S(1)}, u32[]{:S(2)}, u32[]{:S(2)}) collective-permute-start(bf16[4,4,256]{2,1,0:T(4,128)(2,1)S(1)} %constant_dynamic-slice_fusion.2), channel_id=1, source_target_pairs={{0,7},{1,6},{2,5},{3,4},{4,3},{5,2},{6,1},{7,0},{8,15},{9,14},{10,... | collective-permute-start | bytes 24584 | tf_op jit(solution)/shard_map/ppermute | solution.py:103
  7.5 22.2 %all-to-all-start = ((bf16[12,32,128]{2,1,0:T(8,128)(2,1)}), bf16[12,32,128]{2,1,0:T(8,128)(2,1)S(1)}, u32[]{:S(2)}, u32[]{:S(2)}) async-start(bf16[12,32,128]{2,1,0:T(8,128)(2,1)} %broadcast_in_dim.14), calls=%async_computation | async-start | bytes 196608 | tf_op jit(solution)/shard_map/all_to_all | solution.py:124
  19.4 7.2 %copy-start.4 = (s32[8,8]{1,0:T(8,128)S(1)}, s32[8,8]{1,0:T(8,128)}, u32[]{:S(2)}) copy-start(s32[8,8]{1,0:T(8,128)} %param.10) | copy-start | bytes 772
  19.4 7.0 %copy-start.3 = (s32[8,16,3]{1,0,2:T(8,128)S(1)}, s32[8,16,3]{1,0,2:T(8,128)}, u32[]{:S(2)}) copy-start(s32[8,16,3]{1,0,2:T(8,128)} %param.11) | copy-start | bytes 4612
  19.4 29.4 %copy-start.1 = (f32[2,4,32,1024]{3,2,1,0:T(8,128)S(1)}, f32[2,4,32,1024]{3,2,1,0:T(8,128)}, u32[]{:S(2)}) copy-start(f32[2,4,32,1024]{3,2,1,0:T(8,128)} %param.7) | copy-start | bytes 3145732
  19.5 7.2 %collective-permute-start.2 = (bf16[2,144,128]{2,1,0:T(8,128)(2,1)S(1)}, bf16[2,144,128]{2,1,0:T(8,128)(2,1)S(1)}, u32[]{:S(2)}, u32[]{:S(2)}) collective-permute-start(bf16[2,144,128]{2,1,0:T(8,128)(2,1)S(1)} %maximum_bitcast_fusion.own), channel_id=1, source_target_pairs={{0,4},{1,5},{2,6},{3,7},{4,0},{5,1},{6,2},{7,3},{8,12},{9,13},{10,... | collective-permute-start | bytes 221192 | tf_op jit(solution)/shard_map/ppermute | solution.py:103
  24.3 5.4 %collective-permute-start.1 = (bf16[2,144,128]{2,1,0:T(8,128)(2,1)S(1)}, bf16[2,144,128]{2,1,0:T(8,128)(2,1)S(1)}, u32[]{:S(2)}, u32[]{:S(2)}) collective-permute-start(bf16[2,144,128]{2,1,0:T(8,128)(2,1)S(1)} %maximum_bitcast_fusion.own), channel_id=1, source_target_pairs={{0,2},{1,3},{2,0},{3,1},{4,6},{5,7},{6,4},{7,5},{8,10},{9,11},{10,... | collective-permute-start | bytes 221192 | tf_op jit(solution)/shard_map/ppermute | solution.py:103
  30.5 11.0 %all-to-all-start.1 = ((bf16[4,12,32,128]{3,2,1,0:T(8,128)(2,1)}), bf16[4,12,32,128]{3,2,1,0:T(8,128)(2,1)S(1)}, u32[]{:S(2)}, u32[]{:S(2)}) async-start(bf16[4,12,32,128]{3,2,1,0:T(8,128)(2,1)} %broadcast_in_dim.15), calls=%async_computation.1 | async-start | bytes 786432 | tf_op jit(solution)/shard_map/all_to_all | solution.py:130
  34.5 7.0 %collective-permute-start.3 = (bf16[2,144,128]{2,1,0:T(8,128)(2,1)S(1)}, bf16[2,144,128]{2,1,0:T(8,128)(2,1)S(1)}, u32[]{:S(2)}, u32[]{:S(2)}) collective-permute-start(bf16[2,144,128]{2,1,0:T(8,128)(2,1)S(1)} %maximum_bitcast_fusion.own), channel_id=1, source_target_pairs={{0,6},{1,7},{2,4},{3,5},{4,2},{5,3},{6,0},{7,1},{8,14},{9,15},{10,... | collective-permute-start | bytes 221192 | tf_op jit(solution)/shard_map/ppermute | solution.py:103
  41.5 7.2 %collective-permute-start.5 = (bf16[48,32,128]{2,1,0:T(8,128)(2,1)S(1)}, bf16[48,32,128]{2,1,0:T(8,128)(2,1)S(1)}, u32[]{:S(2)}, u32[]{:S(2)}) collective-permute-start(bf16[48,32,128]{2,1,0:T(8,128)(2,1)S(1)} %bitcast.35), channel_id=1, source_target_pairs={{0,8},{8,0},{1,9},{9,1},{2,10},{10,2},{3,11},{11,3},{4,12},{12,4},... | collective-permute-start | bytes 1179656 | tf_op jit(solution)/shard_map/ppermute | solution.py:141
  47.6 0.7 %collective-permute-start.4 = (bf16[4,2,4,4,128]{4,3,2,1,0:T(4,128)(2,1)S(1)}, bf16[4,2,4,4,128]{4,3,2,1,0:T(4,128)(2,1)S(1)}, u32[]{:S(2)}, u32[]{:S(2)}) collective-permute-start(bf16[4,2,4,4,128]{4,3,2,1,0:T(4,128)(2,1)S(1)} %maximum_select_fusion), channel_id=1, source_target_pairs={{384,391},{385,390},{386,389},{387,388},{388,387},{389,386},{390,3... | collective-permute-start | bytes 98312 | tf_op jit(solution)/shard_map/ppermute | solution.py:103

commit v12 on v10

--- a/solution.py
+++ b/solution.py
@@ -12,7 +12,7 @@
 EDGE = PLANES * HALO
 BLOCKS = 8
 BAND = 3
-AHEAD = 5
+AHEAD = 22
 AXES = ("z", "x", "core", "view", "gy")
 SIZES = (12, 4, 2, 4, 2)
 
@@ -89,14 +89,14 @@
         copy.wait()
 
 
-def early(z):
-    return z < AHEAD
+def early(z, x):
+    return z * SIZES[1] + x < AHEAD
 
 
-def permute(array, route, chosen=lambda z: True):
+def permute(array, route, chosen=lambda *at: True):
     pairs = []
     for z, x, core, v, gy in itertools.product(*map(range, SIZES)):
-        if chosen(z):
+        if chosen(z, x):
             to, across = route(v, gy)
             base = ((z * SIZES[1] + x) * SIZES[2] + core) * SIZES[3]
             pairs.append(((base + v) * SIZES[4] + gy, (base + to) * SIZES[4] + across))
@@ -109,7 +109,7 @@
 
 def shards(estimate, observed, psf_blocks, kernel_y, block_source, psf_columns):
     side = lax.axis_index("gy")
-    place = [lax.axis_index("view"), side, lax.axis_index("core"), early(lax.axis_index("z"))]
+    place = [lax.axis_index("view"), side, lax.axis_index("core"), early(lax.axis_index("z"), lax.axis_index("x"))]
     place = jnp.stack([jnp.asarray(entry, jnp.int32) for entry in place])
     shard = psf_blocks.reshape(2, 32, 64).transpose(1, 0, 2).reshape(1, 32, 128)
     spread = jnp.broadcast_to(shard, (12, 32, 128))
@@ -134,7 +134,7 @@
     upper = jnp.stack([part[:, 0:16:4, :HALO] for part in rows])
     lower = jnp.stack([part[:, 3:16:4, HALO:] for part in rows])
     rows = jnp.where(side == 0, lower, upper)
-    edge = permute(rows, mirror, lambda z: not early(z)).reshape(4, 2, EDGE, 128)
+    edge = permute(rows, mirror, lambda *at: not early(*at)).reshape(4, 2, EDGE, 128)
     mine = mine.reshape(48, 32, 128)
     kernel_y, _ = lax.optimization_barrier((kernel_y, mine))
     weights = lax.dynamic_slice_in_dim(kernel_y, first, 2, 0)

time: 51.8 us -> 51.9 us (level)
  the two profiles are of different devices: /device:TPU:321 before, /device:TPU:1 now
where the time goes in v12:
time: 51.9 us; the launch traced here: 51.3 us
  starting transfers between devices  36.5 us (70%)
  waiting for transfers between devices  8.91 us (17%)
  Pallas kernels  2.76 us (5%)
  local copies, waits for them, and re-layouts  2.68 us (5%)
    ppermute x5, starting transfers between devices, permute(): return lax.ppermute(array, AXES, pairs)  15.8 us
    all_to_all x1, starting transfers between devices, shards(): along = lax.all_to_all(spread, 'z', 0, 0, tiled=True)  11.9 us
    ppermute x5, waiting for transfers between devices, permute(): return lax.ppermute(array, AXES, pairs)  7.32 us
    ppermute x1, starting transfers between devices, shards(): other = lax.ppermute(mine, 'core', [(0, 1), (1, 0)])  5.42 us
    all_to_all x1, starting transfers between devices, shards(): lax.all_to_all(jnp.broadcast_to(along[None], (4, 12, 32, 128)), 'x', 0, 0...  3.46 us
    pallas_call x1, Pallas kernels, shards(): pl.pallas_call(fused, out_shape=jax.ShapeDtypeStruct((2, OWN, 1024), jnp....  2.76 us
    all_to_all x1, waiting for transfers between devices, shards(): lax.all_to_all(jnp.broadcast_to(along[None], (4, 12, 32, 128)), 'x', 0, 0...  1.08 us
  transfers between devices with their start and end apart: 8, of which 4 were waited for; matrix products, arithmetic and copies ran while one was open for 1% of the time, Pallas kernels for 0%

profile of v12, /device:TPU:1, one launch (start us, length us, event | category | flops | bytes accessed | tf_op | source)
XLA Modules:
  0.0 51.3 jit_solution(4030968990617666549)
XLA Ops:
  0.0 0.0 copy-start
  0.0 0.8 %reshape.39 = bf16[2,32,64]{2,1,0:T(8,128)(2,1)S(1)} reshape(bf16[2,2048]{1,0:T(2,128)(2,1)} %param.8) | data formatting | bytes 16384 | tf_op jit(solution)/shard_map/reshape | solution.py:114
  0.8 0.1 broadcast_in_dim.6
  0.9 0.0 copy-done.2
  0.9 0.7 %broadcast_in_dim.14 = bf16[12,32,128]{2,1,0:T(8,128)(2,1)} broadcast(bf16[32,128]{1,0:T(8,128)(2,1)S(1)} %broadcast_in_dim.6), dimensions={1,2} | broadcast | bytes 106496 | tf_op jit(solution)/shard_map/broadcast_in_dim | solution.py:115
  1.6 5.9 %collective-permute-start = (bf16[4,4,256]{2,1,0:T(4,128)(2,1)S(1)}, bf16[4,4,256]{2,1,0:T(4,128)(2,1)S(1)}, u32[]{:S(2)}, u32[]{:S(2)}) collective-permute-start(bf16[4,4,256]{2,1,0:T(4,128)(2,1)S(1)} %constant_dynamic-slice_fusion.2), channel_id=1, source_target_pairs={{0,7},{1,6},{2,5},{3,4},{4,3},{5,2},{6,1},{7,0},{8,15},{9,14},{10,... | collective-permute-start | bytes 24584 | tf_op jit(solution)/shard_map/ppermute | solution.py:103
  7.5 11.9 %all-to-all-start = ((bf16[12,32,128]{2,1,0:T(8,128)(2,1)}), bf16[12,32,128]{2,1,0:T(8,128)(2,1)S(1)}, u32[]{:S(2)}, u32[]{:S(2)}) async-start(bf16[12,32,128]{2,1,0:T(8,128)(2,1)} %broadcast_in_dim.14), calls=%async_computation | async-start | bytes 196608 | tf_op jit(solution)/shard_map/all_to_all | solution.py:124
  19.4 0.0 copy-start.3
  19.4 0.0 copy-start.4
  19.4 0.0 copy-start.1
  19.5 0.0 collective-permute-done
  19.5 4.7 %collective-permute-start.2 = (bf16[2,144,128]{2,1,0:T(8,128)(2,1)S(1)}, bf16[2,144,128]{2,1,0:T(8,128)(2,1)S(1)}, u32[]{:S(2)}, u32[]{:S(2)}) collective-permute-start(bf16[2,144,128]{2,1,0:T(8,128)(2,1)S(1)} %maximum_bitcast_fusion.own), channel_id=1, source_target_pairs={{0,6},{1,7},{2,4},{3,5},{4,2},{5,3},{6,0},{7,1},{8,14},{9,15},{10,... | collective-permute-start | bytes 221192 | tf_op jit(solution)/shard_map/ppermute | solution.py:103
  24.2 2.4 %collective-permute-start.1 = (bf16[2,144,128]{2,1,0:T(8,128)(2,1)S(1)}, bf16[2,144,128]{2,1,0:T(8,128)(2,1)S(1)}, u32[]{:S(2)}, u32[]{:S(2)}) collective-permute-start(bf16[2,144,128]{2,1,0:T(8,128)(2,1)S(1)} %maximum_bitcast_fusion.own), channel_id=1, source_target_pairs={{0,4},{1,5},{2,6},{3,7},{4,0},{5,1},{6,2},{7,3},{8,12},{9,13},{10,... | collective-permute-start | bytes 221192 | tf_op jit(solution)/shard_map/ppermute | solution.py:103
  26.6 0.0 copy-done.3
  26.7 0.1 copy.11
  26.8 0.1 copy.12
  26.8 0.1 pad_add_fusion
  26.9 0.0 collective-permute-done.2.three
  26.9 4.4 %collective-permute-done.1.two = bf16[2,144,128]{2,1,0:T(8,128)(2,1)S(1)} collective-permute-done((bf16[2,144,128]{2,1,0:T(8,128)(2,1)S(1)}, bf16[2,144,128]{2,1,0:T(8,128)(2,1)S(1)}, u32[]{:S(2)}, u32[]{:S(2)}) %collective-permute-start.1) | collective-permute-done | bytes 73760 | tf_op jit(solution)/shard_map/ppermute | solution.py:103
  31.3 0.0 all-to-all-done
  31.3 0.8 %broadcast_in_dim.15 = bf16[4,12,32,128]{3,2,1,0:T(8,128)(2,1)} broadcast(bf16[12,32,128]{2,1,0:T(8,128)(2,1)S(1)} %all-to-all-done), dimensions={1,2,3} | broadcast | bytes 491520 | tf_op jit(solution)/shard_map/broadcast_in_dim | solution.py:130
  32.1 3.5 %all-to-all-start.1 = ((bf16[4,12,32,128]{3,2,1,0:T(8,128)(2,1)}), bf16[4,12,32,128]{3,2,1,0:T(8,128)(2,1)S(1)}, u32[]{:S(2)}, u32[]{:S(2)}) async-start(bf16[4,12,32,128]{3,2,1,0:T(8,128)(2,1)} %broadcast_in_dim.15), calls=%async_computation.1 | async-start | bytes 786432 | tf_op jit(solution)/shard_map/all_to_all | solution.py:130
  35.6 2.1 %collective-permute-start.3 = (bf16[2,144,128]{2,1,0:T(8,128)(2,1)S(1)}, bf16[2,144,128]{2,1,0:T(8,128)(2,1)S(1)}, u32[]{:S(2)}, u32[]{:S(2)}) collective-permute-start(bf16[2,144,128]{2,1,0:T(8,128)(2,1)S(1)} %maximum_bitcast_fusion.own), channel_id=1, source_target_pairs={{0,2},{1,3},{2,0},{3,1},{4,6},{5,7},{6,4},{7,5},{8,10},{9,11},{10,... | collective-permute-start | bytes 221192 | tf_op jit(solution)/shard_map/ppermute | solution.py:103
  37.7 0.1 pad_add_fusion.1.place
  37.8 2.9 %collective-permute-done.3.one = bf16[2,144,128]{2,1,0:T(8,128)(2,1)S(1)} collective-permute-done((bf16[2,144,128]{2,1,0:T(8,128)(2,1)S(1)}, bf16[2,144,128]{2,1,0:T(8,128)(2,1)S(1)}, u32[]{:S(2)}, u32[]{:S(2)}) %collective-permute-start.3) | collective-permute-done | bytes 73760 | tf_op jit(solution)/shard_map/ppermute | solution.py:103
  40.7 1.1 %all-to-all-done.1 = bf16[4,12,32,128]{3,2,1,0:T(8,128)(2,1)S(1)} async-done(((bf16[4,12,32,128]{3,2,1,0:T(8,128)(2,1)}), bf16[4,12,32,128]{3,2,1,0:T(8,128)(2,1)S(1)}, u32[]{:S(2)}, u32[]{:S(2)}) %all-to-all-start.1) | async-done | bytes 393248 | tf_op jit(solution)/shard_map/all_to_all | solution.py:130
  41.8 5.4 %collective-permute-start.5 = (bf16[48,32,128]{2,1,0:T(8,128)(2,1)S(1)}, bf16[48,32,128]{2,1,0:T(8,128)(2,1)S(1)}, u32[]{:S(2)}, u32[]{:S(2)}) collective-permute-start(bf16[48,32,128]{2,1,0:T(8,128)(2,1)S(1)} %bitcast.35), channel_id=1, source_target_pairs={{0,8},{8,0},{1,9},{9,1},{2,10},{10,2},{3,11},{11,3},{4,12},{12,4},... | collective-permute-start | bytes 1179656 | tf_op jit(solution)/shard_map/ppermute | solution.py:141
  47.2 0.1 maximum_select_fusion
  47.3 0.7 %collective-permute-start.4 = (bf16[4,2,4,4,128]{4,3,2,1,0:T(4,128)(2,1)S(1)}, bf16[4,2,4,4,128]{4,3,2,1,0:T(4,128)(2,1)S(1)}, u32[]{:S(2)}, u32[]{:S(2)}) collective-permute-start(bf16[4,2,4,4,128]{4,3,2,1,0:T(4,128)(2,1)S(1)} %maximum_select_fusion), channel_id=1, source_target_pairs={{352,359},{353,358},{354,357},{355,356},{356,355},{357,354},{358,3... | collective-permute-start | bytes 98312 | tf_op jit(solution)/shard_map/ppermute | solution.py:103
  48.0 0.0 collective-permute-done.4
  48.0 0.5 collective-permute-done.5.other
  48.5 2.8 %shard_map.64 = f32[2,128,1024]{2,1,0:T(8,128)} custom-call(s32[4]{0:T(128)S(1)} %pad_add_fusion.1.place, s32[2,56]{1,0:T(2,128)S(1)} %constant_dynamic-slice_fusion.1.numbers, f32[2,9]{1,0:T(2,128)S(1)} %constant_dynamic-slice_fusion.weights, bf16[2,144,128]{2,1,0:T(8,128)(2,1)S(1)} %maximum_bitcast_fusion.own, ...), custom_call_target="tpu_custom_call" | custom-call | tf_op jit(solution)/shard_map/pallas_call | solution.py:144
  (16 shorter events, 0.2 us)
Async XLA Ops:
  0.0 48.0 %copy-start = (f32[8,9]{1,0:T(8,128)S(1)}, f32[8,9]{1,0:T(8,128)}, u32[]{:S(2)}) copy-start(f32[8,9]{1,0:T(8,128)} %param.9) | copy-start | bytes 868
  0.0 0.9 %copy-start.2 = (bf16[4,32,256]{2,1,0:T(8,128)(2,1)S(1)}, bf16[4,32,256]{2,1,0:T(8,128)(2,1)}, u32[]{:S(2)}) copy-start(bf16[4,32,256]{2,1,0:T(8,128)(2,1)} %param.6) | copy-start | bytes 196612
  1.6 17.9 %collective-permute-start = (bf16[4,4,256]{2,1,0:T(4,128)(2,1)S(1)}, bf16[4,4,256]{2,1,0:T(4,128)(2,1)S(1)}, u32[]{:S(2)}, u32[]{:S(2)}) collective-permute-start(bf16[4,4,256]{2,1,0:T(4,128)(2,1)S(1)} %constant_dynamic-slice_fusion.2), channel_id=1, source_target_pairs={{0,7},{1,6},{2,5},{3,4},{4,3},{5,2},{6,1},{7,0},{8,15},{9,14},{10,... | collective-permute-start | bytes 24584 | tf_op jit(solution)/shard_map/ppermute | solution.py:103
  7.5 23.8 %all-to-all-start = ((bf16[12,32,128]{2,1,0:T(8,128)(2,1)}), bf16[12,32,128]{2,1,0:T(8,128)(2,1)S(1)}, u32[]{:S(2)}, u32[]{:S(2)}) async-start(bf16[12,32,128]{2,1,0:T(8,128)(2,1)} %broadcast_in_dim.14), calls=%async_computation | async-start | bytes 196608 | tf_op jit(solution)/shard_map/all_to_all | solution.py:124
  19.4 7.3 %copy-start.3 = (s32[8,16,3]{1,0,2:T(8,128)S(1)}, s32[8,16,3]{1,0,2:T(8,128)}, u32[]{:S(2)}) copy-start(s32[8,16,3]{1,0,2:T(8,128)} %param.11) | copy-start | bytes 4612
  19.4 7.4 %copy-start.4 = (s32[8,8]{1,0:T(8,128)S(1)}, s32[8,8]{1,0:T(8,128)}, u32[]{:S(2)}) copy-start(s32[8,8]{1,0:T(8,128)} %param.10) | copy-start | bytes 772
  19.4 29.1 %copy-start.1 = (f32[2,4,32,1024]{3,2,1,0:T(8,128)S(1)}, f32[2,4,32,1024]{3,2,1,0:T(8,128)}, u32[]{:S(2)}) copy-start(f32[2,4,32,1024]{3,2,1,0:T(8,128)} %param.7) | copy-start | bytes 3145732
  19.5 7.4 %collective-permute-start.2 = (bf16[2,144,128]{2,1,0:T(8,128)(2,1)S(1)}, bf16[2,144,128]{2,1,0:T(8,128)(2,1)S(1)}, u32[]{:S(2)}, u32[]{:S(2)}) collective-permute-start(bf16[2,144,128]{2,1,0:T(8,128)(2,1)S(1)} %maximum_bitcast_fusion.own), channel_id=1, source_target_pairs={{0,6},{1,7},{2,4},{3,5},{4,2},{5,3},{6,0},{7,1},{8,14},{9,15},{10,... | collective-permute-start | bytes 221192 | tf_op jit(solution)/shard_map/ppermute | solution.py:103
  24.2 7.1 %collective-permute-start.1 = (bf16[2,144,128]{2,1,0:T(8,128)(2,1)S(1)}, bf16[2,144,128]{2,1,0:T(8,128)(2,1)S(1)}, u32[]{:S(2)}, u32[]{:S(2)}) collective-permute-start(bf16[2,144,128]{2,1,0:T(8,128)(2,1)S(1)} %maximum_bitcast_fusion.own), channel_id=1, source_target_pairs={{0,4},{1,5},{2,6},{3,7},{4,0},{5,1},{6,2},{7,3},{8,12},{9,13},{10,... | collective-permute-start | bytes 221192 | tf_op jit(solution)/shard_map/ppermute | solution.py:103
  32.1 9.7 %all-to-all-start.1 = ((bf16[4,12,32,128]{3,2,1,0:T(8,128)(2,1)}), bf16[4,12,32,128]{3,2,1,0:T(8,128)(2,1)S(1)}, u32[]{:S(2)}, u32[]{:S(2)}) async-start(bf16[4,12,32,128]{3,2,1,0:T(8,128)(2,1)} %broadcast_in_dim.15), calls=%async_computation.1 | async-start | bytes 786432 | tf_op jit(solution)/shard_map/all_to_all | solution.py:130
  35.6 5.1 %collective-permute-start.3 = (bf16[2,144,128]{2,1,0:T(8,128)(2,1)S(1)}, bf16[2,144,128]{2,1,0:T(8,128)(2,1)S(1)}, u32[]{:S(2)}, u32[]{:S(2)}) collective-permute-start(bf16[2,144,128]{2,1,0:T(8,128)(2,1)S(1)} %maximum_bitcast_fusion.own), channel_id=1, source_target_pairs={{0,2},{1,3},{2,0},{3,1},{4,6},{5,7},{6,4},{7,5},{8,10},{9,11},{10,... | collective-permute-start | bytes 221192 | tf_op jit(solution)/shard_map/ppermute | solution.py:103
  41.8 6.8 %collective-permute-start.5 = (bf16[48,32,128]{2,1,0:T(8,128)(2,1)S(1)}, bf16[48,32,128]{2,1,0:T(8,128)(2,1)S(1)}, u32[]{:S(2)}, u32[]{:S(2)}) collective-permute-start(bf16[48,32,128]{2,1,0:T(8,128)(2,1)S(1)} %bitcast.35), channel_id=1, source_target_pairs={{0,8},{8,0},{1,9},{9,1},{2,10},{10,2},{3,11},{11,3},{4,12},{12,4},... | collective-permute-start | bytes 1179656 | tf_op jit(solution)/shard_map/ppermute | solution.py:141
  47.3 0.7 %collective-permute-start.4 = (bf16[4,2,4,4,128]{4,3,2,1,0:T(4,128)(2,1)S(1)}, bf16[4,2,4,4,128]{4,3,2,1,0:T(4,128)(2,1)S(1)}, u32[]{:S(2)}, u32[]{:S(2)}) collective-permute-start(bf16[4,2,4,4,128]{4,3,2,1,0:T(4,128)(2,1)S(1)} %maximum_select_fusion), channel_id=1, source_target_pairs={{352,359},{353,358},{354,357},{355,356},{356,355},{357,354},{358,3... | collective-permute-start | bytes 98312 | tf_op jit(solution)/shard_map/ppermute | solution.py:103

commit v13 on v10

--- a/solution.py
+++ b/solution.py
@@ -21,7 +21,7 @@
     view, side, core = place[0], place[1], place[2]
     for k, part in enumerate((own, one, two, three)):
         seen[view ^ k, :, :OWN] = part[:, :OWN]
-        seen[view ^ k ^ 3, :, OWN:] = jnp.where(place[3] == 1, part[:, OWN:], edge[k])
+        seen[view ^ k ^ 2, :, OWN:] = jnp.where(place[3] == 1, part[:, OWN:], edge[k])
 
     def build(w):
         dense[w] = jnp.zeros_like(dense[w])
@@ -103,8 +103,8 @@
     return lax.ppermute(array, AXES, pairs)
 
 
-def mirror(v, gy):
-    return 3 - v, 1 - gy
+def beyond(v, gy):
+    return v ^ 2, 1 - gy
 
 
 def shards(estimate, observed, psf_blocks, kernel_y, block_source, psf_columns):
@@ -116,7 +116,7 @@
     begin = jnp.where(side == 0, ROWS - HALO, 0)
     ahead = lax.dynamic_slice_in_dim(estimate, begin, HALO, 1)
     ahead, spread, estimate = lax.optimization_barrier((ahead, spread, estimate))
-    ahead = permute(ahead, mirror, early)
+    ahead = permute(ahead, beyond, early)
     ahead, block_source, psf_columns = lax.optimization_barrier((ahead, block_source, psf_columns))
     first = 2 * lax.axis_index("view")
     numbers = jnp.concatenate([block_source, psf_columns.reshape(8, 48)], axis=1)
@@ -134,7 +134,7 @@
     upper = jnp.stack([part[:, 0:16:4, :HALO] for part in rows])
     lower = jnp.stack([part[:, 3:16:4, HALO:] for part in rows])
     rows = jnp.where(side == 0, lower, upper)
-    edge = permute(rows, mirror, lambda z: not early(z)).reshape(4, 2, EDGE, 128)
+    edge = permute(rows, beyond, lambda z: not early(z)).reshape(4, 2, EDGE, 128)
     mine = mine.reshape(48, 32, 128)
     kernel_y, _ = lax.optimization_barrier((kernel_y, mine))
     weights = lax.dynamic_slice_in_dim(kernel_y, first, 2, 0)

time: 51.8 us -> 52 us (level)
  the two profiles are of different devices: /device:TPU:321 before, /device:TPU:320 now
where the time goes in v13:
time: 52 us; the launch traced here: 51.5 us
  starting transfers between devices  31.4 us (60%)
  waiting for transfers between devices  14.3 us (28%)
  Pallas kernels  2.76 us (5%)
  local copies, waits for them, and re-layouts  2.68 us (5%)
    ppermute x5, starting transfers between devices, permute(): return lax.ppermute(array, AXES, pairs)  13.4 us
    ppermute x5, waiting for transfers between devices, permute(): return lax.ppermute(array, AXES, pairs)  13.2 us
    all_to_all x1, starting transfers between devices, shards(): along = lax.all_to_all(spread, 'z', 0, 0, tiled=True)  11.8 us
    all_to_all x1, starting transfers between devices, shards(): lax.all_to_all(jnp.broadcast_to(along[None], (4, 12, 32, 128)), 'x', 0, 0...  4.29 us
    pallas_call x1, Pallas kernels, shards(): pl.pallas_call(fused, out_shape=jax.ShapeDtypeStruct((2, OWN, 1024), jnp....  2.76 us
    ppermute x1, starting transfers between devices, shards(): other = lax.ppermute(mine, 'core', [(0, 1), (1, 0)])  1.91 us
    all_to_all x1, waiting for transfers between devices, shards(): lax.all_to_all(jnp.broadcast_to(along[None], (4, 12, 32, 128)), 'x', 0, 0...  1.15 us
  transfers between devices with their start and end apart: 8, of which 5 were waited for; matrix products, arithmetic and copies ran while one was open for 1% of the time, Pallas kernels for 0%

profile of v13, /device:TPU:320, one launch (start us, length us, event | category | flops | bytes accessed | tf_op | source)
XLA Modules:
  0.0 51.5 jit_solution(7115269761629361527)
XLA Ops:
  0.0 0.0 copy-start
  0.0 0.8 %reshape.39 = bf16[2,32,64]{2,1,0:T(8,128)(2,1)S(1)} reshape(bf16[2,2048]{1,0:T(2,128)(2,1)} %param.8) | data formatting | bytes 16384 | tf_op jit(solution)/shard_map/reshape | solution.py:114
  0.8 0.1 broadcast_in_dim.6
  0.9 0.0 copy-done.2
  0.9 0.7 %broadcast_in_dim.14 = bf16[12,32,128]{2,1,0:T(8,128)(2,1)} broadcast(bf16[32,128]{1,0:T(8,128)(2,1)S(1)} %broadcast_in_dim.6), dimensions={1,2} | broadcast | bytes 106496 | tf_op jit(solution)/shard_map/broadcast_in_dim | solution.py:115
  1.6 0.6 %collective-permute-start = (bf16[4,4,256]{2,1,0:T(4,128)(2,1)S(1)}, bf16[4,4,256]{2,1,0:T(4,128)(2,1)S(1)}, u32[]{:S(2)}, u32[]{:S(2)}) collective-permute-start(bf16[4,4,256]{2,1,0:T(4,128)(2,1)S(1)} %constant_dynamic-slice_fusion.2), channel_id=1, source_target_pairs={{0,5},{1,4},{2,7},{3,6},{4,1},{5,0},{6,3},{7,2},{8,13},{9,12},{10,... | collective-permute-start | bytes 24584 | tf_op jit(solution)/shard_map/ppermute | solution.py:103
  2.3 11.8 %all-to-all-start = ((bf16[12,32,128]{2,1,0:T(8,128)(2,1)}), bf16[12,32,128]{2,1,0:T(8,128)(2,1)S(1)}, u32[]{:S(2)}, u32[]{:S(2)}) async-start(bf16[12,32,128]{2,1,0:T(8,128)(2,1)} %broadcast_in_dim.14), calls=%async_computation | async-start | bytes 196608 | tf_op jit(solution)/shard_map/all_to_all | solution.py:124
  14.1 0.0 copy-start.1
  14.1 0.0 collective-permute-done
  14.2 5.0 %collective-permute-start.2 = (bf16[2,144,128]{2,1,0:T(8,128)(2,1)S(1)}, bf16[2,144,128]{2,1,0:T(8,128)(2,1)S(1)}, u32[]{:S(2)}, u32[]{:S(2)}) collective-permute-start(bf16[2,144,128]{2,1,0:T(8,128)(2,1)S(1)} %maximum_bitcast_fusion.own), channel_id=1, source_target_pairs={{0,6},{1,7},{2,4},{3,5},{4,2},{5,3},{6,0},{7,1},{8,14},{9,15},{10,... | collective-permute-start | bytes 221192 | tf_op jit(solution)/shard_map/ppermute | solution.py:103
  19.2 1.9 %collective-permute-start.1 = (bf16[2,144,128]{2,1,0:T(8,128)(2,1)S(1)}, bf16[2,144,128]{2,1,0:T(8,128)(2,1)S(1)}, u32[]{:S(2)}, u32[]{:S(2)}) collective-permute-start(bf16[2,144,128]{2,1,0:T(8,128)(2,1)S(1)} %maximum_bitcast_fusion.own), channel_id=1, source_target_pairs={{0,4},{1,5},{2,6},{3,7},{4,0},{5,1},{6,2},{7,3},{8,12},{9,13},{10,... | collective-permute-start | bytes 221192 | tf_op jit(solution)/shard_map/ppermute | solution.py:103
  21.1 0.0 copy-done.3
  21.1 0.1 copy.11
  21.2 0.1 copy.12
  21.3 0.0 copy-done.4
  21.3 0.1 pad_add_fusion
  21.4 1.0 %collective-permute-done.2.three = bf16[2,144,128]{2,1,0:T(8,128)(2,1)S(1)} collective-permute-done((bf16[2,144,128]{2,1,0:T(8,128)(2,1)S(1)}, bf16[2,144,128]{2,1,0:T(8,128)(2,1)S(1)}, u32[]{:S(2)}, u32[]{:S(2)}) %collective-permute-start.2) | collective-permute-done | bytes 73760 | tf_op jit(solution)/shard_map/ppermute | solution.py:103
  22.4 4.0 %collective-permute-done.1.two = bf16[2,144,128]{2,1,0:T(8,128)(2,1)S(1)} collective-permute-done((bf16[2,144,128]{2,1,0:T(8,128)(2,1)S(1)}, bf16[2,144,128]{2,1,0:T(8,128)(2,1)S(1)}, u32[]{:S(2)}, u32[]{:S(2)}) %collective-permute-start.1) | collective-permute-done | bytes 73760 | tf_op jit(solution)/shard_map/ppermute | solution.py:103
  26.3 0.0 all-to-all-done
  26.3 0.8 %broadcast_in_dim.15 = bf16[4,12,32,128]{3,2,1,0:T(8,128)(2,1)} broadcast(bf16[12,32,128]{2,1,0:T(8,128)(2,1)S(1)} %all-to-all-done), dimensions={1,2,3} | broadcast | bytes 491520 | tf_op jit(solution)/shard_map/broadcast_in_dim | solution.py:130
  27.1 4.3 %all-to-all-start.1 = ((bf16[4,12,32,128]{3,2,1,0:T(8,128)(2,1)}), bf16[4,12,32,128]{3,2,1,0:T(8,128)(2,1)S(1)}, u32[]{:S(2)}, u32[]{:S(2)}) async-start(bf16[4,12,32,128]{3,2,1,0:T(8,128)(2,1)} %broadcast_in_dim.15), calls=%async_computation.1 | async-start | bytes 786432 | tf_op jit(solution)/shard_map/all_to_all | solution.py:130
  31.4 1.9 %collective-permute-start.3 = (bf16[2,144,128]{2,1,0:T(8,128)(2,1)S(1)}, bf16[2,144,128]{2,1,0:T(8,128)(2,1)S(1)}, u32[]{:S(2)}, u32[]{:S(2)}) collective-permute-start(bf16[2,144,128]{2,1,0:T(8,128)(2,1)S(1)} %maximum_bitcast_fusion.own), channel_id=1, source_target_pairs={{0,2},{1,3},{2,0},{3,1},{4,6},{5,7},{6,4},{7,5},{8,10},{9,11},{10,... | collective-permute-start | bytes 221192 | tf_op jit(solution)/shard_map/ppermute | solution.py:103
  33.3 0.1 pad_add_fusion.1.place
  33.4 4.2 %collective-permute-done.3.one = bf16[2,144,128]{2,1,0:T(8,128)(2,1)S(1)} collective-permute-done((bf16[2,144,128]{2,1,0:T(8,128)(2,1)S(1)}, bf16[2,144,128]{2,1,0:T(8,128)(2,1)S(1)}, u32[]{:S(2)}, u32[]{:S(2)}) %collective-permute-start.3) | collective-permute-done | bytes 73760 | tf_op jit(solution)/shard_map/ppermute | solution.py:103
  37.7 1.1 %all-to-all-done.1 = bf16[4,12,32,128]{3,2,1,0:T(8,128)(2,1)S(1)} async-done(((bf16[4,12,32,128]{3,2,1,0:T(8,128)(2,1)}), bf16[4,12,32,128]{3,2,1,0:T(8,128)(2,1)S(1)}, u32[]{:S(2)}, u32[]{:S(2)}) %all-to-all-start.1) | async-done | bytes 393248 | tf_op jit(solution)/shard_map/all_to_all | solution.py:130
  38.8 1.9 %collective-permute-start.5 = (bf16[48,32,128]{2,1,0:T(8,128)(2,1)S(1)}, bf16[48,32,128]{2,1,0:T(8,128)(2,1)S(1)}, u32[]{:S(2)}, u32[]{:S(2)}) collective-permute-start(bf16[48,32,128]{2,1,0:T(8,128)(2,1)S(1)} %bitcast.35), channel_id=1, source_target_pairs={{0,8},{8,0},{1,9},{9,1},{2,10},{10,2},{3,11},{11,3},{4,12},{12,4},... | collective-permute-start | bytes 1179656 | tf_op jit(solution)/shard_map/ppermute | solution.py:141
  40.8 0.1 maximum_select_fusion
  40.8 3.9 %collective-permute-start.4 = (bf16[4,2,4,4,128]{4,3,2,1,0:T(4,128)(2,1)S(1)}, bf16[4,2,4,4,128]{4,3,2,1,0:T(4,128)(2,1)S(1)}, u32[]{:S(2)}, u32[]{:S(2)}) collective-permute-start(bf16[4,2,4,4,128]{4,3,2,1,0:T(4,128)(2,1)S(1)} %maximum_select_fusion), channel_id=1, source_target_pairs={{320,325},{321,324},{322,327},{323,326},{324,321},{325,320},{326,3... | collective-permute-start | bytes 98312 | tf_op jit(solution)/shard_map/ppermute | solution.py:103
  44.8 0.0 copy-done
  44.8 4.0 %collective-permute-done.4 = bf16[4,2,4,4,128]{4,3,2,1,0:T(4,128)(2,1)S(1)} collective-permute-done((bf16[4,2,4,4,128]{4,3,2,1,0:T(4,128)(2,1)S(1)}, bf16[4,2,4,4,128]{4,3,2,1,0:T(4,128)(2,1)S(1)}, u32[]{:S(2)}, u32[]{:S(2)}) %collective-permute-start.4) | collective-permute-done | bytes 32800 | tf_op jit(solution)/shard_map/ppermute | solution.py:103
  48.8 0.0 collective-permute-done.5.other
  48.8 2.8 %shard_map.64 = f32[2,128,1024]{2,1,0:T(8,128)} custom-call(s32[4]{0:T(128)S(1)} %pad_add_fusion.1.place, s32[2,56]{1,0:T(2,128)S(1)} %constant_dynamic-slice_fusion.1.numbers, f32[2,9]{1,0:T(2,128)S(1)} %constant_dynamic-slice_fusion.weights, bf16[2,144,128]{2,1,0:T(8,128)(2,1)S(1)} %maximum_bitcast_fusion.own, ...), custom_call_target="tpu_custom_call" | custom-call | tf_op jit(solution)/shard_map/pallas_call | solution.py:144
  (16 shorter events, 0.2 us)
Async XLA Ops:
  0.0 44.8 %copy-start = (f32[8,9]{1,0:T(8,128)S(1)}, f32[8,9]{1,0:T(8,128)}, u32[]{:S(2)}) copy-start(f32[8,9]{1,0:T(8,128)} %param.9) | copy-start | bytes 868
  0.0 0.9 %copy-start.2 = (bf16[4,32,256]{2,1,0:T(8,128)(2,1)S(1)}, bf16[4,32,256]{2,1,0:T(8,128)(2,1)}, u32[]{:S(2)}) copy-start(bf16[4,32,256]{2,1,0:T(8,128)(2,1)} %param.6) | copy-start | bytes 196612
  1.6 12.5 %collective-permute-start = (bf16[4,4,256]{2,1,0:T(4,128)(2,1)S(1)}, bf16[4,4,256]{2,1,0:T(4,128)(2,1)S(1)}, u32[]{:S(2)}, u32[]{:S(2)}) collective-permute-start(bf16[4,4,256]{2,1,0:T(4,128)(2,1)S(1)} %constant_dynamic-slice_fusion.2), channel_id=1, source_target_pairs={{0,5},{1,4},{2,7},{3,6},{4,1},{5,0},{6,3},{7,2},{8,13},{9,12},{10,... | collective-permute-start | bytes 24584 | tf_op jit(solution)/shard_map/ppermute | solution.py:103
  2.3 24.1 %all-to-all-start = ((bf16[12,32,128]{2,1,0:T(8,128)(2,1)}), bf16[12,32,128]{2,1,0:T(8,128)(2,1)S(1)}, u32[]{:S(2)}, u32[]{:S(2)}) async-start(bf16[12,32,128]{2,1,0:T(8,128)(2,1)} %broadcast_in_dim.14), calls=%async_computation | async-start | bytes 196608 | tf_op jit(solution)/shard_map/all_to_all | solution.py:124
  14.1 7.2 %copy-start.4 = (s32[8,8]{1,0:T(8,128)S(1)}, s32[8,8]{1,0:T(8,128)}, u32[]{:S(2)}) copy-start(s32[8,8]{1,0:T(8,128)} %param.10) | copy-start | bytes 772
  14.1 7.0 %copy-start.3 = (s32[8,16,3]{1,0,2:T(8,128)S(1)}, s32[8,16,3]{1,0,2:T(8,128)}, u32[]{:S(2)}) copy-start(s32[8,16,3]{1,0,2:T(8,128)} %param.11) | copy-start | bytes 4612
  14.1 34.7 %copy-start.1 = (f32[2,4,32,1024]{3,2,1,0:T(8,128)S(1)}, f32[2,4,32,1024]{3,2,1,0:T(8,128)}, u32[]{:S(2)}) copy-start(f32[2,4,32,1024]{3,2,1,0:T(8,128)} %param.7) | copy-start | bytes 3145732
  14.2 8.2 %collective-permute-start.2 = (bf16[2,144,128]{2,1,0:T(8,128)(2,1)S(1)}, bf16[2,144,128]{2,1,0:T(8,128)(2,1)S(1)}, u32[]{:S(2)}, u32[]{:S(2)}) collective-permute-start(bf16[2,144,128]{2,1,0:T(8,128)(2,1)S(1)} %maximum_bitcast_fusion.own), channel_id=1, source_target_pairs={{0,6},{1,7},{2,4},{3,5},{4,2},{5,3},{6,0},{7,1},{8,14},{9,15},{10,... | collective-permute-start | bytes 221192 | tf_op jit(solution)/shard_map/ppermute | solution.py:103
  19.2 7.1 %collective-permute-start.1 = (bf16[2,144,128]{2,1,0:T(8,128)(2,1)S(1)}, bf16[2,144,128]{2,1,0:T(8,128)(2,1)S(1)}, u32[]{:S(2)}, u32[]{:S(2)}) collective-permute-start(bf16[2,144,128]{2,1,0:T(8,128)(2,1)S(1)} %maximum_bitcast_fusion.own), channel_id=1, source_target_pairs={{0,4},{1,5},{2,6},{3,7},{4,0},{5,1},{6,2},{7,3},{8,12},{9,13},{10,... | collective-permute-start | bytes 221192 | tf_op jit(solution)/shard_map/ppermute | solution.py:103
  27.1 11.7 %all-to-all-start.1 = ((bf16[4,12,32,128]{3,2,1,0:T(8,128)(2,1)}), bf16[4,12,32,128]{3,2,1,0:T(8,128)(2,1)S(1)}, u32[]{:S(2)}, u32[]{:S(2)}) async-start(bf16[4,12,32,128]{3,2,1,0:T(8,128)(2,1)} %broadcast_in_dim.15), calls=%async_computation.1 | async-start | bytes 786432 | tf_op jit(solution)/shard_map/all_to_all | solution.py:130
  31.4 6.2 %collective-permute-start.3 = (bf16[2,144,128]{2,1,0:T(8,128)(2,1)S(1)}, bf16[2,144,128]{2,1,0:T(8,128)(2,1)S(1)}, u32[]{:S(2)}, u32[]{:S(2)}) collective-permute-start(bf16[2,144,128]{2,1,0:T(8,128)(2,1)S(1)} %maximum_bitcast_fusion.own), channel_id=1, source_target_pairs={{0,2},{1,3},{2,0},{3,1},{4,6},{5,7},{6,4},{7,5},{8,10},{9,11},{10,... | collective-permute-start | bytes 221192 | tf_op jit(solution)/shard_map/ppermute | solution.py:103
  38.8 9.9 %collective-permute-start.5 = (bf16[48,32,128]{2,1,0:T(8,128)(2,1)S(1)}, bf16[48,32,128]{2,1,0:T(8,128)(2,1)S(1)}, u32[]{:S(2)}, u32[]{:S(2)}) collective-permute-start(bf16[48,32,128]{2,1,0:T(8,128)(2,1)S(1)} %bitcast.35), channel_id=1, source_target_pairs={{0,8},{8,0},{1,9},{9,1},{2,10},{10,2},{3,11},{11,3},{4,12},{12,4},... | collective-permute-start | bytes 1179656 | tf_op jit(solution)/shard_map/ppermute | solution.py:141
  40.8 7.9 %collective-permute-start.4 = (bf16[4,2,4,4,128]{4,3,2,1,0:T(4,128)(2,1)S(1)}, bf16[4,2,4,4,128]{4,3,2,1,0:T(4,128)(2,1)S(1)}, u32[]{:S(2)}, u32[]{:S(2)}) collective-permute-start(bf16[4,2,4,4,128]{4,3,2,1,0:T(4,128)(2,1)S(1)} %maximum_select_fusion), channel_id=1, source_target_pairs={{320,325},{321,324},{322,327},{323,326},{324,321},{325,320},{326,3... | collective-permute-start | bytes 98312 | tf_op jit(solution)/shard_map/ppermute | solution.py:103

commit v14 on v10

--- a/solution.py
+++ b/solution.py
@@ -17,11 +17,12 @@
 SIZES = (12, 4, 2, 4, 2)
 
 
-def fused(place, numbers, weights, own, one, two, three, edge, mine, other, observed, ratio, dense, seen, done, sems):
+def fused(place, numbers, weights, own, one, late, two, three, edge, mine, other, observed, ratio, dense, seen, done, sems):
     view, side, core = place[0], place[1], place[2]
-    for k, part in enumerate((own, one, two, three)):
+    soon = place[3] == 1
+    for k, part in enumerate((own[...], jnp.where(soon, one[...], late[...]), two[...], three[...])):
         seen[view ^ k, :, :OWN] = part[:, :OWN]
-        seen[view ^ k ^ 3, :, OWN:] = jnp.where(place[3] == 1, part[:, OWN:], edge[k])
+        seen[view ^ k ^ 3, :, OWN:] = jnp.where(soon, part[:, OWN:], edge[k])
 
     def build(w):
         dense[w] = jnp.zeros_like(dense[w])
@@ -126,17 +127,17 @@
     slab = slab.transpose(1, 0, 2)
     two = permute(slab, lambda v, gy: (v ^ 2, gy))
     three = permute(slab, lambda v, gy: (v ^ 3, gy))
-    along, two, three, slab, numbers = lax.optimization_barrier((along, two, three, slab, numbers))
-    mine = lax.all_to_all(jnp.broadcast_to(along[None], (4, 12, 32, 128)), "x", 0, 0, tiled=True)
-    one = permute(slab, lambda v, gy: (v ^ 1, gy))
-    mine, slab, one, two, three = lax.optimization_barrier((mine, slab, one, two, three))
-    rows = [part.reshape(2, 18, 8, 128) for part in (slab, one, two, three)]
+    late = permute(slab, lambda v, gy: (v ^ 1, gy), lambda z: not early(z))
+    rows = [part.reshape(2, 18, 8, 128) for part in (slab, late, two, three)]
     upper = jnp.stack([part[:, 0:16:4, :HALO] for part in rows])
     lower = jnp.stack([part[:, 3:16:4, HALO:] for part in rows])
     rows = jnp.where(side == 0, lower, upper)
+    along, rows, slab, numbers = lax.optimization_barrier((along, rows, slab, numbers))
+    mine = lax.all_to_all(jnp.broadcast_to(along[None], (4, 12, 32, 128)), "x", 0, 0, tiled=True)
+    one = permute(slab, lambda v, gy: (v ^ 1, gy), early)
     edge = permute(rows, mirror, lambda z: not early(z)).reshape(4, 2, EDGE, 128)
+    mine, one, edge, kernel_y = lax.optimization_barrier((mine, one, edge, kernel_y))
     mine = mine.reshape(48, 32, 128)
-    kernel_y, _ = lax.optimization_barrier((kernel_y, mine))
     weights = lax.dynamic_slice_in_dim(kernel_y, first, 2, 0)
     other = lax.ppermute(mine, "core", [(0, 1), (1, 0)])
     smem = pl.BlockSpec(memory_space=pltpu.SMEM)
@@ -144,7 +145,7 @@
     ratio = pl.pallas_call(
         fused,
         out_shape=jax.ShapeDtypeStruct((2, OWN, 1024), jnp.float32),
-        in_specs=[smem] * 3 + [vmem] * 8,
+        in_specs=[smem] * 3 + [vmem] * 9,
         out_specs=pl.BlockSpec(memory_space=pl.ANY),
         scratch_shapes=[
             pltpu.VMEM((2, BLOCKS // 2, 512, 256), jnp.bfloat16),
@@ -159,6 +160,7 @@
         weights,
         slab,
         one,
+        late,
         two,
         three,
         edge,

time: 51.8 us -> 57.1 us (1.10)
  the two profiles are of different devices: /device:TPU:321 before, /device:TPU:1 now
where the time goes in v14:
time: 57.1 us; the launch traced here: 56.6 us
  starting transfers between devices  43.5 us (76%)
  waiting for transfers between devices  7.26 us (13%)
  Pallas kernels  2.78 us (5%)
  local copies, waits for them, and re-layouts  2.69 us (5%)
    ppermute x6, starting transfers between devices, permute(): return lax.ppermute(array, AXES, pairs)  16.8 us
    all_to_all x1, starting transfers between devices, shards(): along = lax.all_to_all(spread, 'z', 0, 0, tiled=True)  15.8 us
    ppermute x1, starting transfers between devices, shards(): other = lax.ppermute(mine, 'core', [(0, 1), (1, 0)])  6.8 us
    ppermute x6, waiting for transfers between devices, permute(): return lax.ppermute(array, AXES, pairs)  4.88 us
    all_to_all x1, starting transfers between devices, shards(): lax.all_to_all(jnp.broadcast_to(along[None], (4, 12, 32, 128)), 'x', 0, 0...  4.01 us
    pallas_call x1, Pallas kernels, shards(): pl.pallas_call(fused, out_shape=jax.ShapeDtypeStruct((2, OWN, 1024), jnp....  2.78 us
    ppermute x1, waiting for transfers between devices, shards(): other = lax.ppermute(mine, 'core', [(0, 1), (1, 0)])  1.23 us
    all_to_all x1, waiting for transfers between devices, shards(): lax.all_to_all(jnp.broadcast_to(along[None], (4, 12, 32, 128)), 'x', 0, 0...  1.15 us
  transfers between devices with their start and end apart: 9, of which 5 were waited for; matrix products, arithmetic and copies ran while one was open for 1% of the time, Pallas kernels for 0%

profile of v14, /device:TPU:1, one launch (start us, length us, event | category | flops | bytes accessed | tf_op | source)
XLA Modules:
  0.0 56.6 jit_solution(8438250562435524911)
XLA Ops:
  0.0 0.0 copy-start
  0.0 0.8 %reshape.39 = bf16[2,32,64]{2,1,0:T(8,128)(2,1)S(1)} reshape(bf16[2,2048]{1,0:T(2,128)(2,1)} %param.8) | data formatting | bytes 16384 | tf_op jit(solution)/shard_map/reshape | solution.py:115
  0.8 0.1 broadcast_in_dim.6
  0.9 0.0 copy-done.2
  0.9 0.7 %broadcast_in_dim.14 = bf16[12,32,128]{2,1,0:T(8,128)(2,1)} broadcast(bf16[32,128]{1,0:T(8,128)(2,1)S(1)} %broadcast_in_dim.6), dimensions={1,2} | broadcast | bytes 106496 | tf_op jit(solution)/shard_map/broadcast_in_dim | solution.py:116
  1.6 15.8 %all-to-all-start = ((bf16[12,32,128]{2,1,0:T(8,128)(2,1)}), bf16[12,32,128]{2,1,0:T(8,128)(2,1)S(1)}, u32[]{:S(2)}, u32[]{:S(2)}) async-start(bf16[12,32,128]{2,1,0:T(8,128)(2,1)} %broadcast_in_dim.14), calls=%async_computation | async-start | bytes 196608 | tf_op jit(solution)/shard_map/all_to_all | solution.py:125
  17.4 0.0 copy-start.1
  17.5 5.2 %collective-permute-start = (bf16[4,4,256]{2,1,0:T(4,128)(2,1)S(1)}, bf16[4,4,256]{2,1,0:T(4,128)(2,1)S(1)}, u32[]{:S(2)}, u32[]{:S(2)}) collective-permute-start(bf16[4,4,256]{2,1,0:T(4,128)(2,1)S(1)} %constant_dynamic-slice_fusion.2), channel_id=1, source_target_pairs={{0,7},{1,6},{2,5},{3,4},{4,3},{5,2},{6,1},{7,0},{8,15},{9,14},{10,... | collective-permute-start | bytes 24584 | tf_op jit(solution)/shard_map/ppermute | solution.py:104
  22.7 1.3 %collective-permute-done = bf16[4,4,256]{2,1,0:T(4,128)(2,1)S(1)} collective-permute-done((bf16[4,4,256]{2,1,0:T(4,128)(2,1)S(1)}, bf16[4,4,256]{2,1,0:T(4,128)(2,1)S(1)}, u32[]{:S(2)}, u32[]{:S(2)}) %collective-permute-start) | collective-permute-done | bytes 8224 | tf_op jit(solution)/shard_map/ppermute | solution.py:104
  24.0 4.4 %collective-permute-start.3 = (bf16[2,144,128]{2,1,0:T(8,128)(2,1)S(1)}, bf16[2,144,128]{2,1,0:T(8,128)(2,1)S(1)}, u32[]{:S(2)}, u32[]{:S(2)}) collective-permute-start(bf16[2,144,128]{2,1,0:T(8,128)(2,1)S(1)} %bitcast.38), channel_id=1, source_target_pairs={{0,6},{1,7},{2,4},{3,5},{4,2},{5,3},{6,0},{7,1},{8,14},{9,15},{10,... | collective-permute-start | bytes 221192 | tf_op jit(solution)/shard_map/ppermute | solution.py:104
  28.5 2.9 %collective-permute-start.2 = (bf16[2,144,128]{2,1,0:T(8,128)(2,1)S(1)}, bf16[2,144,128]{2,1,0:T(8,128)(2,1)S(1)}, u32[]{:S(2)}, u32[]{:S(2)}) collective-permute-start(bf16[2,144,128]{2,1,0:T(8,128)(2,1)S(1)} %bitcast.39), channel_id=1, source_target_pairs={{0,4},{1,5},{2,6},{3,7},{4,0},{5,1},{6,2},{7,3},{8,12},{9,13},{10,... | collective-permute-start | bytes 221192 | tf_op jit(solution)/shard_map/ppermute | solution.py:104
  31.4 0.7 %collective-permute-start.1 = (bf16[2,144,128]{2,1,0:T(8,128)(2,1)S(1)}, bf16[2,144,128]{2,1,0:T(8,128)(2,1)S(1)}, u32[]{:S(2)}, u32[]{:S(2)}) collective-permute-start(bf16[2,144,128]{2,1,0:T(8,128)(2,1)S(1)} %bitcast.40), channel_id=1, source_target_pairs={{320,322},{321,323},{322,320},{323,321},{324,326},{325,327},{326,3... | collective-permute-start | bytes 221192 | tf_op jit(solution)/shard_map/ppermute | solution.py:104
  32.0 0.1 copy.11
  32.1 0.1 copy.12
  32.2 0.0 copy-done.4
  32.2 0.1 pad_add_fusion
  32.3 0.0 collective-permute-done.3.three
  32.3 2.2 %collective-permute-done.2.two = bf16[2,144,128]{2,1,0:T(8,128)(2,1)S(1)} collective-permute-done((bf16[2,144,128]{2,1,0:T(8,128)(2,1)S(1)}, bf16[2,144,128]{2,1,0:T(8,128)(2,1)S(1)}, u32[]{:S(2)}, u32[]{:S(2)}) %collective-permute-start.2) | collective-permute-done | bytes 73760 | tf_op jit(solution)/shard_map/ppermute | solution.py:104
  34.5 0.0 collective-permute-done.1.late
  34.6 0.1 maximum_select_fusion
  34.6 0.0 all-to-all-done
  34.6 0.8 %broadcast_in_dim.15 = bf16[4,12,32,128]{3,2,1,0:T(8,128)(2,1)} broadcast(bf16[12,32,128]{2,1,0:T(8,128)(2,1)S(1)} %all-to-all-done), dimensions={1,2,3} | broadcast | bytes 491520 | tf_op jit(solution)/shard_map/broadcast_in_dim | solution.py:136
  35.4 4.0 %all-to-all-start.1 = ((bf16[4,12,32,128]{3,2,1,0:T(8,128)(2,1)}), bf16[4,12,32,128]{3,2,1,0:T(8,128)(2,1)S(1)}, u32[]{:S(2)}, u32[]{:S(2)}) async-start(bf16[4,12,32,128]{3,2,1,0:T(8,128)(2,1)} %broadcast_in_dim.15), calls=%async_computation.1 | async-start | bytes 786432 | tf_op jit(solution)/shard_map/all_to_all | solution.py:136
  39.4 3.0 %collective-permute-start.4 = (bf16[2,144,128]{2,1,0:T(8,128)(2,1)S(1)}, bf16[2,144,128]{2,1,0:T(8,128)(2,1)S(1)}, u32[]{:S(2)}, u32[]{:S(2)}) collective-permute-start(bf16[2,144,128]{2,1,0:T(8,128)(2,1)S(1)} %bitcast.42), channel_id=1, source_target_pairs={{0,2},{1,3},{2,0},{3,1},{4,6},{5,7},{6,4},{7,5},{8,10},{9,11},{10,... | collective-permute-start | bytes 221192 | tf_op jit(solution)/shard_map/ppermute | solution.py:104
  42.4 0.7 %collective-permute-start.5 = (bf16[4,2,4,4,128]{4,3,2,1,0:T(4,128)(2,1)S(1)}, bf16[4,2,4,4,128]{4,3,2,1,0:T(4,128)(2,1)S(1)}, u32[]{:S(2)}, u32[]{:S(2)}) collective-permute-start(bf16[4,2,4,4,128]{4,3,2,1,0:T(4,128)(2,1)S(1)} %maximum_select_fusion), channel_id=1, source_target_pairs={{320,327},{321,326},{322,325},{323,324},{324,323},{325,322},{326,3... | collective-permute-start | bytes 98312 | tf_op jit(solution)/shard_map/ppermute | solution.py:104
  43.1 0.0 collective-permute-done.5
  43.1 1.4 %collective-permute-done.4.one = bf16[2,144,128]{2,1,0:T(8,128)(2,1)S(1)} collective-permute-done((bf16[2,144,128]{2,1,0:T(8,128)(2,1)S(1)}, bf16[2,144,128]{2,1,0:T(8,128)(2,1)S(1)}, u32[]{:S(2)}, u32[]{:S(2)}) %collective-permute-start.4) | collective-permute-done | bytes 73760 | tf_op jit(solution)/shard_map/ppermute | solution.py:104
  44.5 1.1 %all-to-all-done.1 = bf16[4,12,32,128]{3,2,1,0:T(8,128)(2,1)S(1)} async-done(((bf16[4,12,32,128]{3,2,1,0:T(8,128)(2,1)}), bf16[4,12,32,128]{3,2,1,0:T(8,128)(2,1)S(1)}, u32[]{:S(2)}, u32[]{:S(2)}) %all-to-all-start.1) | async-done | bytes 393248 | tf_op jit(solution)/shard_map/all_to_all | solution.py:136
  45.7 6.8 %collective-permute-start.6 = (bf16[48,32,128]{2,1,0:T(8,128)(2,1)S(1)}, bf16[48,32,128]{2,1,0:T(8,128)(2,1)S(1)}, u32[]{:S(2)}, u32[]{:S(2)}) collective-permute-start(bf16[48,32,128]{2,1,0:T(8,128)(2,1)S(1)} %bitcast.35), channel_id=1, source_target_pairs={{0,8},{8,0},{1,9},{9,1},{2,10},{10,2},{3,11},{11,3},{4,12},{12,4},... | collective-permute-start | bytes 1179656 | tf_op jit(solution)/shard_map/ppermute | solution.py:142
  52.5 0.1 pad_add_fusion.1.place
  52.6 1.2 %collective-permute-done.6.other = bf16[48,32,128]{2,1,0:T(8,128)(2,1)S(1)} collective-permute-done((bf16[48,32,128]{2,1,0:T(8,128)(2,1)S(1)}, bf16[48,32,128]{2,1,0:T(8,128)(2,1)S(1)}, u32[]{:S(2)}, u32[]{:S(2)}) %collective-permute-start.6) | collective-permute-done | bytes 393248 | tf_op jit(solution)/shard_map/ppermute | solution.py:142
  53.8 2.8 %shard_map.64 = f32[2,128,1024]{2,1,0:T(8,128)} custom-call(s32[4]{0:T(128)S(1)} %pad_add_fusion.1.place, s32[2,56]{1,0:T(2,128)S(1)} %constant_dynamic-slice_fusion.1.numbers, f32[2,9]{1,0:T(2,128)S(1)} %constant_dynamic-slice_fusion.weights, bf16[2,144,128]{2,1,0:T(8,128)(2,1)S(1)} %bitcast.43, bf16[2,144,128]{2,1,0:T(8,128)(2,1)S(1)} %collective-permute-done.4.one, ...), custom_call_target="tpu_custom_call" | custom-call | tf_op jit(solution)/shard_map/pallas_call | solution.py:145
  (19 shorter events, 0.2 us)
Async XLA Ops:
  0.0 52.6 %copy-start = (f32[8,9]{1,0:T(8,128)S(1)}, f32[8,9]{1,0:T(8,128)}, u32[]{:S(2)}) copy-start(f32[8,9]{1,0:T(8,128)} %param.9) | copy-start | bytes 868
  0.0 0.9 %copy-start.2 = (bf16[4,32,256]{2,1,0:T(8,128)(2,1)S(1)}, bf16[4,32,256]{2,1,0:T(8,128)(2,1)}, u32[]{:S(2)}) copy-start(bf16[4,32,256]{2,1,0:T(8,128)(2,1)} %param.6) | copy-start | bytes 196612
  1.6 30.4 %copy-start.3 = (s32[8,16,3]{1,0,2:T(8,128)S(1)}, s32[8,16,3]{1,0,2:T(8,128)}, u32[]{:S(2)}) copy-start(s32[8,16,3]{1,0,2:T(8,128)} %param.11) | copy-start | bytes 4612
  1.6 30.6 %copy-start.4 = (s32[8,8]{1,0:T(8,128)S(1)}, s32[8,8]{1,0:T(8,128)}, u32[]{:S(2)}) copy-start(s32[8,8]{1,0:T(8,128)} %param.10) | copy-start | bytes 772
  1.6 33.0 %all-to-all-start = ((bf16[12,32,128]{2,1,0:T(8,128)(2,1)}), bf16[12,32,128]{2,1,0:T(8,128)(2,1)S(1)}, u32[]{:S(2)}, u32[]{:S(2)}) async-start(bf16[12,32,128]{2,1,0:T(8,128)(2,1)} %broadcast_in_dim.14), calls=%async_computation | async-start | bytes 196608 | tf_op jit(solution)/shard_map/all_to_all | solution.py:125
  17.4 36.4 %copy-start.1 = (f32[2,4,32,1024]{3,2,1,0:T(8,128)S(1)}, f32[2,4,32,1024]{3,2,1,0:T(8,128)}, u32[]{:S(2)}) copy-start(f32[2,4,32,1024]{3,2,1,0:T(8,128)} %param.7) | copy-start | bytes 3145732
  17.5 6.6 %collective-permute-start = (bf16[4,4,256]{2,1,0:T(4,128)(2,1)S(1)}, bf16[4,4,256]{2,1,0:T(4,128)(2,1)S(1)}, u32[]{:S(2)}, u32[]{:S(2)}) collective-permute-start(bf16[4,4,256]{2,1,0:T(4,128)(2,1)S(1)} %constant_dynamic-slice_fusion.2), channel_id=1, source_target_pairs={{0,7},{1,6},{2,5},{3,4},{4,3},{5,2},{6,1},{7,0},{8,15},{9,14},{10,... | collective-permute-start | bytes 24584 | tf_op jit(solution)/shard_map/ppermute | solution.py:104
  24.0 8.3 %collective-permute-start.3 = (bf16[2,144,128]{2,1,0:T(8,128)(2,1)S(1)}, bf16[2,144,128]{2,1,0:T(8,128)(2,1)S(1)}, u32[]{:S(2)}, u32[]{:S(2)}) collective-permute-start(bf16[2,144,128]{2,1,0:T(8,128)(2,1)S(1)} %bitcast.38), channel_id=1, source_target_pairs={{0,6},{1,7},{2,4},{3,5},{4,2},{5,3},{6,0},{7,1},{8,14},{9,15},{10,... | collective-permute-start | bytes 221192 | tf_op jit(solution)/shard_map/ppermute | solution.py:104
  28.5 6.1 %collective-permute-start.2 = (bf16[2,144,128]{2,1,0:T(8,128)(2,1)S(1)}, bf16[2,144,128]{2,1,0:T(8,128)(2,1)S(1)}, u32[]{:S(2)}, u32[]{:S(2)}) collective-permute-start(bf16[2,144,128]{2,1,0:T(8,128)(2,1)S(1)} %bitcast.39), channel_id=1, source_target_pairs={{0,4},{1,5},{2,6},{3,7},{4,0},{5,1},{6,2},{7,3},{8,12},{9,13},{10,... | collective-permute-start | bytes 221192 | tf_op jit(solution)/shard_map/ppermute | solution.py:104
  31.4 3.2 %collective-permute-start.1 = (bf16[2,144,128]{2,1,0:T(8,128)(2,1)S(1)}, bf16[2,144,128]{2,1,0:T(8,128)(2,1)S(1)}, u32[]{:S(2)}, u32[]{:S(2)}) collective-permute-start(bf16[2,144,128]{2,1,0:T(8,128)(2,1)S(1)} %bitcast.40), channel_id=1, source_target_pairs={{320,322},{321,323},{322,320},{323,321},{324,326},{325,327},{326,3... | collective-permute-start | bytes 221192 | tf_op jit(solution)/shard_map/ppermute | solution.py:104
  35.4 10.2 %all-to-all-start.1 = ((bf16[4,12,32,128]{3,2,1,0:T(8,128)(2,1)}), bf16[4,12,32,128]{3,2,1,0:T(8,128)(2,1)S(1)}, u32[]{:S(2)}, u32[]{:S(2)}) async-start(bf16[4,12,32,128]{3,2,1,0:T(8,128)(2,1)} %broadcast_in_dim.15), calls=%async_computation.1 | async-start | bytes 786432 | tf_op jit(solution)/shard_map/all_to_all | solution.py:136
  39.4 5.1 %collective-permute-start.4 = (bf16[2,144,128]{2,1,0:T(8,128)(2,1)S(1)}, bf16[2,144,128]{2,1,0:T(8,128)(2,1)S(1)}, u32[]{:S(2)}, u32[]{:S(2)}) collective-permute-start(bf16[2,144,128]{2,1,0:T(8,128)(2,1)S(1)} %bitcast.42), channel_id=1, source_target_pairs={{0,2},{1,3},{2,0},{3,1},{4,6},{5,7},{6,4},{7,5},{8,10},{9,11},{10,... | collective-permute-start | bytes 221192 | tf_op jit(solution)/shard_map/ppermute | solution.py:104
  42.4 0.7 %collective-permute-start.5 = (bf16[4,2,4,4,128]{4,3,2,1,0:T(4,128)(2,1)S(1)}, bf16[4,2,4,4,128]{4,3,2,1,0:T(4,128)(2,1)S(1)}, u32[]{:S(2)}, u32[]{:S(2)}) collective-permute-start(bf16[4,2,4,4,128]{4,3,2,1,0:T(4,128)(2,1)S(1)} %maximum_select_fusion), channel_id=1, source_target_pairs={{320,327},{321,326},{322,325},{323,324},{324,323},{325,322},{326,3... | collective-permute-start | bytes 98312 | tf_op jit(solution)/shard_map/ppermute | solution.py:104
  45.7 8.1 %collective-permute-start.6 = (bf16[48,32,128]{2,1,0:T(8,128)(2,1)S(1)}, bf16[48,32,128]{2,1,0:T(8,128)(2,1)S(1)}, u32[]{:S(2)}, u32[]{:S(2)}) collective-permute-start(bf16[48,32,128]{2,1,0:T(8,128)(2,1)S(1)} %bitcast.35), channel_id=1, source_target_pairs={{0,8},{8,0},{1,9},{9,1},{2,10},{10,2},{3,11},{11,3},{4,12},{12,4},... | collective-permute-start | bytes 1179656 | tf_op jit(solution)/shard_map/ppermute | solution.py:142

commit v15 on v14

--- a/solution.py
+++ b/solution.py
@@ -124,7 +124,7 @@
     numbers = lax.dynamic_slice_in_dim(numbers, first, 2, 0)
     along = lax.all_to_all(spread, "z", 0, 0, tiled=True)
     slab = jnp.concatenate([estimate.reshape(OWN, 2, 128), ahead.reshape(EDGE, 2, 128)], axis=0)
-    slab = slab.transpose(1, 0, 2)
+    slab = lax.optimization_barrier(slab.transpose(1, 0, 2))
     two = permute(slab, lambda v, gy: (v ^ 2, gy))
     three = permute(slab, lambda v, gy: (v ^ 3, gy))
     late = permute(slab, lambda v, gy: (v ^ 1, gy), lambda z: not early(z))

time: 57.1 us -> 51 us (0.89)
  starting transfers between devices: 43.5 us -> 36.8 us
  waiting for transfers between devices: 7.26 us -> 7.88 us
    all_to_all x1, starting transfers between devices: 15.8 us -> 10.5 us  [shards(): along = lax.all_to_all(spread, 'z', 0, 0, tiled=True)]
    ppermute x1, starting transfers between devices: 6.8 us -> 5.52 us  [shards(): other = lax.ppermute(mine, 'core', [(0, 1), (1, 0)])]
    ppermute x6, waiting for transfers between devices: 4.88 us -> 5.5 us  [permute(): return lax.ppermute(array, AXES, pairs)]
  transfers between devices with their start and end apart: 9 -> 9, of which waited for: 5 -> 4; matrix products, arithmetic and copies ran while one was open for 1% -> 1% of each run, Pallas kernels for 0% -> 0%
where the time goes in v15:
time: 51 us; the launch traced here: 50.6 us
  starting transfers between devices  36.8 us (72%)
  waiting for transfers between devices  7.88 us (15%)
  Pallas kernels  2.78 us (5%)
  local copies, waits for them, and re-layouts  2.69 us (5%)
    ppermute x6, starting transfers between devices, permute(): return lax.ppermute(array, AXES, pairs)  16.8 us
    all_to_all x1, starting transfers between devices, shards(): along = lax.all_to_all(spread, 'z', 0, 0, tiled=True)  10.5 us
    ppermute x1, starting transfers between devices, shards(): other = lax.ppermute(mine, 'core', [(0, 1), (1, 0)])  5.52 us
    ppermute x6, waiting for transfers between devices, permute(): return lax.ppermute(array, AXES, pairs)  5.5 us
    all_to_all x1, starting transfers between devices, shards(): lax.all_to_all(jnp.broadcast_to(along[None], (4, 12, 32, 128)), 'x', 0, 0...  4.01 us
    pallas_call x1, Pallas kernels, shards(): pl.pallas_call(fused, out_shape=jax.ShapeDtypeStruct((2, OWN, 1024), jnp....  2.78 us
    ppermute x1, waiting for transfers between devices, shards(): other = lax.ppermute(mine, 'core', [(0, 1), (1, 0)])  1.23 us
    all_to_all x1, waiting for transfers between devices, shards(): lax.all_to_all(jnp.broadcast_to(along[None], (4, 12, 32, 128)), 'x', 0, 0...  1.15 us
  transfers between devices with their start and end apart: 9, of which 4 were waited for; matrix products, arithmetic and copies ran while one was open for 1% of the time, Pallas kernels for 0%

profile of v15, /device:TPU:1, one launch (start us, length us, event | category | flops | bytes accessed | tf_op | source)
XLA Modules:
  0.0 50.6 jit_solution(9740005456062588419)
XLA Ops:
  0.0 0.0 copy-start
  0.0 0.8 %reshape.39 = bf16[2,32,64]{2,1,0:T(8,128)(2,1)S(1)} reshape(bf16[2,2048]{1,0:T(2,128)(2,1)} %param.8) | data formatting | bytes 16384 | tf_op jit(solution)/shard_map/reshape | solution.py:115
  0.8 0.1 broadcast_in_dim.6
  0.9 0.7 %broadcast_in_dim.14 = bf16[12,32,128]{2,1,0:T(8,128)(2,1)} broadcast(bf16[32,128]{1,0:T(8,128)(2,1)S(1)} %broadcast_in_dim.6), dimensions={1,2} | broadcast | bytes 106496 | tf_op jit(solution)/shard_map/broadcast_in_dim | solution.py:116
  1.6 5.9 %collective-permute-start = (bf16[4,4,256]{2,1,0:T(4,128)(2,1)S(1)}, bf16[4,4,256]{2,1,0:T(4,128)(2,1)S(1)}, u32[]{:S(2)}, u32[]{:S(2)}) collective-permute-start(bf16[4,4,256]{2,1,0:T(4,128)(2,1)S(1)} %constant_dynamic-slice_fusion.2), channel_id=1, source_target_pairs={{0,7},{1,6},{2,5},{3,4},{4,3},{5,2},{6,1},{7,0},{8,15},{9,14},{10,... | collective-permute-start | bytes 24584 | tf_op jit(solution)/shard_map/ppermute | solution.py:104
  7.5 10.5 %all-to-all-start = ((bf16[12,32,128]{2,1,0:T(8,128)(2,1)}), bf16[12,32,128]{2,1,0:T(8,128)(2,1)S(1)}, u32[]{:S(2)}, u32[]{:S(2)}) async-start(bf16[12,32,128]{2,1,0:T(8,128)(2,1)} %broadcast_in_dim.14), calls=%async_computation | async-start | bytes 196608 | tf_op jit(solution)/shard_map/all_to_all | solution.py:125
  18.0 0.0 copy-start.4
  18.0 0.0 copy-start.3
  18.0 0.0 copy-start.1
  18.1 0.0 collective-permute-done
  18.1 5.4 %collective-permute-start.3 = (bf16[2,144,128]{2,1,0:T(8,128)(2,1)S(1)}, bf16[2,144,128]{2,1,0:T(8,128)(2,1)S(1)}, u32[]{:S(2)}, u32[]{:S(2)}) collective-permute-start(bf16[2,144,128]{2,1,0:T(8,128)(2,1)S(1)} %maximum_bitcast_fusion.own), channel_id=1, source_target_pairs={{0,6},{1,7},{2,4},{3,5},{4,2},{5,3},{6,0},{7,1},{8,14},{9,15},{10,... | collective-permute-start | bytes 221192 | tf_op jit(solution)/shard_map/ppermute | solution.py:104
  23.5 1.9 %collective-permute-start.2 = (bf16[2,144,128]{2,1,0:T(8,128)(2,1)S(1)}, bf16[2,144,128]{2,1,0:T(8,128)(2,1)S(1)}, u32[]{:S(2)}, u32[]{:S(2)}) collective-permute-start(bf16[2,144,128]{2,1,0:T(8,128)(2,1)S(1)} %maximum_bitcast_fusion.own), channel_id=1, source_target_pairs={{0,4},{1,5},{2,6},{3,7},{4,0},{5,1},{6,2},{7,3},{8,12},{9,13},{10,... | collective-permute-start | bytes 221192 | tf_op jit(solution)/shard_map/ppermute | solution.py:104
  25.4 0.7 %collective-permute-start.1 = (bf16[2,144,128]{2,1,0:T(8,128)(2,1)S(1)}, bf16[2,144,128]{2,1,0:T(8,128)(2,1)S(1)}, u32[]{:S(2)}, u32[]{:S(2)}) collective-permute-start(bf16[2,144,128]{2,1,0:T(8,128)(2,1)S(1)} %maximum_bitcast_fusion.own), channel_id=1, source_target_pairs={{320,322},{321,323},{322,320},{323,321},{324,326},{325,327},{326,3... | collective-permute-start | bytes 221192 | tf_op jit(solution)/shard_map/ppermute | solution.py:104
  26.1 0.1 copy.11
  26.2 0.1 copy.12
  26.3 0.1 pad_add_fusion
  26.4 0.0 collective-permute-done.3.three
  26.4 3.4 %collective-permute-done.2.two = bf16[2,144,128]{2,1,0:T(8,128)(2,1)S(1)} collective-permute-done((bf16[2,144,128]{2,1,0:T(8,128)(2,1)S(1)}, bf16[2,144,128]{2,1,0:T(8,128)(2,1)S(1)}, u32[]{:S(2)}, u32[]{:S(2)}) %collective-permute-start.2) | collective-permute-done | bytes 73760 | tf_op jit(solution)/shard_map/ppermute | solution.py:104
  29.8 0.0 collective-permute-done.1.late
  29.8 0.1 maximum_select_fusion
  29.9 0.0 all-to-all-done
  29.9 0.8 %broadcast_in_dim.15 = bf16[4,12,32,128]{3,2,1,0:T(8,128)(2,1)} broadcast(bf16[12,32,128]{2,1,0:T(8,128)(2,1)S(1)} %all-to-all-done), dimensions={1,2,3} | broadcast | bytes 491520 | tf_op jit(solution)/shard_map/broadcast_in_dim | solution.py:136
  30.7 4.0 %all-to-all-start.1 = ((bf16[4,12,32,128]{3,2,1,0:T(8,128)(2,1)}), bf16[4,12,32,128]{3,2,1,0:T(8,128)(2,1)S(1)}, u32[]{:S(2)}, u32[]{:S(2)}) async-start(bf16[4,12,32,128]{3,2,1,0:T(8,128)(2,1)} %broadcast_in_dim.15), calls=%async_computation.1 | async-start | bytes 786432 | tf_op jit(solution)/shard_map/all_to_all | solution.py:136
  34.7 2.3 %collective-permute-start.4 = (bf16[2,144,128]{2,1,0:T(8,128)(2,1)S(1)}, bf16[2,144,128]{2,1,0:T(8,128)(2,1)S(1)}, u32[]{:S(2)}, u32[]{:S(2)}) collective-permute-start(bf16[2,144,128]{2,1,0:T(8,128)(2,1)S(1)} %maximum_bitcast_fusion.own), channel_id=1, source_target_pairs={{0,2},{1,3},{2,0},{3,1},{4,6},{5,7},{6,4},{7,5},{8,10},{9,11},{10,... | collective-permute-start | bytes 221192 | tf_op jit(solution)/shard_map/ppermute | solution.py:104
  37.0 0.7 %collective-permute-start.5 = (bf16[4,2,4,4,128]{4,3,2,1,0:T(4,128)(2,1)S(1)}, bf16[4,2,4,4,128]{4,3,2,1,0:T(4,128)(2,1)S(1)}, u32[]{:S(2)}, u32[]{:S(2)}) collective-permute-start(bf16[4,2,4,4,128]{4,3,2,1,0:T(4,128)(2,1)S(1)} %maximum_select_fusion), channel_id=1, source_target_pairs={{320,327},{321,326},{322,325},{323,324},{324,323},{325,322},{326,3... | collective-permute-start | bytes 98312 | tf_op jit(solution)/shard_map/ppermute | solution.py:104
  37.7 0.0 collective-permute-done.5
  37.7 2.1 %collective-permute-done.4.one = bf16[2,144,128]{2,1,0:T(8,128)(2,1)S(1)} collective-permute-done((bf16[2,144,128]{2,1,0:T(8,128)(2,1)S(1)}, bf16[2,144,128]{2,1,0:T(8,128)(2,1)S(1)}, u32[]{:S(2)}, u32[]{:S(2)}) %collective-permute-start.4) | collective-permute-done | bytes 73760 | tf_op jit(solution)/shard_map/ppermute | solution.py:104
  39.8 1.1 %all-to-all-done.1 = bf16[4,12,32,128]{3,2,1,0:T(8,128)(2,1)S(1)} async-done(((bf16[4,12,32,128]{3,2,1,0:T(8,128)(2,1)}), bf16[4,12,32,128]{3,2,1,0:T(8,128)(2,1)S(1)}, u32[]{:S(2)}, u32[]{:S(2)}) %all-to-all-start.1) | async-done | bytes 393248 | tf_op jit(solution)/shard_map/all_to_all | solution.py:136
  40.9 5.5 %collective-permute-start.6 = (bf16[48,32,128]{2,1,0:T(8,128)(2,1)S(1)}, bf16[48,32,128]{2,1,0:T(8,128)(2,1)S(1)}, u32[]{:S(2)}, u32[]{:S(2)}) collective-permute-start(bf16[48,32,128]{2,1,0:T(8,128)(2,1)S(1)} %bitcast.35), channel_id=1, source_target_pairs={{0,8},{8,0},{1,9},{9,1},{2,10},{10,2},{3,11},{11,3},{4,12},{12,4},... | collective-permute-start | bytes 1179656 | tf_op jit(solution)/shard_map/ppermute | solution.py:142
  46.5 0.1 pad_add_fusion.1.place
  46.6 1.2 %collective-permute-done.6.other = bf16[48,32,128]{2,1,0:T(8,128)(2,1)S(1)} collective-permute-done((bf16[48,32,128]{2,1,0:T(8,128)(2,1)S(1)}, bf16[48,32,128]{2,1,0:T(8,128)(2,1)S(1)}, u32[]{:S(2)}, u32[]{:S(2)}) %collective-permute-start.6) | collective-permute-done | bytes 393248 | tf_op jit(solution)/shard_map/ppermute | solution.py:142
  47.8 2.8 %shard_map.64 = f32[2,128,1024]{2,1,0:T(8,128)} custom-call(s32[4]{0:T(128)S(1)} %pad_add_fusion.1.place, s32[2,56]{1,0:T(2,128)S(1)} %constant_dynamic-slice_fusion.1.numbers, f32[2,9]{1,0:T(2,128)S(1)} %constant_dynamic-slice_fusion.weights, bf16[2,144,128]{2,1,0:T(8,128)(2,1)S(1)} %maximum_bitcast_fusion.own, ...), custom_call_target="tpu_custom_call" | custom-call | tf_op jit(solution)/shard_map/pallas_call | solution.py:145
  (20 shorter events, 0.2 us)
Async XLA Ops:
  0.0 46.6 %copy-start = (f32[8,9]{1,0:T(8,128)S(1)}, f32[8,9]{1,0:T(8,128)}, u32[]{:S(2)}) copy-start(f32[8,9]{1,0:T(8,128)} %param.9) | copy-start | bytes 868
  0.0 0.9 %copy-start.2 = (bf16[4,32,256]{2,1,0:T(8,128)(2,1)S(1)}, bf16[4,32,256]{2,1,0:T(8,128)(2,1)}, u32[]{:S(2)}) copy-start(bf16[4,32,256]{2,1,0:T(8,128)(2,1)} %param.6) | copy-start | bytes 196612
  1.6 16.5 %collective-permute-start = (bf16[4,4,256]{2,1,0:T(4,128)(2,1)S(1)}, bf16[4,4,256]{2,1,0:T(4,128)(2,1)S(1)}, u32[]{:S(2)}, u32[]{:S(2)}) collective-permute-start(bf16[4,4,256]{2,1,0:T(4,128)(2,1)S(1)} %constant_dynamic-slice_fusion.2), channel_id=1, source_target_pairs={{0,7},{1,6},{2,5},{3,4},{4,3},{5,2},{6,1},{7,0},{8,15},{9,14},{10,... | collective-permute-start | bytes 24584 | tf_op jit(solution)/shard_map/ppermute | solution.py:104
  7.5 22.4 %all-to-all-start = ((bf16[12,32,128]{2,1,0:T(8,128)(2,1)}), bf16[12,32,128]{2,1,0:T(8,128)(2,1)S(1)}, u32[]{:S(2)}, u32[]{:S(2)}) async-start(bf16[12,32,128]{2,1,0:T(8,128)(2,1)} %broadcast_in_dim.14), calls=%async_computation | async-start | bytes 196608 | tf_op jit(solution)/shard_map/all_to_all | solution.py:125
  18.0 8.3 %copy-start.4 = (s32[8,8]{1,0:T(8,128)S(1)}, s32[8,8]{1,0:T(8,128)}, u32[]{:S(2)}) copy-start(s32[8,8]{1,0:T(8,128)} %param.10) | copy-start | bytes 772
  18.0 8.1 %copy-start.3 = (s32[8,16,3]{1,0,2:T(8,128)S(1)}, s32[8,16,3]{1,0,2:T(8,128)}, u32[]{:S(2)}) copy-start(s32[8,16,3]{1,0,2:T(8,128)} %param.11) | copy-start | bytes 4612
  18.0 29.8 %copy-start.1 = (f32[2,4,32,1024]{3,2,1,0:T(8,128)S(1)}, f32[2,4,32,1024]{3,2,1,0:T(8,128)}, u32[]{:S(2)}) copy-start(f32[2,4,32,1024]{3,2,1,0:T(8,128)} %param.7) | copy-start | bytes 3145732
  18.1 8.3 %collective-permute-start.3 = (bf16[2,144,128]{2,1,0:T(8,128)(2,1)S(1)}, bf16[2,144,128]{2,1,0:T(8,128)(2,1)S(1)}, u32[]{:S(2)}, u32[]{:S(2)}) collective-permute-start(bf16[2,144,128]{2,1,0:T(8,128)(2,1)S(1)} %maximum_bitcast_fusion.own), channel_id=1, source_target_pairs={{0,6},{1,7},{2,4},{3,5},{4,2},{5,3},{6,0},{7,1},{8,14},{9,15},{10,... | collective-permute-start | bytes 221192 | tf_op jit(solution)/shard_map/ppermute | solution.py:104
  23.5 6.3 %collective-permute-start.2 = (bf16[2,144,128]{2,1,0:T(8,128)(2,1)S(1)}, bf16[2,144,128]{2,1,0:T(8,128)(2,1)S(1)}, u32[]{:S(2)}, u32[]{:S(2)}) collective-permute-start(bf16[2,144,128]{2,1,0:T(8,128)(2,1)S(1)} %maximum_bitcast_fusion.own), channel_id=1, source_target_pairs={{0,4},{1,5},{2,6},{3,7},{4,0},{5,1},{6,2},{7,3},{8,12},{9,13},{10,... | collective-permute-start | bytes 221192 | tf_op jit(solution)/shard_map/ppermute | solution.py:104
  25.4 4.4 %collective-permute-start.1 = (bf16[2,144,128]{2,1,0:T(8,128)(2,1)S(1)}, bf16[2,144,128]{2,1,0:T(8,128)(2,1)S(1)}, u32[]{:S(2)}, u32[]{:S(2)}) collective-permute-start(bf16[2,144,128]{2,1,0:T(8,128)(2,1)S(1)} %maximum_bitcast_fusion.own), channel_id=1, source_target_pairs={{320,322},{321,323},{322,320},{323,321},{324,326},{325,327},{326,3... | collective-permute-start | bytes 221192 | tf_op jit(solution)/shard_map/ppermute | solution.py:104
  30.7 10.2 %all-to-all-start.1 = ((bf16[4,12,32,128]{3,2,1,0:T(8,128)(2,1)}), bf16[4,12,32,128]{3,2,1,0:T(8,128)(2,1)S(1)}, u32[]{:S(2)}, u32[]{:S(2)}) async-start(bf16[4,12,32,128]{3,2,1,0:T(8,128)(2,1)} %broadcast_in_dim.15), calls=%async_computation.1 | async-start | bytes 786432 | tf_op jit(solution)/shard_map/all_to_all | solution.py:136
  34.7 5.1 %collective-permute-start.4 = (bf16[2,144,128]{2,1,0:T(8,128)(2,1)S(1)}, bf16[2,144,128]{2,1,0:T(8,128)(2,1)S(1)}, u32[]{:S(2)}, u32[]{:S(2)}) collective-permute-start(bf16[2,144,128]{2,1,0:T(8,128)(2,1)S(1)} %maximum_bitcast_fusion.own), channel_id=1, source_target_pairs={{0,2},{1,3},{2,0},{3,1},{4,6},{5,7},{6,4},{7,5},{8,10},{9,11},{10,... | collective-permute-start | bytes 221192 | tf_op jit(solution)/shard_map/ppermute | solution.py:104
  37.0 0.7 %collective-permute-start.5 = (bf16[4,2,4,4,128]{4,3,2,1,0:T(4,128)(2,1)S(1)}, bf16[4,2,4,4,128]{4,3,2,1,0:T(4,128)(2,1)S(1)}, u32[]{:S(2)}, u32[]{:S(2)}) collective-permute-start(bf16[4,2,4,4,128]{4,3,2,1,0:T(4,128)(2,1)S(1)} %maximum_select_fusion), channel_id=1, source_target_pairs={{320,327},{321,326},{322,325},{323,324},{324,323},{325,322},{326,3... | collective-permute-start | bytes 98312 | tf_op jit(solution)/shard_map/ppermute | solution.py:104
  40.9 6.9 %collective-permute-start.6 = (bf16[48,32,128]{2,1,0:T(8,128)(2,1)S(1)}, bf16[48,32,128]{2,1,0:T(8,128)(2,1)S(1)}, u32[]{:S(2)}, u32[]{:S(2)}) collective-permute-start(bf16[48,32,128]{2,1,0:T(8,128)(2,1)S(1)} %bitcast.35), channel_id=1, source_target_pairs={{0,8},{8,0},{1,9},{9,1},{2,10},{10,2},{3,11},{11,3},{4,12},{12,4},... | collective-permute-start | bytes 1179656 | tf_op jit(solution)/shard_map/ppermute | solution.py:142

commit v16 on v15

--- a/solution.py
+++ b/solution.py
@@ -24,22 +24,19 @@
         seen[view ^ k, :, :OWN] = part[:, :OWN]
         seen[view ^ k ^ 3, :, OWN:] = jnp.where(soon, part[:, OWN:], edge[k])
 
-    def build(w):
-        dense[w] = jnp.zeros_like(dense[w])
-        for i in range(2 * BLOCKS):
-            j, quarter = i // 4, i % 4
+    def build(n):
+        w, j = n // 4, n % 4
+        dense[w, j] = jnp.zeros_like(dense[w, j])
+        for quarter in range(4):
+            i = 4 * j + quarter
+            lanes = pl.ds(64 * quarter, 64)
             for k in range(BAND):
-                shift = (numbers[w, BLOCKS + i * BAND + k] - (4 * j - 2)) & 15
-                base = shift * 64
-                lanes = pl.ds(64 * quarter, 64)
+                base = 64 * ((numbers[w, BLOCKS + i * BAND + k] - (4 * j - 2)) & 15)
                 q = i * BAND + k
                 s = q % 4 * 12 + q // 4
-                dense[w, j, pl.ds(pl.multiple_of(base + 32 * core, 32), 32), lanes] = mine[
-                    s, :, 64 * w : 64 * w + 64
-                ]
-                dense[w, j, pl.ds(pl.multiple_of(base + 32 * (1 - core), 32), 32), lanes] = other[
-                    s, :, 64 * w : 64 * w + 64
-                ]
+                for half, rows in ((core, mine), (1 - core, other)):
+                    at = pl.ds(pl.multiple_of(base + 32 * half, 32), 32)
+                    dense[w, j, at, lanes] = rows[s, :, 64 * w : 64 * w + 64]
 
     build(0)
 
@@ -81,8 +78,8 @@
 
     rows = lateral(0)
     for n in range(8):
-        if n == 0:
-            build(1)
+        if n < 7:
+            build(n + 1)
         after = lateral(n + 1) if n < 7 else None
         finish(n, rows)
         rows = after

time: 51 us -> 50.9 us (level)
  no operation moved by 1% of the time
where the time goes in v16:
time: 50.9 us; the launch traced here: 50.5 us
  starting transfers between devices  36.8 us (72%)
  waiting for transfers between devices  7.88 us (15%)
  local copies, waits for them, and re-layouts  2.69 us (5%)
  Pallas kernels  2.65 us (5%)
    ppermute x6, starting transfers between devices, permute(): return lax.ppermute(array, AXES, pairs)  16.8 us
    all_to_all x1, starting transfers between devices, shards(): along = lax.all_to_all(spread, 'z', 0, 0, tiled=True)  10.5 us
    ppermute x1, starting transfers between devices, shards(): other = lax.ppermute(mine, 'core', [(0, 1), (1, 0)])  5.52 us
    ppermute x6, waiting for transfers between devices, permute(): return lax.ppermute(array, AXES, pairs)  5.5 us
    all_to_all x1, starting transfers between devices, shards(): lax.all_to_all(jnp.broadcast_to(along[None], (4, 12, 32, 128)), 'x', 0, 0...  4.01 us
    pallas_call x1, Pallas kernels, shards(): pl.pallas_call(fused, out_shape=jax.ShapeDtypeStruct((2, OWN, 1024), jnp....  2.65 us
    ppermute x1, waiting for transfers between devices, shards(): other = lax.ppermute(mine, 'core', [(0, 1), (1, 0)])  1.23 us
    all_to_all x1, waiting for transfers between devices, shards(): lax.all_to_all(jnp.broadcast_to(along[None], (4, 12, 32, 128)), 'x', 0, 0...  1.15 us
  transfers between devices with their start and end apart: 9, of which 4 were waited for; matrix products, arithmetic and copies ran while one was open for 1% of the time, Pallas kernels for 0%

profile of v16, /device:TPU:1, one launch (start us, length us, event | category | flops | bytes accessed | tf_op | source)
XLA Modules:
  0.0 50.5 jit_solution(14066377623027401286)
XLA Ops:
  0.0 0.0 copy-start
  0.0 0.8 %reshape.39 = bf16[2,32,64]{2,1,0:T(8,128)(2,1)S(1)} reshape(bf16[2,2048]{1,0:T(2,128)(2,1)} %param.8) | data formatting | bytes 16384 | tf_op jit(solution)/shard_map/reshape | solution.py:112
  0.8 0.1 broadcast_in_dim.6
  0.9 0.7 %broadcast_in_dim.14 = bf16[12,32,128]{2,1,0:T(8,128)(2,1)} broadcast(bf16[32,128]{1,0:T(8,128)(2,1)S(1)} %broadcast_in_dim.6), dimensions={1,2} | broadcast | bytes 106496 | tf_op jit(solution)/shard_map/broadcast_in_dim | solution.py:113
  1.6 5.9 %collective-permute-start = (bf16[4,4,256]{2,1,0:T(4,128)(2,1)S(1)}, bf16[4,4,256]{2,1,0:T(4,128)(2,1)S(1)}, u32[]{:S(2)}, u32[]{:S(2)}) collective-permute-start(bf16[4,4,256]{2,1,0:T(4,128)(2,1)S(1)} %constant_dynamic-slice_fusion.2), channel_id=1, source_target_pairs={{0,7},{1,6},{2,5},{3,4},{4,3},{5,2},{6,1},{7,0},{8,15},{9,14},{10,... | collective-permute-start | bytes 24584 | tf_op jit(solution)/shard_map/ppermute | solution.py:101
  7.5 10.5 %all-to-all-start = ((bf16[12,32,128]{2,1,0:T(8,128)(2,1)}), bf16[12,32,128]{2,1,0:T(8,128)(2,1)S(1)}, u32[]{:S(2)}, u32[]{:S(2)}) async-start(bf16[12,32,128]{2,1,0:T(8,128)(2,1)} %broadcast_in_dim.14), calls=%async_computation | async-start | bytes 196608 | tf_op jit(solution)/shard_map/all_to_all | solution.py:122
  18.0 0.0 copy-start.4
  18.0 0.0 copy-start.3
  18.0 0.0 copy-start.1
  18.1 0.0 collective-permute-done
  18.1 5.4 %collective-permute-start.3 = (bf16[2,144,128]{2,1,0:T(8,128)(2,1)S(1)}, bf16[2,144,128]{2,1,0:T(8,128)(2,1)S(1)}, u32[]{:S(2)}, u32[]{:S(2)}) collective-permute-start(bf16[2,144,128]{2,1,0:T(8,128)(2,1)S(1)} %maximum_bitcast_fusion.own), channel_id=1, source_target_pairs={{0,6},{1,7},{2,4},{3,5},{4,2},{5,3},{6,0},{7,1},{8,14},{9,15},{10,... | collective-permute-start | bytes 221192 | tf_op jit(solution)/shard_map/ppermute | solution.py:101
  23.5 1.9 %collective-permute-start.2 = (bf16[2,144,128]{2,1,0:T(8,128)(2,1)S(1)}, bf16[2,144,128]{2,1,0:T(8,128)(2,1)S(1)}, u32[]{:S(2)}, u32[]{:S(2)}) collective-permute-start(bf16[2,144,128]{2,1,0:T(8,128)(2,1)S(1)} %maximum_bitcast_fusion.own), channel_id=1, source_target_pairs={{0,4},{1,5},{2,6},{3,7},{4,0},{5,1},{6,2},{7,3},{8,12},{9,13},{10,... | collective-permute-start | bytes 221192 | tf_op jit(solution)/shard_map/ppermute | solution.py:101
  25.4 0.7 %collective-permute-start.1 = (bf16[2,144,128]{2,1,0:T(8,128)(2,1)S(1)}, bf16[2,144,128]{2,1,0:T(8,128)(2,1)S(1)}, u32[]{:S(2)}, u32[]{:S(2)}) collective-permute-start(bf16[2,144,128]{2,1,0:T(8,128)(2,1)S(1)} %maximum_bitcast_fusion.own), channel_id=1, source_target_pairs={{320,322},{321,323},{322,320},{323,321},{324,326},{325,327},{326,3... | collective-permute-start | bytes 221192 | tf_op jit(solution)/shard_map/ppermute | solution.py:101
  26.1 0.1 copy.11
  26.2 0.1 copy.12
  26.3 0.1 pad_add_fusion
  26.4 0.0 collective-permute-done.3.three
  26.4 3.4 %collective-permute-done.2.two = bf16[2,144,128]{2,1,0:T(8,128)(2,1)S(1)} collective-permute-done((bf16[2,144,128]{2,1,0:T(8,128)(2,1)S(1)}, bf16[2,144,128]{2,1,0:T(8,128)(2,1)S(1)}, u32[]{:S(2)}, u32[]{:S(2)}) %collective-permute-start.2) | collective-permute-done | bytes 73760 | tf_op jit(solution)/shard_map/ppermute | solution.py:101
  29.8 0.0 collective-permute-done.1.late
  29.8 0.1 maximum_select_fusion
  29.9 0.0 all-to-all-done
  29.9 0.8 %broadcast_in_dim.15 = bf16[4,12,32,128]{3,2,1,0:T(8,128)(2,1)} broadcast(bf16[12,32,128]{2,1,0:T(8,128)(2,1)S(1)} %all-to-all-done), dimensions={1,2,3} | broadcast | bytes 491520 | tf_op jit(solution)/shard_map/broadcast_in_dim | solution.py:133
  30.7 4.0 %all-to-all-start.1 = ((bf16[4,12,32,128]{3,2,1,0:T(8,128)(2,1)}), bf16[4,12,32,128]{3,2,1,0:T(8,128)(2,1)S(1)}, u32[]{:S(2)}, u32[]{:S(2)}) async-start(bf16[4,12,32,128]{3,2,1,0:T(8,128)(2,1)} %broadcast_in_dim.15), calls=%async_computation.1 | async-start | bytes 786432 | tf_op jit(solution)/shard_map/all_to_all | solution.py:133
  34.7 2.3 %collective-permute-start.4 = (bf16[2,144,128]{2,1,0:T(8,128)(2,1)S(1)}, bf16[2,144,128]{2,1,0:T(8,128)(2,1)S(1)}, u32[]{:S(2)}, u32[]{:S(2)}) collective-permute-start(bf16[2,144,128]{2,1,0:T(8,128)(2,1)S(1)} %maximum_bitcast_fusion.own), channel_id=1, source_target_pairs={{0,2},{1,3},{2,0},{3,1},{4,6},{5,7},{6,4},{7,5},{8,10},{9,11},{10,... | collective-permute-start | bytes 221192 | tf_op jit(solution)/shard_map/ppermute | solution.py:101
  37.0 0.7 %collective-permute-start.5 = (bf16[4,2,4,4,128]{4,3,2,1,0:T(4,128)(2,1)S(1)}, bf16[4,2,4,4,128]{4,3,2,1,0:T(4,128)(2,1)S(1)}, u32[]{:S(2)}, u32[]{:S(2)}) collective-permute-start(bf16[4,2,4,4,128]{4,3,2,1,0:T(4,128)(2,1)S(1)} %maximum_select_fusion), channel_id=1, source_target_pairs={{320,327},{321,326},{322,325},{323,324},{324,323},{325,322},{326,3... | collective-permute-start | bytes 98312 | tf_op jit(solution)/shard_map/ppermute | solution.py:101
  37.7 0.0 collective-permute-done.5
  37.7 2.1 %collective-permute-done.4.one = bf16[2,144,128]{2,1,0:T(8,128)(2,1)S(1)} collective-permute-done((bf16[2,144,128]{2,1,0:T(8,128)(2,1)S(1)}, bf16[2,144,128]{2,1,0:T(8,128)(2,1)S(1)}, u32[]{:S(2)}, u32[]{:S(2)}) %collective-permute-start.4) | collective-permute-done | bytes 73760 | tf_op jit(solution)/shard_map/ppermute | solution.py:101
  39.8 1.1 %all-to-all-done.1 = bf16[4,12,32,128]{3,2,1,0:T(8,128)(2,1)S(1)} async-done(((bf16[4,12,32,128]{3,2,1,0:T(8,128)(2,1)}), bf16[4,12,32,128]{3,2,1,0:T(8,128)(2,1)S(1)}, u32[]{:S(2)}, u32[]{:S(2)}) %all-to-all-start.1) | async-done | bytes 393248 | tf_op jit(solution)/shard_map/all_to_all | solution.py:133
  40.9 5.5 %collective-permute-start.6 = (bf16[48,32,128]{2,1,0:T(8,128)(2,1)S(1)}, bf16[48,32,128]{2,1,0:T(8,128)(2,1)S(1)}, u32[]{:S(2)}, u32[]{:S(2)}) collective-permute-start(bf16[48,32,128]{2,1,0:T(8,128)(2,1)S(1)} %bitcast.35), channel_id=1, source_target_pairs={{0,8},{8,0},{1,9},{9,1},{2,10},{10,2},{3,11},{11,3},{4,12},{12,4},... | collective-permute-start | bytes 1179656 | tf_op jit(solution)/shard_map/ppermute | solution.py:139
  46.5 0.1 pad_add_fusion.1.place
  46.6 1.2 %collective-permute-done.6.other = bf16[48,32,128]{2,1,0:T(8,128)(2,1)S(1)} collective-permute-done((bf16[48,32,128]{2,1,0:T(8,128)(2,1)S(1)}, bf16[48,32,128]{2,1,0:T(8,128)(2,1)S(1)}, u32[]{:S(2)}, u32[]{:S(2)}) %collective-permute-start.6) | collective-permute-done | bytes 393248 | tf_op jit(solution)/shard_map/ppermute | solution.py:139
  47.8 2.7 %shard_map.64 = f32[2,128,1024]{2,1,0:T(8,128)} custom-call(s32[4]{0:T(128)S(1)} %pad_add_fusion.1.place, s32[2,56]{1,0:T(2,128)S(1)} %constant_dynamic-slice_fusion.1.numbers, f32[2,9]{1,0:T(2,128)S(1)} %constant_dynamic-slice_fusion.weights, bf16[2,144,128]{2,1,0:T(8,128)(2,1)S(1)} %maximum_bitcast_fusion.own, ...), custom_call_target="tpu_custom_call" | custom-call | tf_op jit(solution)/shard_map/pallas_call | solution.py:142
  (20 shorter events, 0.2 us)
Async XLA Ops:
  0.0 46.6 %copy-start = (f32[8,9]{1,0:T(8,128)S(1)}, f32[8,9]{1,0:T(8,128)}, u32[]{:S(2)}) copy-start(f32[8,9]{1,0:T(8,128)} %param.9) | copy-start | bytes 868
  0.0 0.9 %copy-start.2 = (bf16[4,32,256]{2,1,0:T(8,128)(2,1)S(1)}, bf16[4,32,256]{2,1,0:T(8,128)(2,1)}, u32[]{:S(2)}) copy-start(bf16[4,32,256]{2,1,0:T(8,128)(2,1)} %param.6) | copy-start | bytes 196612
  1.6 16.5 %collective-permute-start = (bf16[4,4,256]{2,1,0:T(4,128)(2,1)S(1)}, bf16[4,4,256]{2,1,0:T(4,128)(2,1)S(1)}, u32[]{:S(2)}, u32[]{:S(2)}) collective-permute-start(bf16[4,4,256]{2,1,0:T(4,128)(2,1)S(1)} %constant_dynamic-slice_fusion.2), channel_id=1, source_target_pairs={{0,7},{1,6},{2,5},{3,4},{4,3},{5,2},{6,1},{7,0},{8,15},{9,14},{10,... | collective-permute-start | bytes 24584 | tf_op jit(solution)/shard_map/ppermute | solution.py:101
  7.5 22.4 %all-to-all-start = ((bf16[12,32,128]{2,1,0:T(8,128)(2,1)}), bf16[12,32,128]{2,1,0:T(8,128)(2,1)S(1)}, u32[]{:S(2)}, u32[]{:S(2)}) async-start(bf16[12,32,128]{2,1,0:T(8,128)(2,1)} %broadcast_in_dim.14), calls=%async_computation | async-start | bytes 196608 | tf_op jit(solution)/shard_map/all_to_all | solution.py:122
  18.0 8.3 %copy-start.4 = (s32[8,8]{1,0:T(8,128)S(1)}, s32[8,8]{1,0:T(8,128)}, u32[]{:S(2)}) copy-start(s32[8,8]{1,0:T(8,128)} %param.10) | copy-start | bytes 772
  18.0 8.1 %copy-start.3 = (s32[8,16,3]{1,0,2:T(8,128)S(1)}, s32[8,16,3]{1,0,2:T(8,128)}, u32[]{:S(2)}) copy-start(s32[8,16,3]{1,0,2:T(8,128)} %param.11) | copy-start | bytes 4612
  18.0 29.8 %copy-start.1 = (f32[2,4,32,1024]{3,2,1,0:T(8,128)S(1)}, f32[2,4,32,1024]{3,2,1,0:T(8,128)}, u32[]{:S(2)}) copy-start(f32[2,4,32,1024]{3,2,1,0:T(8,128)} %param.7) | copy-start | bytes 3145732
  18.1 8.3 %collective-permute-start.3 = (bf16[2,144,128]{2,1,0:T(8,128)(2,1)S(1)}, bf16[2,144,128]{2,1,0:T(8,128)(2,1)S(1)}, u32[]{:S(2)}, u32[]{:S(2)}) collective-permute-start(bf16[2,144,128]{2,1,0:T(8,128)(2,1)S(1)} %maximum_bitcast_fusion.own), channel_id=1, source_target_pairs={{0,6},{1,7},{2,4},{3,5},{4,2},{5,3},{6,0},{7,1},{8,14},{9,15},{10,... | collective-permute-start | bytes 221192 | tf_op jit(solution)/shard_map/ppermute | solution.py:101
  23.5 6.3 %collective-permute-start.2 = (bf16[2,144,128]{2,1,0:T(8,128)(2,1)S(1)}, bf16[2,144,128]{2,1,0:T(8,128)(2,1)S(1)}, u32[]{:S(2)}, u32[]{:S(2)}) collective-permute-start(bf16[2,144,128]{2,1,0:T(8,128)(2,1)S(1)} %maximum_bitcast_fusion.own), channel_id=1, source_target_pairs={{0,4},{1,5},{2,6},{3,7},{4,0},{5,1},{6,2},{7,3},{8,12},{9,13},{10,... | collective-permute-start | bytes 221192 | tf_op jit(solution)/shard_map/ppermute | solution.py:101
  25.4 4.4 %collective-permute-start.1 = (bf16[2,144,128]{2,1,0:T(8,128)(2,1)S(1)}, bf16[2,144,128]{2,1,0:T(8,128)(2,1)S(1)}, u32[]{:S(2)}, u32[]{:S(2)}) collective-permute-start(bf16[2,144,128]{2,1,0:T(8,128)(2,1)S(1)} %maximum_bitcast_fusion.own), channel_id=1, source_target_pairs={{320,322},{321,323},{322,320},{323,321},{324,326},{325,327},{326,3... | collective-permute-start | bytes 221192 | tf_op jit(solution)/shard_map/ppermute | solution.py:101
  30.7 10.2 %all-to-all-start.1 = ((bf16[4,12,32,128]{3,2,1,0:T(8,128)(2,1)}), bf16[4,12,32,128]{3,2,1,0:T(8,128)(2,1)S(1)}, u32[]{:S(2)}, u32[]{:S(2)}) async-start(bf16[4,12,32,128]{3,2,1,0:T(8,128)(2,1)} %broadcast_in_dim.15), calls=%async_computation.1 | async-start | bytes 786432 | tf_op jit(solution)/shard_map/all_to_all | solution.py:133
  34.7 5.1 %collective-permute-start.4 = (bf16[2,144,128]{2,1,0:T(8,128)(2,1)S(1)}, bf16[2,144,128]{2,1,0:T(8,128)(2,1)S(1)}, u32[]{:S(2)}, u32[]{:S(2)}) collective-permute-start(bf16[2,144,128]{2,1,0:T(8,128)(2,1)S(1)} %maximum_bitcast_fusion.own), channel_id=1, source_target_pairs={{0,2},{1,3},{2,0},{3,1},{4,6},{5,7},{6,4},{7,5},{8,10},{9,11},{10,... | collective-permute-start | bytes 221192 | tf_op jit(solution)/shard_map/ppermute | solution.py:101
  37.0 0.7 %collective-permute-start.5 = (bf16[4,2,4,4,128]{4,3,2,1,0:T(4,128)(2,1)S(1)}, bf16[4,2,4,4,128]{4,3,2,1,0:T(4,128)(2,1)S(1)}, u32[]{:S(2)}, u32[]{:S(2)}) collective-permute-start(bf16[4,2,4,4,128]{4,3,2,1,0:T(4,128)(2,1)S(1)} %maximum_select_fusion), channel_id=1, source_target_pairs={{320,327},{321,326},{322,325},{323,324},{324,323},{325,322},{326,3... | collective-permute-start | bytes 98312 | tf_op jit(solution)/shard_map/ppermute | solution.py:101
  40.9 6.9 %collective-permute-start.6 = (bf16[48,32,128]{2,1,0:T(8,128)(2,1)S(1)}, bf16[48,32,128]{2,1,0:T(8,128)(2,1)S(1)}, u32[]{:S(2)}, u32[]{:S(2)}) collective-permute-start(bf16[48,32,128]{2,1,0:T(8,128)(2,1)S(1)} %bitcast.35), channel_id=1, source_target_pairs={{0,8},{8,0},{1,9},{9,1},{2,10},{10,2},{3,11},{11,3},{4,12},{12,4},... | collective-permute-start | bytes 1179656 | tf_op jit(solution)/shard_map/ppermute | solution.py:139

commit v17 on v16

--- a/solution.py
+++ b/solution.py
@@ -12,7 +12,7 @@
 EDGE = PLANES * HALO
 BLOCKS = 8
 BAND = 3
-AHEAD = 5
+AHEAD = 4
 AXES = ("z", "x", "core", "view", "gy")
 SIZES = (12, 4, 2, 4, 2)
 

time: 50.9 us -> 50.8 us (level)
  starting transfers between devices: 36.8 us -> 35.6 us
  waiting for transfers between devices: 7.88 us -> 9 us
    ppermute x6, waiting for transfers between devices: 5.5 us -> 6.89 us  [permute(): return lax.ppermute(array, AXES, pairs)]
    ppermute x1, starting transfers between devices: 5.52 us -> 4.67 us  [shards(): other = lax.ppermute(mine, 'core', [(0, 1), (1, 0)])]
where the time goes in v17:
time: 50.8 us; the launch traced here: 50.4 us
  starting transfers between devices  35.6 us (70%)
  waiting for transfers between devices  9 us (18%)
  local copies, waits for them, and re-layouts  2.69 us (5%)
  Pallas kernels  2.65 us (5%)
    ppermute x6, starting transfers between devices, permute(): return lax.ppermute(array, AXES, pairs)  16.4 us
    all_to_all x1, starting transfers between devices, shards(): along = lax.all_to_all(spread, 'z', 0, 0, tiled=True)  10.5 us
    ppermute x6, waiting for transfers between devices, permute(): return lax.ppermute(array, AXES, pairs)  6.89 us
    ppermute x1, starting transfers between devices, shards(): other = lax.ppermute(mine, 'core', [(0, 1), (1, 0)])  4.67 us
    all_to_all x1, starting transfers between devices, shards(): lax.all_to_all(jnp.broadcast_to(along[None], (4, 12, 32, 128)), 'x', 0, 0...  4.01 us
    pallas_call x1, Pallas kernels, shards(): pl.pallas_call(fused, out_shape=jax.ShapeDtypeStruct((2, OWN, 1024), jnp....  2.65 us
    ppermute x1, waiting for transfers between devices, shards(): other = lax.ppermute(mine, 'core', [(0, 1), (1, 0)])  1.23 us
  transfers between devices with their start and end apart: 9, of which 4 were waited for; matrix products, arithmetic and copies ran while one was open for 1% of the time, Pallas kernels for 0%

profile of v17, /device:TPU:1, one launch (start us, length us, event | category | flops | bytes accessed | tf_op | source)
XLA Modules:
  0.0 50.4 jit_solution(9831795983637172062)
XLA Ops:
  0.0 0.0 copy-start
  0.0 0.8 %reshape.39 = bf16[2,32,64]{2,1,0:T(8,128)(2,1)S(1)} reshape(bf16[2,2048]{1,0:T(2,128)(2,1)} %param.8) | data formatting | bytes 16384 | tf_op jit(solution)/shard_map/reshape | solution.py:112
  0.8 0.1 broadcast_in_dim.6
  0.9 0.7 %broadcast_in_dim.14 = bf16[12,32,128]{2,1,0:T(8,128)(2,1)} broadcast(bf16[32,128]{1,0:T(8,128)(2,1)S(1)} %broadcast_in_dim.6), dimensions={1,2} | broadcast | bytes 106496 | tf_op jit(solution)/shard_map/broadcast_in_dim | solution.py:113
  1.6 5.9 %collective-permute-start = (bf16[4,4,256]{2,1,0:T(4,128)(2,1)S(1)}, bf16[4,4,256]{2,1,0:T(4,128)(2,1)S(1)}, u32[]{:S(2)}, u32[]{:S(2)}) collective-permute-start(bf16[4,4,256]{2,1,0:T(4,128)(2,1)S(1)} %constant_dynamic-slice_fusion.2), channel_id=1, source_target_pairs={{0,7},{1,6},{2,5},{3,4},{4,3},{5,2},{6,1},{7,0},{8,15},{9,14},{10,... | collective-permute-start | bytes 24584 | tf_op jit(solution)/shard_map/ppermute | solution.py:101
  7.5 10.5 %all-to-all-start = ((bf16[12,32,128]{2,1,0:T(8,128)(2,1)}), bf16[12,32,128]{2,1,0:T(8,128)(2,1)S(1)}, u32[]{:S(2)}, u32[]{:S(2)}) async-start(bf16[12,32,128]{2,1,0:T(8,128)(2,1)} %broadcast_in_dim.14), calls=%async_computation | async-start | bytes 196608 | tf_op jit(solution)/shard_map/all_to_all | solution.py:122
  18.0 0.0 copy-start.4
  18.0 0.0 copy-start.3
  18.0 0.0 copy-start.1
  18.1 0.0 collective-permute-done
  18.1 5.4 %collective-permute-start.3 = (bf16[2,144,128]{2,1,0:T(8,128)(2,1)S(1)}, bf16[2,144,128]{2,1,0:T(8,128)(2,1)S(1)}, u32[]{:S(2)}, u32[]{:S(2)}) collective-permute-start(bf16[2,144,128]{2,1,0:T(8,128)(2,1)S(1)} %maximum_bitcast_fusion.own), channel_id=1, source_target_pairs={{0,6},{1,7},{2,4},{3,5},{4,2},{5,3},{6,0},{7,1},{8,14},{9,15},{10,... | collective-permute-start | bytes 221192 | tf_op jit(solution)/shard_map/ppermute | solution.py:101
  23.5 1.9 %collective-permute-start.2 = (bf16[2,144,128]{2,1,0:T(8,128)(2,1)S(1)}, bf16[2,144,128]{2,1,0:T(8,128)(2,1)S(1)}, u32[]{:S(2)}, u32[]{:S(2)}) collective-permute-start(bf16[2,144,128]{2,1,0:T(8,128)(2,1)S(1)} %maximum_bitcast_fusion.own), channel_id=1, source_target_pairs={{0,4},{1,5},{2,6},{3,7},{4,0},{5,1},{6,2},{7,3},{8,12},{9,13},{10,... | collective-permute-start | bytes 221192 | tf_op jit(solution)/shard_map/ppermute | solution.py:101
  25.4 0.7 %collective-permute-start.1 = (bf16[2,144,128]{2,1,0:T(8,128)(2,1)S(1)}, bf16[2,144,128]{2,1,0:T(8,128)(2,1)S(1)}, u32[]{:S(2)}, u32[]{:S(2)}) collective-permute-start(bf16[2,144,128]{2,1,0:T(8,128)(2,1)S(1)} %maximum_bitcast_fusion.own), channel_id=1, source_target_pairs={{256,258},{257,259},{258,256},{259,257},{260,262},{261,263},{262,2... | collective-permute-start | bytes 221192 | tf_op jit(solution)/shard_map/ppermute | solution.py:101
  26.1 0.1 copy.11
  26.2 0.1 copy.12
  26.3 0.1 pad_add_fusion
  26.4 0.0 collective-permute-done.3.three
  26.4 4.1 %collective-permute-done.2.two = bf16[2,144,128]{2,1,0:T(8,128)(2,1)S(1)} collective-permute-done((bf16[2,144,128]{2,1,0:T(8,128)(2,1)S(1)}, bf16[2,144,128]{2,1,0:T(8,128)(2,1)S(1)}, u32[]{:S(2)}, u32[]{:S(2)}) %collective-permute-start.2) | collective-permute-done | bytes 73760 | tf_op jit(solution)/shard_map/ppermute | solution.py:101
  30.5 0.0 collective-permute-done.1.late
  30.6 0.1 maximum_select_fusion
  30.6 0.0 all-to-all-done
  30.6 0.8 %broadcast_in_dim.15 = bf16[4,12,32,128]{3,2,1,0:T(8,128)(2,1)} broadcast(bf16[12,32,128]{2,1,0:T(8,128)(2,1)S(1)} %all-to-all-done), dimensions={1,2,3} | broadcast | bytes 491520 | tf_op jit(solution)/shard_map/broadcast_in_dim | solution.py:133
  31.4 4.0 %all-to-all-start.1 = ((bf16[4,12,32,128]{3,2,1,0:T(8,128)(2,1)}), bf16[4,12,32,128]{3,2,1,0:T(8,128)(2,1)S(1)}, u32[]{:S(2)}, u32[]{:S(2)}) async-start(bf16[4,12,32,128]{3,2,1,0:T(8,128)(2,1)} %broadcast_in_dim.15), calls=%async_computation.1 | async-start | bytes 786432 | tf_op jit(solution)/shard_map/all_to_all | solution.py:133
  35.4 1.9 %collective-permute-start.4 = (bf16[2,144,128]{2,1,0:T(8,128)(2,1)S(1)}, bf16[2,144,128]{2,1,0:T(8,128)(2,1)S(1)}, u32[]{:S(2)}, u32[]{:S(2)}) collective-permute-start(bf16[2,144,128]{2,1,0:T(8,128)(2,1)S(1)} %maximum_bitcast_fusion.own), channel_id=1, source_target_pairs={{0,2},{1,3},{2,0},{3,1},{4,6},{5,7},{6,4},{7,5},{8,10},{9,11},{10,... | collective-permute-start | bytes 221192 | tf_op jit(solution)/shard_map/ppermute | solution.py:101
  37.4 0.7 %collective-permute-start.5 = (bf16[4,2,4,4,128]{4,3,2,1,0:T(4,128)(2,1)S(1)}, bf16[4,2,4,4,128]{4,3,2,1,0:T(4,128)(2,1)S(1)}, u32[]{:S(2)}, u32[]{:S(2)}) collective-permute-start(bf16[4,2,4,4,128]{4,3,2,1,0:T(4,128)(2,1)S(1)} %maximum_select_fusion), channel_id=1, source_target_pairs={{256,263},{257,262},{258,261},{259,260},{260,259},{261,258},{262,2... | collective-permute-start | bytes 98312 | tf_op jit(solution)/shard_map/ppermute | solution.py:101
  38.0 0.0 collective-permute-done.5
  38.0 2.8 %collective-permute-done.4.one = bf16[2,144,128]{2,1,0:T(8,128)(2,1)S(1)} collective-permute-done((bf16[2,144,128]{2,1,0:T(8,128)(2,1)S(1)}, bf16[2,144,128]{2,1,0:T(8,128)(2,1)S(1)}, u32[]{:S(2)}, u32[]{:S(2)}) %collective-permute-start.4) | collective-permute-done | bytes 73760 | tf_op jit(solution)/shard_map/ppermute | solution.py:101
  40.8 0.9 %all-to-all-done.1 = bf16[4,12,32,128]{3,2,1,0:T(8,128)(2,1)S(1)} async-done(((bf16[4,12,32,128]{3,2,1,0:T(8,128)(2,1)}), bf16[4,12,32,128]{3,2,1,0:T(8,128)(2,1)S(1)}, u32[]{:S(2)}, u32[]{:S(2)}) %all-to-all-start.1) | async-done | bytes 393248 | tf_op jit(solution)/shard_map/all_to_all | solution.py:133
  41.7 4.7 %collective-permute-start.6 = (bf16[48,32,128]{2,1,0:T(8,128)(2,1)S(1)}, bf16[48,32,128]{2,1,0:T(8,128)(2,1)S(1)}, u32[]{:S(2)}, u32[]{:S(2)}) collective-permute-start(bf16[48,32,128]{2,1,0:T(8,128)(2,1)S(1)} %bitcast.35), channel_id=1, source_target_pairs={{0,8},{8,0},{1,9},{9,1},{2,10},{10,2},{3,11},{11,3},{4,12},{12,4},... | collective-permute-start | bytes 1179656 | tf_op jit(solution)/shard_map/ppermute | solution.py:139
  46.4 0.1 pad_add_fusion.1.place
  46.5 1.2 %collective-permute-done.6.other = bf16[48,32,128]{2,1,0:T(8,128)(2,1)S(1)} collective-permute-done((bf16[48,32,128]{2,1,0:T(8,128)(2,1)S(1)}, bf16[48,32,128]{2,1,0:T(8,128)(2,1)S(1)}, u32[]{:S(2)}, u32[]{:S(2)}) %collective-permute-start.6) | collective-permute-done | bytes 393248 | tf_op jit(solution)/shard_map/ppermute | solution.py:139
  47.7 2.6 %shard_map.64 = f32[2,128,1024]{2,1,0:T(8,128)} custom-call(s32[4]{0:T(128)S(1)} %pad_add_fusion.1.place, s32[2,56]{1,0:T(2,128)S(1)} %constant_dynamic-slice_fusion.1.numbers, f32[2,9]{1,0:T(2,128)S(1)} %constant_dynamic-slice_fusion.weights, bf16[2,144,128]{2,1,0:T(8,128)(2,1)S(1)} %maximum_bitcast_fusion.own, ...), custom_call_target="tpu_custom_call" | custom-call | tf_op jit(solution)/shard_map/pallas_call | solution.py:142
  (20 shorter events, 0.2 us)
Async XLA Ops:
  0.0 46.5 %copy-start = (f32[8,9]{1,0:T(8,128)S(1)}, f32[8,9]{1,0:T(8,128)}, u32[]{:S(2)}) copy-start(f32[8,9]{1,0:T(8,128)} %param.9) | copy-start | bytes 868
  0.0 0.9 %copy-start.2 = (bf16[4,32,256]{2,1,0:T(8,128)(2,1)S(1)}, bf16[4,32,256]{2,1,0:T(8,128)(2,1)}, u32[]{:S(2)}) copy-start(bf16[4,32,256]{2,1,0:T(8,128)(2,1)} %param.6) | copy-start | bytes 196612
  1.6 16.5 %collective-permute-start = (bf16[4,4,256]{2,1,0:T(4,128)(2,1)S(1)}, bf16[4,4,256]{2,1,0:T(4,128)(2,1)S(1)}, u32[]{:S(2)}, u32[]{:S(2)}) collective-permute-start(bf16[4,4,256]{2,1,0:T(4,128)(2,1)S(1)} %constant_dynamic-slice_fusion.2), channel_id=1, source_target_pairs={{0,7},{1,6},{2,5},{3,4},{4,3},{5,2},{6,1},{7,0},{8,15},{9,14},{10,... | collective-permute-start | bytes 24584 | tf_op jit(solution)/shard_map/ppermute | solution.py:101
  7.5 23.1 %all-to-all-start = ((bf16[12,32,128]{2,1,0:T(8,128)(2,1)}), bf16[12,32,128]{2,1,0:T(8,128)(2,1)S(1)}, u32[]{:S(2)}, u32[]{:S(2)}) async-start(bf16[12,32,128]{2,1,0:T(8,128)(2,1)} %broadcast_in_dim.14), calls=%async_computation | async-start | bytes 196608 | tf_op jit(solution)/shard_map/all_to_all | solution.py:122
  18.0 8.3 %copy-start.4 = (s32[8,8]{1,0:T(8,128)S(1)}, s32[8,8]{1,0:T(8,128)}, u32[]{:S(2)}) copy-start(s32[8,8]{1,0:T(8,128)} %param.10) | copy-start | bytes 772
  18.0 8.1 %copy-start.3 = (s32[8,16,3]{1,0,2:T(8,128)S(1)}, s32[8,16,3]{1,0,2:T(8,128)}, u32[]{:S(2)}) copy-start(s32[8,16,3]{1,0,2:T(8,128)} %param.11) | copy-start | bytes 4612
  18.0 29.7 %copy-start.1 = (f32[2,4,32,1024]{3,2,1,0:T(8,128)S(1)}, f32[2,4,32,1024]{3,2,1,0:T(8,128)}, u32[]{:S(2)}) copy-start(f32[2,4,32,1024]{3,2,1,0:T(8,128)} %param.7) | copy-start | bytes 3145732
  18.1 8.3 %collective-permute-start.3 = (bf16[2,144,128]{2,1,0:T(8,128)(2,1)S(1)}, bf16[2,144,128]{2,1,0:T(8,128)(2,1)S(1)}, u32[]{:S(2)}, u32[]{:S(2)}) collective-permute-start(bf16[2,144,128]{2,1,0:T(8,128)(2,1)S(1)} %maximum_bitcast_fusion.own), channel_id=1, source_target_pairs={{0,6},{1,7},{2,4},{3,5},{4,2},{5,3},{6,0},{7,1},{8,14},{9,15},{10,... | collective-permute-start | bytes 221192 | tf_op jit(solution)/shard_map/ppermute | solution.py:101
  23.5 7.0 %collective-permute-start.2 = (bf16[2,144,128]{2,1,0:T(8,128)(2,1)S(1)}, bf16[2,144,128]{2,1,0:T(8,128)(2,1)S(1)}, u32[]{:S(2)}, u32[]{:S(2)}) collective-permute-start(bf16[2,144,128]{2,1,0:T(8,128)(2,1)S(1)} %maximum_bitcast_fusion.own), channel_id=1, source_target_pairs={{0,4},{1,5},{2,6},{3,7},{4,0},{5,1},{6,2},{7,3},{8,12},{9,13},{10,... | collective-permute-start | bytes 221192 | tf_op jit(solution)/shard_map/ppermute | solution.py:101
  25.4 5.1 %collective-permute-start.1 = (bf16[2,144,128]{2,1,0:T(8,128)(2,1)S(1)}, bf16[2,144,128]{2,1,0:T(8,128)(2,1)S(1)}, u32[]{:S(2)}, u32[]{:S(2)}) collective-permute-start(bf16[2,144,128]{2,1,0:T(8,128)(2,1)S(1)} %maximum_bitcast_fusion.own), channel_id=1, source_target_pairs={{256,258},{257,259},{258,256},{259,257},{260,262},{261,263},{262,2... | collective-permute-start | bytes 221192 | tf_op jit(solution)/shard_map/ppermute | solution.py:101
  31.4 10.3 %all-to-all-start.1 = ((bf16[4,12,32,128]{3,2,1,0:T(8,128)(2,1)}), bf16[4,12,32,128]{3,2,1,0:T(8,128)(2,1)S(1)}, u32[]{:S(2)}, u32[]{:S(2)}) async-start(bf16[4,12,32,128]{3,2,1,0:T(8,128)(2,1)} %broadcast_in_dim.15), calls=%async_computation.1 | async-start | bytes 786432 | tf_op jit(solution)/shard_map/all_to_all | solution.py:133
  35.4 5.4 %collective-permute-start.4 = (bf16[2,144,128]{2,1,0:T(8,128)(2,1)S(1)}, bf16[2,144,128]{2,1,0:T(8,128)(2,1)S(1)}, u32[]{:S(2)}, u32[]{:S(2)}) collective-permute-start(bf16[2,144,128]{2,1,0:T(8,128)(2,1)S(1)} %maximum_bitcast_fusion.own), channel_id=1, source_target_pairs={{0,2},{1,3},{2,0},{3,1},{4,6},{5,7},{6,4},{7,5},{8,10},{9,11},{10,... | collective-permute-start | bytes 221192 | tf_op jit(solution)/shard_map/ppermute | solution.py:101
  37.4 0.7 %collective-permute-start.5 = (bf16[4,2,4,4,128]{4,3,2,1,0:T(4,128)(2,1)S(1)}, bf16[4,2,4,4,128]{4,3,2,1,0:T(4,128)(2,1)S(1)}, u32[]{:S(2)}, u32[]{:S(2)}) collective-permute-start(bf16[4,2,4,4,128]{4,3,2,1,0:T(4,128)(2,1)S(1)} %maximum_select_fusion), channel_id=1, source_target_pairs={{256,263},{257,262},{258,261},{259,260},{260,259},{261,258},{262,2... | collective-permute-start | bytes 98312 | tf_op jit(solution)/shard_map/ppermute | solution.py:101
  41.7 6.0 %collective-permute-start.6 = (bf16[48,32,128]{2,1,0:T(8,128)(2,1)S(1)}, bf16[48,32,128]{2,1,0:T(8,128)(2,1)S(1)}, u32[]{:S(2)}, u32[]{:S(2)}) collective-permute-start(bf16[48,32,128]{2,1,0:T(8,128)(2,1)S(1)} %bitcast.35), channel_id=1, source_target_pairs={{0,8},{8,0},{1,9},{9,1},{2,10},{10,2},{3,11},{11,3},{4,12},{12,4},... | collective-permute-start | bytes 1179656 | tf_op jit(solution)/shard_map/ppermute | solution.py:139

commit v18 on v17

--- a/solution.py
+++ b/solution.py
@@ -12,7 +12,7 @@
 EDGE = PLANES * HALO
 BLOCKS = 8
 BAND = 3
-AHEAD = 4
+AHEAD = 3
 AXES = ("z", "x", "core", "view", "gy")
 SIZES = (12, 4, 2, 4, 2)
 

time: 50.8 us -> 51.7 us (1.018)
  the two profiles are of different devices: /device:TPU:1 before, /device:TPU:211 now
where the time goes in v18:
time: 51.7 us; the launch traced here: 51.3 us
  starting transfers between devices  39.1 us (76%)
  waiting for transfers between devices  6.42 us (12%)
  local copies, waits for them, and re-layouts  2.68 us (5%)
  Pallas kernels  2.65 us (5%)
    ppermute x6, starting transfers between devices, permute(): return lax.ppermute(array, AXES, pairs)  15.9 us
    all_to_all x1, starting transfers between devices, shards(): along = lax.all_to_all(spread, 'z', 0, 0, tiled=True)  12.4 us
    ppermute x1, starting transfers between devices, shards(): other = lax.ppermute(mine, 'core', [(0, 1), (1, 0)])  6.55 us
    ppermute x6, waiting for transfers between devices, permute(): return lax.ppermute(array, AXES, pairs)  5.19 us
    all_to_all x1, starting transfers between devices, shards(): lax.all_to_all(jnp.broadcast_to(along[None], (4, 12, 32, 128)), 'x', 0, 0...  4.26 us
    pallas_call x1, Pallas kernels, shards(): pl.pallas_call(fused, out_shape=jax.ShapeDtypeStruct((2, OWN, 1024), jnp....  2.65 us
    ppermute x1, waiting for transfers between devices, shards(): other = lax.ppermute(mine, 'core', [(0, 1), (1, 0)])  1.23 us
  transfers between devices with their start and end apart: 9, of which 4 were waited for; matrix products, arithmetic and copies ran while one was open for 1% of the time, Pallas kernels for 0%

profile of v18, /device:TPU:211, one launch (start us, length us, event | category | flops | bytes accessed | tf_op | source)
XLA Modules:
  0.0 51.3 jit_solution(6657197880655499301)
XLA Ops:
  0.0 0.0 copy-start
  0.0 0.8 %reshape.39 = bf16[2,32,64]{2,1,0:T(8,128)(2,1)S(1)} reshape(bf16[2,2048]{1,0:T(2,128)(2,1)} %param.8) | data formatting | bytes 16384 | tf_op jit(solution)/shard_map/reshape | solution.py:112
  0.8 0.1 broadcast_in_dim.6
  0.9 0.0 copy-done.2
  0.9 0.7 %broadcast_in_dim.14 = bf16[12,32,128]{2,1,0:T(8,128)(2,1)} broadcast(bf16[32,128]{1,0:T(8,128)(2,1)S(1)} %broadcast_in_dim.6), dimensions={1,2} | broadcast | bytes 106496 | tf_op jit(solution)/shard_map/broadcast_in_dim | solution.py:113
  1.6 0.6 %collective-permute-start = (bf16[4,4,256]{2,1,0:T(4,128)(2,1)S(1)}, bf16[4,4,256]{2,1,0:T(4,128)(2,1)S(1)}, u32[]{:S(2)}, u32[]{:S(2)}) collective-permute-start(bf16[4,4,256]{2,1,0:T(4,128)(2,1)S(1)} %constant_dynamic-slice_fusion.2), channel_id=1, source_target_pairs={{0,7},{1,6},{2,5},{3,4},{4,3},{5,2},{6,1},{7,0},{8,15},{9,14},{10,... | collective-permute-start | bytes 24584 | tf_op jit(solution)/shard_map/ppermute | solution.py:101
  2.3 12.4 %all-to-all-start = ((bf16[12,32,128]{2,1,0:T(8,128)(2,1)}), bf16[12,32,128]{2,1,0:T(8,128)(2,1)S(1)}, u32[]{:S(2)}, u32[]{:S(2)}) async-start(bf16[12,32,128]{2,1,0:T(8,128)(2,1)} %broadcast_in_dim.14), calls=%async_computation | async-start | bytes 196608 | tf_op jit(solution)/shard_map/all_to_all | solution.py:122
  14.7 0.0 copy-start.1
  14.7 0.0 collective-permute-done
  14.8 2.2 %collective-permute-start.3 = (bf16[2,144,128]{2,1,0:T(8,128)(2,1)S(1)}, bf16[2,144,128]{2,1,0:T(8,128)(2,1)S(1)}, u32[]{:S(2)}, u32[]{:S(2)}) collective-permute-start(bf16[2,144,128]{2,1,0:T(8,128)(2,1)S(1)} %maximum_bitcast_fusion.own), channel_id=1, source_target_pairs={{0,6},{1,7},{2,4},{3,5},{4,2},{5,3},{6,0},{7,1},{8,14},{9,15},{10,... | collective-permute-start | bytes 221192 | tf_op jit(solution)/shard_map/ppermute | solution.py:101
  17.0 5.1 %collective-permute-start.2 = (bf16[2,144,128]{2,1,0:T(8,128)(2,1)S(1)}, bf16[2,144,128]{2,1,0:T(8,128)(2,1)S(1)}, u32[]{:S(2)}, u32[]{:S(2)}) collective-permute-start(bf16[2,144,128]{2,1,0:T(8,128)(2,1)S(1)} %maximum_bitcast_fusion.own), channel_id=1, source_target_pairs={{0,4},{1,5},{2,6},{3,7},{4,0},{5,1},{6,2},{7,3},{8,12},{9,13},{10,... | collective-permute-start | bytes 221192 | tf_op jit(solution)/shard_map/ppermute | solution.py:101
  22.1 1.9 %collective-permute-start.1 = (bf16[2,144,128]{2,1,0:T(8,128)(2,1)S(1)}, bf16[2,144,128]{2,1,0:T(8,128)(2,1)S(1)}, u32[]{:S(2)}, u32[]{:S(2)}) collective-permute-start(bf16[2,144,128]{2,1,0:T(8,128)(2,1)S(1)} %maximum_bitcast_fusion.own), channel_id=1, source_target_pairs={{192,194},{193,195},{194,192},{195,193},{196,198},{197,199},{198,1... | collective-permute-start | bytes 221192 | tf_op jit(solution)/shard_map/ppermute | solution.py:101
  24.1 0.0 copy-done.3
  24.1 0.1 copy.11
  24.2 0.1 copy.12
  24.3 0.1 pad_add_fusion
  24.4 0.0 collective-permute-done.3.three
  24.4 0.1 collective-permute-done.2.two
  24.5 2.7 %collective-permute-done.1.late = bf16[2,144,128]{2,1,0:T(8,128)(2,1)S(1)} collective-permute-done((bf16[2,144,128]{2,1,0:T(8,128)(2,1)S(1)}, bf16[2,144,128]{2,1,0:T(8,128)(2,1)S(1)}, u32[]{:S(2)}, u32[]{:S(2)}) %collective-permute-start.1) | collective-permute-done | bytes 73760 | tf_op jit(solution)/shard_map/ppermute | solution.py:101
  27.2 0.1 maximum_select_fusion
  27.3 0.0 all-to-all-done
  27.3 0.8 %broadcast_in_dim.15 = bf16[4,12,32,128]{3,2,1,0:T(8,128)(2,1)} broadcast(bf16[12,32,128]{2,1,0:T(8,128)(2,1)S(1)} %all-to-all-done), dimensions={1,2,3} | broadcast | bytes 491520 | tf_op jit(solution)/shard_map/broadcast_in_dim | solution.py:133
  28.1 4.3 %all-to-all-start.1 = ((bf16[4,12,32,128]{3,2,1,0:T(8,128)(2,1)}), bf16[4,12,32,128]{3,2,1,0:T(8,128)(2,1)S(1)}, u32[]{:S(2)}, u32[]{:S(2)}) async-start(bf16[4,12,32,128]{3,2,1,0:T(8,128)(2,1)} %broadcast_in_dim.15), calls=%async_computation.1 | async-start | bytes 786432 | tf_op jit(solution)/shard_map/all_to_all | solution.py:133
  32.4 0.7 %collective-permute-start.4 = (bf16[2,144,128]{2,1,0:T(8,128)(2,1)S(1)}, bf16[2,144,128]{2,1,0:T(8,128)(2,1)S(1)}, u32[]{:S(2)}, u32[]{:S(2)}) collective-permute-start(bf16[2,144,128]{2,1,0:T(8,128)(2,1)S(1)} %maximum_bitcast_fusion.own), channel_id=1, source_target_pairs={{0,2},{1,3},{2,0},{3,1},{4,6},{5,7},{6,4},{7,5},{8,10},{9,11},{10,... | collective-permute-start | bytes 221192 | tf_op jit(solution)/shard_map/ppermute | solution.py:101
  33.0 5.3 %collective-permute-start.5 = (bf16[4,2,4,4,128]{4,3,2,1,0:T(4,128)(2,1)S(1)}, bf16[4,2,4,4,128]{4,3,2,1,0:T(4,128)(2,1)S(1)}, u32[]{:S(2)}, u32[]{:S(2)}) collective-permute-start(bf16[4,2,4,4,128]{4,3,2,1,0:T(4,128)(2,1)S(1)} %maximum_select_fusion), channel_id=1, source_target_pairs={{192,199},{193,198},{194,197},{195,196},{196,195},{197,194},{198,1... | collective-permute-start | bytes 98312 | tf_op jit(solution)/shard_map/ppermute | solution.py:101
  38.4 2.3 %collective-permute-done.5 = bf16[4,2,4,4,128]{4,3,2,1,0:T(4,128)(2,1)S(1)} collective-permute-done((bf16[4,2,4,4,128]{4,3,2,1,0:T(4,128)(2,1)S(1)}, bf16[4,2,4,4,128]{4,3,2,1,0:T(4,128)(2,1)S(1)}, u32[]{:S(2)}, u32[]{:S(2)}) %collective-permute-start.5) | collective-permute-done | bytes 32800 | tf_op jit(solution)/shard_map/ppermute | solution.py:101
  40.7 0.0 collective-permute-done.4.one
  40.7 0.0 all-to-all-done.1
  40.7 6.6 %collective-permute-start.6 = (bf16[48,32,128]{2,1,0:T(8,128)(2,1)S(1)}, bf16[48,32,128]{2,1,0:T(8,128)(2,1)S(1)}, u32[]{:S(2)}, u32[]{:S(2)}) collective-permute-start(bf16[48,32,128]{2,1,0:T(8,128)(2,1)S(1)} %bitcast.35), channel_id=1, source_target_pairs={{0,8},{8,0},{1,9},{9,1},{2,10},{10,2},{3,11},{11,3},{4,12},{12,4},... | collective-permute-start | bytes 1179656 | tf_op jit(solution)/shard_map/ppermute | solution.py:139
  47.3 0.1 pad_add_fusion.1.place
  47.4 1.2 %collective-permute-done.6.other = bf16[48,32,128]{2,1,0:T(8,128)(2,1)S(1)} collective-permute-done((bf16[48,32,128]{2,1,0:T(8,128)(2,1)S(1)}, bf16[48,32,128]{2,1,0:T(8,128)(2,1)S(1)}, u32[]{:S(2)}, u32[]{:S(2)}) %collective-permute-start.6) | collective-permute-done | bytes 393248 | tf_op jit(solution)/shard_map/ppermute | solution.py:139
  48.6 2.7 %shard_map.64 = f32[2,128,1024]{2,1,0:T(8,128)} custom-call(s32[4]{0:T(128)S(1)} %pad_add_fusion.1.place, s32[2,56]{1,0:T(2,128)S(1)} %constant_dynamic-slice_fusion.1.numbers, f32[2,9]{1,0:T(2,128)S(1)} %constant_dynamic-slice_fusion.weights, bf16[2,144,128]{2,1,0:T(8,128)(2,1)S(1)} %maximum_bitcast_fusion.own, ...), custom_call_target="tpu_custom_call" | custom-call | tf_op jit(solution)/shard_map/pallas_call | solution.py:142
  (20 shorter events, 0.2 us)
Async XLA Ops:
  0.0 47.4 %copy-start = (f32[8,9]{1,0:T(8,128)S(1)}, f32[8,9]{1,0:T(8,128)}, u32[]{:S(2)}) copy-start(f32[8,9]{1,0:T(8,128)} %param.9) | copy-start | bytes 868
  0.0 0.9 %copy-start.2 = (bf16[4,32,256]{2,1,0:T(8,128)(2,1)S(1)}, bf16[4,32,256]{2,1,0:T(8,128)(2,1)}, u32[]{:S(2)}) copy-start(bf16[4,32,256]{2,1,0:T(8,128)(2,1)} %param.6) | copy-start | bytes 196612
  1.6 13.1 %collective-permute-start = (bf16[4,4,256]{2,1,0:T(4,128)(2,1)S(1)}, bf16[4,4,256]{2,1,0:T(4,128)(2,1)S(1)}, u32[]{:S(2)}, u32[]{:S(2)}) collective-permute-start(bf16[4,4,256]{2,1,0:T(4,128)(2,1)S(1)} %constant_dynamic-slice_fusion.2), channel_id=1, source_target_pairs={{0,7},{1,6},{2,5},{3,4},{4,3},{5,2},{6,1},{7,0},{8,15},{9,14},{10,... | collective-permute-start | bytes 24584 | tf_op jit(solution)/shard_map/ppermute | solution.py:101
  2.3 25.0 %all-to-all-start = ((bf16[12,32,128]{2,1,0:T(8,128)(2,1)}), bf16[12,32,128]{2,1,0:T(8,128)(2,1)S(1)}, u32[]{:S(2)}, u32[]{:S(2)}) async-start(bf16[12,32,128]{2,1,0:T(8,128)(2,1)} %broadcast_in_dim.14), calls=%async_computation | async-start | bytes 196608 | tf_op jit(solution)/shard_map/all_to_all | solution.py:122
  14.7 9.6 %copy-start.4 = (s32[8,8]{1,0:T(8,128)S(1)}, s32[8,8]{1,0:T(8,128)}, u32[]{:S(2)}) copy-start(s32[8,8]{1,0:T(8,128)} %param.10) | copy-start | bytes 772
  14.7 9.4 %copy-start.3 = (s32[8,16,3]{1,0,2:T(8,128)S(1)}, s32[8,16,3]{1,0,2:T(8,128)}, u32[]{:S(2)}) copy-start(s32[8,16,3]{1,0,2:T(8,128)} %param.11) | copy-start | bytes 4612
  14.7 33.9 %copy-start.1 = (f32[2,4,32,1024]{3,2,1,0:T(8,128)S(1)}, f32[2,4,32,1024]{3,2,1,0:T(8,128)}, u32[]{:S(2)}) copy-start(f32[2,4,32,1024]{3,2,1,0:T(8,128)} %param.7) | copy-start | bytes 3145732
  14.8 9.6 %collective-permute-start.3 = (bf16[2,144,128]{2,1,0:T(8,128)(2,1)S(1)}, bf16[2,144,128]{2,1,0:T(8,128)(2,1)S(1)}, u32[]{:S(2)}, u32[]{:S(2)}) collective-permute-start(bf16[2,144,128]{2,1,0:T(8,128)(2,1)S(1)} %maximum_bitcast_fusion.own), channel_id=1, source_target_pairs={{0,6},{1,7},{2,4},{3,5},{4,2},{5,3},{6,0},{7,1},{8,14},{9,15},{10,... | collective-permute-start | bytes 221192 | tf_op jit(solution)/shard_map/ppermute | solution.py:101
  17.0 7.5 %collective-permute-start.2 = (bf16[2,144,128]{2,1,0:T(8,128)(2,1)S(1)}, bf16[2,144,128]{2,1,0:T(8,128)(2,1)S(1)}, u32[]{:S(2)}, u32[]{:S(2)}) collective-permute-start(bf16[2,144,128]{2,1,0:T(8,128)(2,1)S(1)} %maximum_bitcast_fusion.own), channel_id=1, source_target_pairs={{0,4},{1,5},{2,6},{3,7},{4,0},{5,1},{6,2},{7,3},{8,12},{9,13},{10,... | collective-permute-start | bytes 221192 | tf_op jit(solution)/shard_map/ppermute | solution.py:101
  22.1 5.1 %collective-permute-start.1 = (bf16[2,144,128]{2,1,0:T(8,128)(2,1)S(1)}, bf16[2,144,128]{2,1,0:T(8,128)(2,1)S(1)}, u32[]{:S(2)}, u32[]{:S(2)}) collective-permute-start(bf16[2,144,128]{2,1,0:T(8,128)(2,1)S(1)} %maximum_bitcast_fusion.own), channel_id=1, source_target_pairs={{192,194},{193,195},{194,192},{195,193},{196,198},{197,199},{198,1... | collective-permute-start | bytes 221192 | tf_op jit(solution)/shard_map/ppermute | solution.py:101
  28.1 12.6 %all-to-all-start.1 = ((bf16[4,12,32,128]{3,2,1,0:T(8,128)(2,1)}), bf16[4,12,32,128]{3,2,1,0:T(8,128)(2,1)S(1)}, u32[]{:S(2)}, u32[]{:S(2)}) async-start(bf16[4,12,32,128]{3,2,1,0:T(8,128)(2,1)} %broadcast_in_dim.15), calls=%async_computation.1 | async-start | bytes 786432 | tf_op jit(solution)/shard_map/all_to_all | solution.py:133
  32.4 8.3 %collective-permute-start.4 = (bf16[2,144,128]{2,1,0:T(8,128)(2,1)S(1)}, bf16[2,144,128]{2,1,0:T(8,128)(2,1)S(1)}, u32[]{:S(2)}, u32[]{:S(2)}) collective-permute-start(bf16[2,144,128]{2,1,0:T(8,128)(2,1)S(1)} %maximum_bitcast_fusion.own), channel_id=1, source_target_pairs={{0,2},{1,3},{2,0},{3,1},{4,6},{5,7},{6,4},{7,5},{8,10},{9,11},{10,... | collective-permute-start | bytes 221192 | tf_op jit(solution)/shard_map/ppermute | solution.py:101
  33.0 7.7 %collective-permute-start.5 = (bf16[4,2,4,4,128]{4,3,2,1,0:T(4,128)(2,1)S(1)}, bf16[4,2,4,4,128]{4,3,2,1,0:T(4,128)(2,1)S(1)}, u32[]{:S(2)}, u32[]{:S(2)}) collective-permute-start(bf16[4,2,4,4,128]{4,3,2,1,0:T(4,128)(2,1)S(1)} %maximum_select_fusion), channel_id=1, source_target_pairs={{192,199},{193,198},{194,197},{195,196},{196,195},{197,194},{198,1... | collective-permute-start | bytes 98312 | tf_op jit(solution)/shard_map/ppermute | solution.py:101
  40.7 7.9 %collective-permute-start.6 = (bf16[48,32,128]{2,1,0:T(8,128)(2,1)S(1)}, bf16[48,32,128]{2,1,0:T(8,128)(2,1)S(1)}, u32[]{:S(2)}, u32[]{:S(2)}) collective-permute-start(bf16[48,32,128]{2,1,0:T(8,128)(2,1)S(1)} %bitcast.35), channel_id=1, source_target_pairs={{0,8},{8,0},{1,9},{9,1},{2,10},{10,2},{3,11},{11,3},{4,12},{12,4},... | collective-permute-start | bytes 1179656 | tf_op jit(solution)/shard_map/ppermute | solution.py:139
